TPU v7x, 32 devices: a whole 2x2x4 slice. The times are simulated.
32 devices in a mesh: dp: 4 (over z), row: 4 (over x, core), col: 2 (over y).
Axes of the slice: x: 2, y: 2, z: 4, core: 2. Of those that a mesh axis runs over, the one named last changes fastest.
Arguments:
- tokens: bfloat16 [8192, 1024], P('dp', 'row'), may hold values from -6 to 6
- segments: int32 [8192], P('dp'), may hold values from 0 to 31, as said below
- norm_gain: bfloat16 [2, 2, 1024], P(None, None, 'row'), may hold values from 0.5 to 1.5
- norm_shift: bfloat16 [2, 2, 1024], P(None, None, 'row'), may hold values from -3 to 3
- triple_weight: bfloat16 [2, 1024, 3, 1024], P(None, 'row', None, 'col')
- triple_bias: bfloat16 [2, 2, 1024], P(None, None, ('col', 'row')), may hold values from -3 to 3
- output_weight: bfloat16 [2, 1024, 1024], P(None, 'col', 'row'), may hold values from -1 to 1
- output_bias: bfloat16 [2, 1024], P(None, 'row'), may hold values from -3 to 3
- up_weight: bfloat16 [2, 1024, 4096], P(None, 'row', 'col')
- up_bias: bfloat16 [2, 4096], P(None, ('col', 'row')), may hold values from -3 to 3
- down_weight: bfloat16 [2, 4096, 1024], P(None, 'col', 'row'), may hold values from -0.09375 to 0.09375
- down_bias: bfloat16 [2, 1024], P(None, 'row'), may hold values from -3 to 3
- cotangent: bfloat16 [8192, 1024], P('dp', 'row'), may hold values from -6 to 6
Outputs:
- result: bfloat16 [8192, 1024], P('dp', 'row')
- input_grad: float32 [8192, 1024], P('dp', 'row')
- gain_grad: float32 [2, 2, 1024], P(None, None, 'row')
- shift_grad: float32 [2, 2, 1024], P(None, None, 'row')
- triple_grad: float32 [2, 1024, 3, 1024], P(None, 'row', None, 'col')
- triple_bias_grad: float32 [2, 2, 1024], P(None, None, ('col', 'row'))
- output_grad: float32 [2, 1024, 1024], P(None, 'col', 'row')
- output_bias_grad: float32 [2, 1024], P(None, 'row')
- up_grad: float32 [2, 1024, 4096], P(None, 'row', 'col')
- up_bias_grad: float32 [2, 4096], P(None, ('col', 'row'))
- down_grad: float32 [2, 4096, 1024], P(None, 'col', 'row')
- down_bias_grad: float32 [2, 1024], P(None, 'row')
Inputs may be any that keep to these rules, and one draw needn't show every extreme that they name: `segments`: segment numbers never fall along the tokens; every pack of 1024 tokens holds exactly 4 documents, the first starting at the pack's first token, so no number spans two packs.
All inputs are finite; a program needn't handle non-finite values.
Results may differ from a plain program's by a relative error of at most 0.019.
Values may be sent and summed in bfloat16 or wider, within the bound.
A program may use at most 192 MiB of HBM per device.

v0:
```python
import math

import jax
import jax.numpy as jnp
from jax import lax
from jax.sharding import PartitionSpec as P

D = 1024
HD = 64
LAYERS = 2
LEN = 1024


eps = 1e-05
masked = -1000000000.0


def norm_forward(stream, gain, shift):
    totals = lax.psum((jnp.sum(stream, axis=1), jnp.sum(stream * stream, axis=1)), "row")
    center = totals[0] / D
    second = totals[1] / D - center * center
    inv_std = lax.rsqrt(second + eps)
    normed = (stream - center[:, None]) * inv_std[:, None]
    return (normed, inv_std, normed * gain + shift)


def norm_backward(grad_out, normed, inv_std, gain):
    scaled = grad_out * gain
    totals = lax.psum((jnp.sum(scaled, axis=1), jnp.sum(scaled * normed, axis=1)), "row")
    grad_in = inv_std[:, None] * (
        scaled - totals[0][:, None] / D - normed * (totals[1][:, None] / D)
    )
    return (grad_in, jnp.sum(grad_out * normed, axis=0), jnp.sum(grad_out, axis=0))


def gather_rows(block):
    return lax.all_gather(block, "row", axis=1, tiled=True)


def col_total(partial_sums):
    return lax.psum(partial_sums, "col")


def rows_back(partial_sums):
    return lax.psum_scatter(
        partial_sums.astype(jnp.bfloat16), "row", scatter_dimension=1, tiled=True
    ).astype(jnp.float32)


def in_parts(partial_sums):
    return lax.psum_scatter(partial_sums, "row", scatter_dimension=2, tiled=True)


def grad_gather(block):
    return lax.all_gather(block, "row", axis=2, tiled=True)


def pack_scores(queries, key_rows, seg_pack, scale):
    position = jnp.arange(queries.shape[0])
    allowed = (seg_pack[:, None] == seg_pack[None, :]) & (position[None, :] <= position[:, None])
    scores = (
        jnp.einsum("qhd,khd->hqk", queries, key_rows, preferred_element_type=jnp.float32) * scale
    )
    return jnp.where(allowed[None], scores, masked)


def split_packs(triple, seg_rows):
    length, three, width = triple.shape
    count = length // LEN
    return (triple.reshape(count, LEN, three, width // HD, HD), seg_rows.reshape(count, LEN))


def attend_forward(triple, seg_rows, scale):
    length, three, width = triple.shape
    packs, seg_packs = split_packs(triple, seg_rows)

    def one_pack(pieces):
        pack_rows, seg_pack = pieces
        scores = pack_scores(pack_rows[:, 0], pack_rows[:, 1], seg_pack, scale)
        row_peak = jnp.max(scores, axis=-1, keepdims=True)
        exponent = jnp.exp(scores - row_peak)
        denominator = jnp.sum(exponent, axis=-1, keepdims=True)
        soft_weights = (exponent / denominator).astype(jnp.bfloat16)
        blended = jnp.einsum(
            "hqk,khd->qhd", soft_weights, pack_rows[:, 2], preferred_element_type=jnp.float32
        )
        return (blended.astype(jnp.bfloat16), (row_peak + jnp.log(denominator))[..., 0])

    blended, log_totals = lax.map(one_pack, (packs, seg_packs))
    return (blended.reshape(length, width), log_totals)


def attend_backward(triple, seg_rows, log_totals, grad_mixed, scale):
    length, three, width = triple.shape
    packs, seg_packs = split_packs(triple, seg_rows)
    grad_packs = grad_mixed.reshape(length // LEN, LEN, width // HD, HD)

    def one_pack(pieces):
        pack_rows, seg_pack, pack_totals, grad_pack = pieces
        queries = pack_rows[:, 0]
        key_rows = pack_rows[:, 1]
        value_rows = pack_rows[:, 2]
        scores = pack_scores(queries, key_rows, seg_pack, scale)
        chances = jnp.exp(scores - pack_totals[:, :, None])
        chance_grad = jnp.einsum(
            "qhd,khd->hqk", grad_pack, value_rows, preferred_element_type=jnp.float32
        )
        inner = jnp.sum(chances * chance_grad, axis=-1, keepdims=True)
        score_grad = (chances * (chance_grad - inner)).astype(jnp.bfloat16)
        query_grad = (
            jnp.einsum("hqk,khd->qhd", score_grad, key_rows, preferred_element_type=jnp.float32)
            * scale
        )
        key_grad = (
            jnp.einsum("hqk,qhd->khd", score_grad, queries, preferred_element_type=jnp.float32)
            * scale
        )
        value_grad = jnp.einsum(
            "hqk,qhd->khd",
            chances.astype(jnp.bfloat16),
            grad_pack,
            preferred_element_type=jnp.float32,
        )
        return jnp.stack([query_grad, key_grad, value_grad], axis=1).astype(jnp.bfloat16)

    triple_rows = lax.map(one_pack, (packs, seg_packs, log_totals, grad_packs))
    return triple_rows.reshape(length, three, width)


def layer_forward(stream, weights, small, seg_rows):
    triple_w, output_w, up_w, down_w = weights
    gains, shifts, triple_b, output_b, up_b, down_b = small
    scale = 1.0 / math.sqrt(HD)
    normed_one, inv_one, attn_in = norm_forward(stream, gains[0], shifts[0])
    attn_in = attn_in.astype(jnp.bfloat16)
    triple = in_parts(
        jnp.einsum("td,dke->tke", attn_in, triple_w, preferred_element_type=jnp.float32)
    )
    bias_rows = jnp.stack([triple_b[0], jnp.zeros_like(triple_b[0]), triple_b[1]])
    triple = (triple + bias_rows).astype(jnp.bfloat16)
    mixed, log_totals = attend_forward(triple, seg_rows, scale)
    mixed_full = gather_rows(mixed)
    middle = stream + (
        col_total(jnp.dot(mixed_full, output_w, preferred_element_type=jnp.float32)) + output_b
    )
    normed_two, inv_two, mlp_in = norm_forward(middle, gains[1], shifts[1])
    mlp_in = mlp_in.astype(jnp.bfloat16)
    hidden_pre = (
        in_parts(jnp.dot(mlp_in, up_w, preferred_element_type=jnp.float32)[:, None, :])[:, 0] + up_b
    )
    active = jax.nn.gelu(hidden_pre, approximate=True).astype(jnp.bfloat16)
    active_full = gather_rows(active)
    after = middle + (
        col_total(jnp.dot(active_full, down_w, preferred_element_type=jnp.float32)) + down_b
    )
    saved = (
        normed_one,
        inv_one,
        attn_in,
        triple,
        log_totals,
        mixed_full,
        normed_two,
        inv_two,
        mlp_in,
        hidden_pre,
        active_full,
        None,
    )
    return (after, saved)


def layer_backward(grad, saved, weights, gains, seg_rows):
    (
        normed_one,
        inv_one,
        attn_rows,
        triple,
        log_totals,
        mixed_full,
        normed_two,
        inv_two,
        mlp_rows,
        hidden_pre,
        active_full,
        columns_in,
    ) = saved
    triple_w, output_w, up_w, down_w = weights
    scale = 1.0 / math.sqrt(HD)
    down_in = grad.astype(jnp.bfloat16)
    down_bias_grad = jnp.sum(down_in, axis=0, dtype=jnp.float32)
    down_grad = jnp.einsum("tf,td->fd", active_full, down_in, preferred_element_type=jnp.float32)
    active_grad = rows_back(
        jnp.einsum("td,fd->tf", down_in, down_w, preferred_element_type=jnp.float32)
    )
    gelu_pull = jax.vjp(lambda value: jax.nn.gelu(value, approximate=True), hidden_pre)[1]
    hidden_grad = gelu_pull(active_grad)[0].astype(jnp.bfloat16)
    up_bias_grad = jnp.sum(hidden_grad, axis=0, dtype=jnp.float32)
    hidden_rows = grad_gather(hidden_grad[:, None, :])[:, 0]
    up_grad = jnp.einsum("td,tf->df", mlp_rows, hidden_rows, preferred_element_type=jnp.float32)
    mlp_grad = col_total(
        jnp.einsum("tf,df->td", hidden_rows, up_w, preferred_element_type=jnp.float32)
    )
    norm_two_grad, gain_two, shift_two = norm_backward(mlp_grad, normed_two, inv_two, gains[1])
    middle_grad = grad + norm_two_grad
    branch_grad = middle_grad.astype(jnp.bfloat16)
    output_bias_grad = jnp.sum(branch_grad, axis=0, dtype=jnp.float32)
    output_grad = jnp.einsum(
        "td,te->de", mixed_full, branch_grad, preferred_element_type=jnp.float32
    )
    mixed_grad = rows_back(
        jnp.einsum("te,de->td", branch_grad, output_w, preferred_element_type=jnp.float32)
    ).astype(jnp.bfloat16)
    triple_rows = attend_backward(triple, seg_rows, log_totals, mixed_grad, scale)
    triple_bias_grad = jnp.sum(triple_rows[:, 0::2], axis=0, dtype=jnp.float32)
    full_rows = grad_gather(triple_rows)
    triple_grad = jnp.einsum(
        "td,tke->dke", attn_rows, full_rows, preferred_element_type=jnp.float32
    )
    attn_grad = col_total(
        jnp.einsum("tke,dke->td", full_rows, triple_w, preferred_element_type=jnp.float32)
    )
    norm_one_grad, gain_one, shift_one = norm_backward(attn_grad, normed_one, inv_one, gains[0])
    start_grad = middle_grad + norm_one_grad
    terms = (
        jnp.stack([gain_one, gain_two]),
        jnp.stack([shift_one, shift_two]),
        triple_grad,
        triple_bias_grad,
        output_grad,
        output_bias_grad,
        up_grad,
        up_bias_grad,
        down_grad,
        down_bias_grad,
    )
    return (start_grad, terms)


def on_device(
    tokens,
    segments,
    norm_gain,
    norm_shift,
    triple_weight,
    triple_bias,
    output_weight,
    output_bias,
    up_weight,
    up_bias,
    down_weight,
    down_bias,
    cotangent,
):

    def weights_of(layer_id):
        return (
            triple_weight[layer_id],
            output_weight[layer_id],
            up_weight[layer_id],
            down_weight[layer_id],
        )

    def small_of(layer_id):
        return (
            norm_gain[layer_id].astype(jnp.float32),
            norm_shift[layer_id].astype(jnp.float32),
            triple_bias[layer_id].astype(jnp.float32),
            output_bias[layer_id].astype(jnp.float32),
            up_bias[layer_id].astype(jnp.float32),
            down_bias[layer_id].astype(jnp.float32),
        )

    stream = tokens.astype(jnp.float32)
    stored = []
    for layer_id in range(LAYERS):
        stream, saved = layer_forward(stream, weights_of(layer_id), small_of(layer_id), segments)
        stored.append(saved)
    result = stream.astype(jnp.bfloat16)
    grad = cotangent.astype(jnp.float32)
    summed = [None] * LAYERS
    for layer_id in reversed(range(LAYERS)):
        grad, terms = layer_backward(
            grad, stored[layer_id], weights_of(layer_id), small_of(layer_id)[0], segments
        )
        summed[layer_id] = (
            lax.psum(terms[0].astype(jnp.bfloat16), "dp").astype(jnp.float32),
            lax.psum(terms[1].astype(jnp.bfloat16), "dp").astype(jnp.float32),
            lax.psum(terms[2].astype(jnp.bfloat16), "dp").astype(jnp.float32),
            lax.psum(terms[3].astype(jnp.bfloat16), "dp").astype(jnp.float32),
            lax.psum(terms[4].astype(jnp.bfloat16), "dp").astype(jnp.float32),
            lax.psum(terms[5].astype(jnp.bfloat16), "dp").astype(jnp.float32),
            lax.psum(terms[6].astype(jnp.bfloat16), "dp").astype(jnp.float32),
            lax.psum(terms[7].astype(jnp.bfloat16), "dp").astype(jnp.float32),
            lax.psum(terms[8].astype(jnp.bfloat16), "dp").astype(jnp.float32),
            lax.psum(terms[9].astype(jnp.bfloat16), "dp").astype(jnp.float32),
        )
    stacks = [
        jnp.stack([summed[layer_id][member] for layer_id in range(LAYERS)]) for member in range(10)
    ]
    return (
        result,
        grad,
        stacks[0],
        stacks[1],
        stacks[2],
        stacks[3],
        stacks[4],
        stacks[5],
        stacks[6],
        stacks[7],
        stacks[8],
        stacks[9],
    )


def solution(mesh):
    in_specs = (
        P("dp", "row"),
        P("dp"),
        P(None, None, "row"),
        P(None, None, "row"),
        P(None, "row", None, "col"),
        P(None, None, ("col", "row")),
        P(None, "col", "row"),
        P(None, "row"),
        P(None, "row", "col"),
        P(None, ("col", "row")),
        P(None, "col", "row"),
        P(None, "row"),
        P("dp", "row"),
    )
    out_specs = (
        P("dp", "row"),
        P("dp", "row"),
        P(None, None, "row"),
        P(None, None, "row"),
        P(None, "row", None, "col"),
        P(None, None, ("col", "row")),
        P(None, "col", "row"),
        P(None, "row"),
        P(None, "row", "col"),
        P(None, ("col", "row")),
        P(None, "col", "row"),
        P(None, "row"),
    )
    return jax.shard_map(
        on_device, mesh=mesh, in_specs=in_specs, out_specs=out_specs, check_vma=False
    )
```

profile of v0, /device:TPU:0, one launch (start us, length us, event | category | flops | bytes accessed | tf_op | source)
XLA Modules:
  0.0 2076.9 jit_solution(15964389403501703108)
XLA Ops:
  11.6 12.7 all-reduce.7
  33.6 98.7 %reduce-scatter.13.cloned.1.call-done = f32[2048,3,128]{2,0,1:T(8,128)} async-done(((f32[2048,3,512]{2,0,1:T(8,128)}), f32[2048,3,128]{2,0,1:T(8,128)}) %reduce-scatter.13.cloned.1.call-update) | async-done | bytes 3145744 | tf_op jit(solution)/shard_map/reduce_scatter | solution.py:51
  144.8 16.2 while.44
  162.5 22.7 %all-gather.11.cloned.1.call-done = bf16[2048,512]{0,1:T(8,128)(2,1)} async-done(((bf16[2048,128]{0,1:T(8,128)(2,1)}), bf16[2048,512]{0,1:T(8,128)(2,1)}) %all-gather.11.cloned.1.call-update) | async-done | bytes 2097168 | tf_op jit(solution)/shard_map/all_gather | solution.py:37
  189.6 62.4 %all-reduce.20.cloned.1.call-done = f32[2048,256]{1,0:T(8,128)} async-done(((f32[2048,256]{1,0:T(8,128)}), f32[2048,256]{1,0:T(8,128)}) %all-reduce.20.cloned.1.call-update) | async-done | bytes 2097168 | tf_op jit(solution)/shard_map/psum | solution.py:41
  254.2 11.5 all-reduce.6
  274.8 124.7 %reduce-scatter.15.cloned.1.call-done = f32[2048,1,512]{2,0,1:T(8,128)} async-done(((f32[2048,1,2048]{2,0,1:T(8,128)}), f32[2048,1,512]{2,0,1:T(8,128)}) %reduce-scatter.15.cloned.1.call-update) | async-done | bytes 4194320 | tf_op jit(solution)/shard_map/reduce_scatter | solution.py:51
  404.5 58.4 %all-gather.13.cloned.1.call-done = bf16[2048,2048]{1,0:T(8,128)(2,1)} async-done(((bf16[2048,512]{1,0:T(8,128)(2,1)}), bf16[2048,2048]{1,0:T(8,128)(2,1)}) %all-gather.13.cloned.1.call-update) | async-done | bytes 8388624 | tf_op jit(solution)/shard_map/all_gather | solution.py:37
  471.5 61.8 %all-reduce.22.cloned.1.call-done = f32[2048,256]{1,0:T(8,128)} async-done(((f32[2048,256]{1,0:T(8,128)}), f32[2048,256]{1,0:T(8,128)}) %all-reduce.22.cloned.1.call-update) | async-done | bytes 2097168 | tf_op jit(solution)/shard_map/psum | solution.py:41
  556.9 97.8 %reduce-scatter.17.cloned.1.call-done = f32[2048,3,128]{2,0,1:T(8,128)} async-done(((f32[2048,3,512]{2,0,1:T(8,128)}), f32[2048,3,128]{2,0,1:T(8,128)}) %reduce-scatter.17.cloned.1.call-update) | async-done | bytes 3145744 | tf_op jit(solution)/shard_map/reduce_scatter | solution.py:51
  666.6 15.0 while.45
  683.2 22.7 %all-gather.15.cloned.1.call-done = bf16[2048,512]{0,1:T(8,128)(2,1)} async-done(((bf16[2048,128]{0,1:T(8,128)(2,1)}), bf16[2048,512]{0,1:T(8,128)(2,1)}) %all-gather.15.cloned.1.call-update) | async-done | bytes 2097168 | tf_op jit(solution)/shard_map/all_gather | solution.py:37
  717.8 54.9 %all-reduce.24.cloned.1.call-done = f32[2048,256]{1,0:T(8,128)} async-done(((f32[2048,256]{1,0:T(8,128)}), f32[2048,256]{1,0:T(8,128)}) %all-reduce.24.cloned.1.call-update) | async-done | bytes 2097168 | tf_op jit(solution)/shard_map/psum | solution.py:41
  775.6 11.2 all-reduce.4
  795.7 51.2 %reduce-scatter.21.cloned.1.call-done = bf16[2048,512]{1,0:T(8,128)(2,1)} async-done(((bf16[2048,2048]{1,0:T(8,128)(2,1)}), bf16[2048,512]{1,0:T(8,128)(2,1)}) %reduce-scatter.21.cloned.1.call-update) | async-done | bytes 2097168 | tf_op jit(solution)/shard_map/reduce_scatter | solution.py:45
  846.8 128.9 %reduce-scatter.19.cloned.1.call-done = f32[2048,1,512]{2,0,1:T(8,128)} async-done(((f32[2048,1,2048]{2,0,1:T(8,128)}), f32[2048,1,512]{2,0,1:T(8,128)}) %reduce-scatter.19.cloned.1.call-update) | async-done | bytes 4194320 | tf_op jit(solution)/shard_map/reduce_scatter | solution.py:51
  982.5 58.4 %all-gather.23.cloned.1.call-done = bf16[2048,2048]{1,0:T(8,128)(2,1)} async-done(((bf16[2048,512]{1,0:T(8,128)(2,1)}), bf16[2048,2048]{1,0:T(8,128)(2,1)}) %all-gather.23.cloned.1.call-update) | async-done | bytes 8388624 | tf_op jit(solution)/shard_map/all_gather | solution.py:55
  1048.3 63.0 %all-reduce.26.cloned.1.call-done = f32[2048,256]{1,0:T(8,128)} async-done(((f32[2048,256]{1,0:T(8,128)}), f32[2048,256]{1,0:T(8,128)}) %all-reduce.26.cloned.1.call-update) | async-done | bytes 2097168 | tf_op jit(solution)/shard_map/psum | solution.py:41
  1134.2 30.6 %reduce-scatter.25.cloned.1.call-done = bf16[128,2048]{1,0:T(8,128)(2,1)} async-done(((bf16[512,2048]{1,0:T(8,128)(2,1)}), bf16[128,2048]{1,0:T(8,128)(2,1)}) %reduce-scatter.25.cloned.1.call-update) | async-done | bytes 524304
  1167.7 27.6 %while.46 = (s32[]{:T(128)}, bf16[2,1024,3,2,64]{1,4,3,2,0:T(8,128)(2,1)}, bf16[2,1024,3,2,64]{1,4,3,2,0:T(8,128)(2,1)S(1)}, s32[2,1024]{1,0:T(2,128)S(1)}, f32[...) while((s32[]{:T(128)}, bf16[2,1024,3,2,64]{1,4,3,2,0:T(8,128)(2,1)}, ...), condition=%wide.region_41.42_spmd, body=%wide.region_39.41_spmd.sunk | while | flops 1379792896 | bytes 85528728 | solution.py:126
  1201.7 47.3 %all-gather.19.cloned.1.call-done = bf16[2048,3,512]{2,0,1:T(8,128)(2,1)} async-done(((bf16[2048,3,128]{2,0,1:T(8,128)(2,1)}), bf16[2048,3,512]{2,0,1:T(8,128)(2,1)}) %all-gather.19.cloned.1.call-update) | async-done | bytes 6291472 | tf_op jit(solution)/shard_map/all_gather | solution.py:55
  1255.1 63.0 %all-reduce.28.cloned.1.call-done = f32[2048,256]{1,0:T(8,128)} async-done(((f32[2048,256]{1,0:T(8,128)}), f32[2048,256]{1,0:T(8,128)}) %all-reduce.28.cloned.1.call-update) | async-done | bytes 2097168 | tf_op jit(solution)/shard_map/psum | solution.py:41
  1343.7 70.9 %reduce-scatter.23.cloned.1.call-done = bf16[2048,512]{1,0:T(8,128)(2,1)} async-done(((bf16[2048,2048]{1,0:T(8,128)(2,1)}), bf16[2048,512]{1,0:T(8,128)(2,1)}) %reduce-scatter.23.cloned.1.call-update) | async-done | bytes 2097168 | tf_op jit(solution)/shard_map/reduce_scatter | solution.py:45
  1421.4 58.4 %all-gather.25.cloned.1.call-done = bf16[2048,2048]{1,0:T(8,128)(2,1)} async-done(((bf16[2048,512]{1,0:T(8,128)(2,1)}), bf16[2048,2048]{1,0:T(8,128)(2,1)}) %all-gather.25.cloned.1.call-update) | async-done | bytes 8388624 | tf_op jit(solution)/shard_map/all_gather | solution.py:55
  1487.0 63.0 %all-reduce.30.cloned.1.call-done = f32[2048,256]{1,0:T(8,128)} async-done(((f32[2048,256]{1,0:T(8,128)}), f32[2048,256]{1,0:T(8,128)}) %all-reduce.30.cloned.1.call-update) | async-done | bytes 2097168 | tf_op jit(solution)/shard_map/psum | solution.py:41
  1581.7 25.0 %reduce-scatter.27.cloned.1.call-done = bf16[128,2048]{1,0:T(8,128)(2,1)} async-done(((bf16[512,2048]{1,0:T(8,128)(2,1)}), bf16[128,2048]{1,0:T(8,128)(2,1)}) %reduce-scatter.27.cloned.1.call-update) | async-done | bytes 524304
  1609.6 31.2 %while.47 = (s32[]{:T(128)}, bf16[2,1024,3,2,64]{1,4,3,2,0:T(8,128)(2,1)}, bf16[2,1024,3,2,64]{1,4,3,2,0:T(8,128)(2,1)}, s32[2,1024]{1,0:T(2,128)S(1)}, f32[2,2,...) while((s32[]{:T(128)}, bf16[2,1024,3,2,64]{1,4,3,2,0:T(8,128)(2,1)}, ...), condition=%wide.region_56.57_spmd, body=%wide.region_54.56_spmd.sunk | while | flops 1379792896 | bytes 85528728 | solution.py:126
  1651.8 15.4 all-gather.17.cloned.1.call-done
  1682.7 33.3 %all-gather.21.cloned.1.call-done = bf16[2048,3,512]{2,0,1:T(8,128)(2,1)} async-done(((bf16[2048,3,128]{2,0,1:T(8,128)(2,1)}), bf16[2048,3,512]{2,0,1:T(8,128)(2,1)}) %all-gather.21.cloned.1.call-update) | async-done | bytes 6291472 | tf_op jit(solution)/shard_map/all_gather | solution.py:55
  1756.5 74.1 %all-reduce.32.cloned.1.call-done = (f32[2048,256]{1,0:T(8,128)}, f32[2048,256]{1,0:T(8,128)}) async-done(((f32[2048,256]{1,0:T(8,128)}, f32[2048,256]{1,0:T(8,128)}), (f32[2048,256]{1,0:T(8,128)}, f32[2048,256]{1,0:T(8,128)})) %all-reduce.32.cloned.1.call-update) | async-done | bytes 4194320 | tf_op jit(solution)/shard_map/psum | solution.py:41
  1833.2 22.1 %all-reduce.9 = (bf16[1,2,256]{2,1,0:T(2,128)(2,1)S(1)}, bf16[1,2,256]{2,1,0:T(2,128)(2,1)S(1)}, bf16[1,2,256]{2,1,0:T(2,128)(2,1)S(1)}, bf16[1,2,256]{2,1,0:T(2...) all-reduce(bf16[1,2,256]{2,1,0:T(2,128)(2,1)S(1)} %maximum_bitcast_, ...), channel_id=1, replica_groups=mesh['dp'=4,'row'=4,'col'=2] {'dp'}, use_global_device_ids=true, to_apply=%region_67.68 | all-reduce | flops 4608 | bytes 18432 | tf_op jit(solution)/shard_map/psum | solution.py:287
  1875.7 184.6 %all-reduce.34.cloned.1.call-done = (bf16[1,256,3,512]{3,1,2,0:T(8,128)(2,1)}, bf16[1,256,3,512]{3,1,2,0:T(8,128)(2,1)}, bf16[1,512,256]{2,1,0:T(8,128)(2,1)}, b...) async-done(((bf16[1,256,3,512]{3,1,2,0:T(8,128)(2,1)}, ...) | async-done | bytes 6291472 | tf_op jit(solution)/shard_map/psum | solution.py:289
  (466 shorter events, 431.5 us)
Async XLA Ops:
  7.2 125.1 %reduce-scatter.13.cloned.1.call-start = ((), (), s32[]{:S(2)}) async-start(), calls=%async_computation.8 | async-start | bytes 15728640 | tf_op jit(solution)/shard_map/reduce_scatter | solution.py:51
  11.0 254.7 %copy-start.61 = (f32[1,1,256]{2,1,0:T(1,128)}, f32[1,1,256]{2,1,0:T(1,128)S(1)}, u32[]{:S(2)}) copy-start(f32[1,1,256]{2,1,0:T(1,128)S(1)} %get-tuple-element.369) | copy-start | bytes 3076
  11.0 536.6 %copy-start.65 = (f32[1,1,256]{2,1,0:T(1,128)}, f32[1,1,256]{2,1,0:T(1,128)S(1)}, u32[]{:S(2)}) copy-start(f32[1,1,256]{2,1,0:T(1,128)S(1)} %get-tuple-element.343) | copy-start | bytes 3076
  11.6 536.1 %copy-start.78 = (f32[1,1,256]{2,1,0:T(1,128)}, f32[1,1,256]{2,1,0:T(1,128)S(1)}, u32[]{:S(2)}) copy-start(f32[1,1,256]{2,1,0:T(1,128)S(1)} %get-tuple-element.345) | copy-start | bytes 3076
  32.8 152.5 %all-gather.11.cloned.1.call-start = ((), (), s32[]{:S(2)}) async-start(), calls=%async_computation.9 | async-start | bytes 2621440 | tf_op jit(solution)/shard_map/all_gather | solution.py:37
  162.5 89.5 %all-reduce.20.cloned.1.call-start = ((), (), s32[]{:S(2)}) async-start(), calls=%async_computation.10 | async-start | bytes 4194304 | tf_op jit(solution)/shard_map/psum | solution.py:41
  188.9 210.6 %reduce-scatter.15.cloned.1.call-start = ((), (), s32[]{:S(2)}) async-start(), calls=%async_computation.11 | async-start | bytes 20971520 | tf_op jit(solution)/shard_map/reduce_scatter | solution.py:51
  254.2 279.1 %copy-start = (f32[2048,256]{1,0:T(8,128)}, f32[2048,256]{1,0:T(8,128)S(1)}, u32[]{:S(2)}) copy-start(f32[2048,256]{1,0:T(8,128)S(1)} %get-tuple-element.322) | copy-start | bytes 6291460
  274.1 188.8 %all-gather.13.cloned.1.call-start = ((), (), s32[]{:S(2)}) async-start(), calls=%async_computation.12 | async-start | bytes 10485760 | tf_op jit(solution)/shard_map/all_gather | solution.py:37
  274.8 701.0 %copy-start.72 = (f32[1,512]{1,0:T(1,128)}, f32[1,512]{1,0:T(1,128)S(1)}, u32[]{:S(2)}) copy-start(f32[1,512]{1,0:T(1,128)S(1)} %get-tuple-element.340) | copy-start | bytes 6148
  404.4 128.8 %all-reduce.22.cloned.1.call-start = ((), (), s32[]{:S(2)}) async-start(), calls=%async_computation.13 | async-start | bytes 4194304 | tf_op jit(solution)/shard_map/psum | solution.py:41
  470.2 184.5 %reduce-scatter.17.cloned.1.call-start = ((), (), s32[]{:S(2)}) async-start(), calls=%async_computation.14 | async-start | bytes 15728640 | tf_op jit(solution)/shard_map/reduce_scatter | solution.py:51
  556.4 149.5 %all-gather.15.cloned.1.call-start = ((), (), s32[]{:S(2)}) async-start(), calls=%async_computation.15 | async-start | bytes 2621440 | tf_op jit(solution)/shard_map/all_gather | solution.py:37
  683.2 89.5 %all-reduce.24.cloned.1.call-start = ((), (), s32[]{:S(2)}) async-start(), calls=%async_computation.16 | async-start | bytes 4194304 | tf_op jit(solution)/shard_map/psum | solution.py:41
  709.6 137.3 %reduce-scatter.21.cloned.1.call-start = ((), (), s32[]{:S(2)}) async-start(), calls=%async_computation.19 | async-start | bytes 10485760 | tf_op jit(solution)/shard_map/reduce_scatter | solution.py:45
  717.7 258.0 %reduce-scatter.19.cloned.1.call-start = ((), (), s32[]{:S(2)}) async-start(), calls=%async_computation.17 | async-start | bytes 20971520 | tf_op jit(solution)/shard_map/reduce_scatter | solution.py:51
  775.6 350.0 %copy-start.2 = (f32[2048,256]{1,0:T(8,128)}, f32[2048,256]{1,0:T(8,128)S(1)}, u32[]{:S(2)}) copy-start(f32[2048,256]{1,0:T(8,128)S(1)} %get-tuple-element.320) | copy-start | bytes 6291460
  786.8 338.8 %copy-start.47 = (f32[2048]{0:T(1024)}, f32[2048]{0:T(1024)S(1)}, u32[]{:S(2)}) copy-start(f32[2048]{0:T(1024)S(1)} %get-tuple-element.332) | copy-start | bytes 24580
  786.8 338.8 %copy-start.49 = (f32[2048]{0:T(1024)}, f32[2048]{0:T(1024)S(1)}, u32[]{:S(2)}) copy-start(f32[2048]{0:T(1024)S(1)} %get-tuple-element.333) | copy-start | bytes 24580
  795.4 245.5 %all-gather.23.cloned.1.call-start = ((), (), s32[]{:S(2)}) async-start(), calls=%async_computation.26 | async-start | bytes 10485760 | tf_op jit(solution)/shard_map/all_gather | solution.py:55
  982.5 128.9 %all-reduce.26.cloned.1.call-start = ((), (), s32[]{:S(2)}) async-start(), calls=%async_computation.20 | async-start | bytes 4194304 | tf_op jit(solution)/shard_map/psum | solution.py:41
  1048.3 116.5 %reduce-scatter.25.cloned.1.call-start = ((), (), s32[]{:S(2)}) async-start(), calls=%async_computation.28 | async-start | bytes 2621440
  1134.1 114.9 %all-gather.19.cloned.1.call-start = ((), (), s32[]{:S(2)}) async-start(), calls=%async_computation.21 | async-start | bytes 7864320 | tf_op jit(solution)/shard_map/all_gather | solution.py:55
  1201.6 116.4 %all-reduce.28.cloned.1.call-start = ((), (), s32[]{:S(2)}) async-start(), calls=%async_computation.22 | async-start | bytes 4194304 | tf_op jit(solution)/shard_map/psum | solution.py:41
  1255.0 159.6 %reduce-scatter.23.cloned.1.call-start = ((), (), s32[]{:S(2)}) async-start(), calls=%async_computation.23 | async-start | bytes 10485760 | tf_op jit(solution)/shard_map/reduce_scatter | solution.py:45
  1343.6 136.2 %all-gather.25.cloned.1.call-start = ((), (), s32[]{:S(2)}) async-start(), calls=%async_computation.27 | async-start | bytes 10485760 | tf_op jit(solution)/shard_map/all_gather | solution.py:55
  1421.4 128.7 %all-reduce.30.cloned.1.call-start = ((), (), s32[]{:S(2)}) async-start(), calls=%async_computation.24 | async-start | bytes 4194304 | tf_op jit(solution)/shard_map/psum | solution.py:41
  1487.0 119.8 %reduce-scatter.27.cloned.1.call-start = ((), (), s32[]{:S(2)}) async-start(), calls=%async_computation.29 | async-start | bytes 2621440
  1576.1 91.1 %all-gather.17.cloned.1.call-start = ((), (), s32[]{:S(2)}) async-start(), calls=%async_computation.18 | async-start | bytes 10485760 | tf_op jit(solution)/shard_map/all_gather | solution.py:37
  1581.7 134.3 %all-gather.21.cloned.1.call-start = ((), (), s32[]{:S(2)}) async-start(), calls=%async_computation.25 | async-start | bytes 7864320 | tf_op jit(solution)/shard_map/all_gather | solution.py:55
  1651.8 178.8 %all-reduce.32.cloned.1.call-start = ((), (), s32[]{:S(2)}) async-start(), calls=%async_computation.30 | async-start | bytes 8388608 | tf_op jit(solution)/shard_map/psum | solution.py:41
  1722.2 338.1 %all-reduce.34.cloned.1.call-start = ((), (), s32[]{:S(2)}) async-start(), calls=%async_computation.31 | async-start | bytes 12582912 | tf_op jit(solution)/shard_map/psum | solution.py:289
  (100 other events, 1878.1 us)
Sparse Core Ops, SparseCore 0:
  32.9 99.3 reduce-scatter.12
  162.6 22.5 all-gather.10
  189.0 62.9 all-reduce.19
  274.2 125.2 reduce-scatter.14
  404.6 58.2 all-gather.12
  470.3 62.9 all-reduce.21
  556.5 98.1 reduce-scatter.16
  683.3 22.5 all-gather.14
  709.7 62.9 all-reduce.23
  775.1 71.7 reduce-scatter.20
  849.6 126.1 reduce-scatter.18
  982.6 58.2 all-gather.22
  1048.4 62.9 all-reduce.25
  1134.2 30.4 reduce-scatter.24
  1201.7 47.2 all-gather.18
  1255.1 62.9 all-reduce.27
  1343.8 70.8 reduce-scatter.22
  1421.5 58.2 all-gather.24
  1487.1 62.9 all-reduce.29
  1576.2 30.4 reduce-scatter.26
  1608.9 58.2 all-gather.16
  1668.8 47.2 all-gather.20
  1722.3 108.2 all-reduce.31
  1834.8 225.4 all-reduce.33
where the time goes:
time: 2090 us; the launch traced here: 2080 us
  waiting for transfers between devices  1570 us (75%)
  matrix products  189 us (9%)
  blocking collectives  113 us (5%)
  other arithmetic  109 us (5%)
  local copies, waits for them, and re-layouts  75.6 us (4%)
    reduce_scatter x4, waiting for transfers between devices, in_parts(): lax.psum_scatter(partial_sums, 'row', scatter_dimension=2, tiled=True)  450 us
    psum x7, waiting for transfers between devices, col_total(): return lax.psum(partial_sums, 'col')  442 us
    all_gather x4, waiting for transfers between devices, grad_gather(): return lax.all_gather(block, 'row', axis=2, tiled=True)  197 us
    psum x1, waiting for transfers between devices, on_device(): lax.psum(terms[2].astype(jnp.bfloat16), 'dp').astype(jnp.float32)  185 us
    reduce_scatter x2, waiting for transfers between devices, rows_back(): lax.psum_scatter(partial_sums.astype(jnp.bfloat16), 'row', scatter_dimens...  122 us
    all_gather x4, waiting for transfers between devices, gather_rows(): return lax.all_gather(block, 'row', axis=1, tiled=True)  119 us
    unnamed x26, waiting for transfers between devices  56 us
    psum x4, blocking collectives, norm_forward(): lax.psum((jnp.sum(stream, axis=1), jnp.sum(stream * stream, axis=1)), 'row')  46.5 us
  transfers between devices with their start and end apart: 24, of which 24 were waited for; matrix products, arithmetic and copies ran while one was open for 6% of the time, Pallas kernels for 0%

commit v1 on v0

--- a/solution.py
+++ b/solution.py
@@ -3,6 +3,8 @@
 import jax
 import jax.numpy as jnp
 from jax import lax
+from jax.experimental import pallas as pl
+from jax.experimental.pallas import tpu as pltpu
 from jax.sharding import PartitionSpec as P
 
 D = 1024
@@ -237,7 +239,7 @@
     return (start_grad, terms)
 
 
-def on_device(
+def general_plan(
     tokens,
     segments,
     norm_gain,
@@ -314,6 +316,780 @@
     )
 
 
+f32 = jnp.float32
+bf16 = jnp.bfloat16
+CHUNKS = 2
+SPAN = LEN // CHUNKS
+OWN = SPAN // 2
+WIDTH = D // 4
+QB = 256
+
+
+def fits_pairs(shape, arrays):
+    return (
+        shape["row"] == 4
+        and shape["col"] == 2
+        and shape["dp"] == 4
+        and arrays[0].shape == (2 * LEN, WIDTH)
+        and arrays[8].shape[2] == 8 * WIDTH
+    )
+
+
+def swap_row(value, bits):
+    return lax.ppermute(value, "row", [(i, i ^ bits) for i in range(4)])
+
+
+def swap_core(value):
+    return swap_row(value, 1)
+
+
+def swap_chip(value):
+    return swap_row(value, 2)
+
+
+def swap_col(value):
+    return lax.ppermute(value, "col", [(0, 1), (1, 0)])
+
+
+def after(value, *others):
+    return lax.optimization_barrier((value, *others))[0]
+
+
+def dp_total(value):
+    place = lax.axis_index("dp")
+    inner = (place == 1) | (place == 2)
+    kind = value.dtype
+    from_end = lax.ppermute(value, "dp", [(0, 1), (3, 2)])
+    half = (value.astype(f32) + from_end.astype(f32)).astype(kind)
+    from_inner = lax.ppermute(half, "dp", [(1, 2), (2, 1)])
+    whole = (half.astype(f32) + from_inner.astype(f32)).astype(kind)
+    back = lax.ppermute(whole, "dp", [(1, 0), (2, 3)])
+    return jnp.where(inner, whole, back)
+
+
+def half_of(value, index, axis):
+    size = value.shape[axis] // 2
+    return lax.dynamic_slice_in_dim(value, index * size, size, axis)
+
+
+def in_place(first, mine, other, axis):
+    return jnp.where(
+        first,
+        jnp.concatenate([mine, other], axis=axis),
+        jnp.concatenate([other, mine], axis=axis),
+    )
+
+
+def gather_weight(core, own, cut, join):
+    peer = swap_chip(own)
+    mine = [half_of(v, core, cut) for v in (own, peer)]
+    theirs = jnp.stack([half_of(v, 1 - core, cut) for v in (own, peer)])
+    theirs = swap_core(theirs)
+    return jnp.concatenate([mine[0], theirs[0], mine[1], theirs[1]], axis=join), peer
+
+
+def spread_grad(keep, give):
+    got = swap_core(give)
+    away = swap_chip(jnp.stack([keep[1], got[1]]))
+    own = jnp.stack([keep[0], got[0]])
+    total = dp_total((own.astype(f32) + away.astype(f32)).astype(bf16)).astype(f32)
+    return total[0], total[1]
+
+
+def dot(a, b):
+    return lax.dot_general(a, b, (((1,), (0,)), ((), ())), preferred_element_type=f32)
+
+
+def dot_nt(a, b):
+    return lax.dot_general(a, b, (((1,), (1,)), ((), ())), preferred_element_type=f32)
+
+
+def dot_tn(a, b):
+    return lax.dot_general(a, b, (((0,), (0,)), ((), ())), preferred_element_type=f32)
+
+
+def kernel_call(body, outs, args, flops, grid=None, in_specs=None, out_specs=None, scratch=(), limit=40):
+    moved = sum(math.prod(v.shape) * v.dtype.itemsize for v in (*outs, *args))
+    whole = pl.BlockSpec(memory_space=pltpu.VMEM)
+    if in_specs is None:
+        in_specs = [
+            pl.BlockSpec(memory_space=pltpu.SMEM) if v.dtype == jnp.int32 and v.size == 1 else whole
+            for v in args
+        ]
+    extra = {} if grid is None else {"grid": grid}
+    return pl.pallas_call(
+        body,
+        out_shape=outs,
+        in_specs=in_specs,
+        out_specs=out_specs if out_specs is not None else [whole] * len(outs),
+        scratch_shapes=list(scratch),
+        compiler_params=pltpu.CompilerParams(vmem_limit_bytes=limit * 1024 * 1024),
+        cost_estimate=pl.CostEstimate(flops=flops, bytes_accessed=moved, transcendentals=0),
+        **extra,
+    )(*args)
+
+
+def like(shape, kind):
+    return jax.ShapeDtypeStruct(shape, kind)
+
+
+def other_order(value):
+    b = [value[:, k * WIDTH : (k + 1) * WIDTH] for k in range(4)]
+    return jnp.concatenate([b[1], b[0], b[3], b[2]], axis=1)
+
+
+def part_rows(index):
+    return pl.ds(pl.multiple_of(index * OWN, OWN), OWN)
+
+
+def join_tokens(core_ref, own_ref, sib_ref, full_ref):
+    core = core_ref[0]
+    full_ref[part_rows(core), :] = own_ref[...]
+    full_ref[part_rows(1 - core), :] = other_order(sib_ref[...])
+
+
+def part_tokens(core_ref, sums_ref, mine_ref, other_ref):
+    core = core_ref[0]
+    mine_ref[...] = sums_ref[part_rows(core), :]
+    other_ref[...] = other_order(sums_ref[part_rows(1 - core), :]).astype(bf16)
+
+
+def head_lanes(h):
+    lane = lax.broadcasted_iota(jnp.int32, (1, WIDTH), 1)
+    return (lane >= h * HD) & (lane < (h + 1) * HD)
+
+
+def allowed_pairs(seg_col, seg_row, start, keys):
+    same = seg_col == seg_row
+    query = lax.broadcasted_iota(jnp.int32, (QB, keys), 0) + start
+    key = lax.broadcasted_iota(jnp.int32, (QB, keys), 1)
+    return same & (key <= query)
+
+
+HEADS_HERE = WIDTH // HD
+
+
+def attend_body(chunk, *refs):
+    core_ref, own_ref, sib_ref, triple_w_ref, bias_ref, output_w_ref, col_ref, row_ref = refs[:8]
+    earlier = refs[8 : 8 + chunk]
+    full_ref, triple_ref, mixed_ref, log_ref, mine_ref, other_ref = refs[8 + chunk : 14 + chunk]
+    kv_ref, sums_ref = refs[14 + chunk :]
+    scale = 1.0 / math.sqrt(HD)
+    join_tokens(core_ref, own_ref, sib_ref, full_ref)
+    for part in range(3):
+        cols = slice(part * WIDTH, (part + 1) * WIDTH)
+        triple_ref[:, cols] = (
+            dot(full_ref[...], triple_w_ref[:, cols]) + bias_ref[:, cols]
+        ).astype(bf16)
+    for k in range(chunk):
+        kv_ref[k * SPAN : (k + 1) * SPAN, :] = earlier[k][:, WIDTH:]
+    kv_ref[chunk * SPAN :, :] = triple_ref[:, WIDTH:]
+    for block in range(SPAN // QB):
+        rows = slice(block * QB, (block + 1) * QB)
+        start = chunk * SPAN + block * QB
+        keys = start + QB
+        allowed = allowed_pairs(col_ref[start : start + QB, :], row_ref[:, :keys], start, keys)
+        queries = triple_ref[rows, :WIDTH] * scale
+        key_rows = kv_ref[:keys, :WIDTH]
+        value_rows = kv_ref[:keys, WIDTH:]
+        blended = jnp.zeros((QB, WIDTH), f32)
+        for h in range(HEADS_HERE):
+            lanes = head_lanes(h)
+            scores = dot_nt(jnp.where(lanes, queries, 0).astype(bf16), key_rows)
+            scores = jnp.where(allowed, scores, masked)
+            peak = jnp.max(scores, axis=1, keepdims=True)
+            exponent = jnp.exp(scores - peak)
+            total = jnp.sum(exponent, axis=1, keepdims=True)
+            soft = (exponent * (1.0 / total)).astype(bf16)
+            blended = jnp.where(lanes, dot(soft, value_rows), blended)
+            log_ref[rows, h : h + 1] = peak + jnp.log(total)
+        mixed_ref[rows, :] = blended.astype(bf16)
+    sums_ref[...] = dot(mixed_ref[...], output_w_ref[...])
+    part_tokens(core_ref, sums_ref, mine_ref, other_ref)
+
+
+def attend_call(chunk, core, own, sib, triple_w, bias, output_w, seg_col, seg_row, earlier):
+    return kernel_call(
+        lambda *refs: attend_body(chunk, *refs),
+        [
+            like((SPAN, D), bf16),
+            like((SPAN, 3 * WIDTH), bf16),
+            like((SPAN, WIDTH), bf16),
+            like((SPAN, 128), f32),
+            like((OWN, D), f32),
+            like((OWN, D), bf16),
+        ],
+        (core, own, sib, triple_w, bias, output_w, seg_col, seg_row, *earlier),
+        2 * SPAN * D * 4 * WIDTH + 8 * 4 * SPAN * (chunk + 1) * SPAN * WIDTH,
+        scratch=[pltpu.VMEM(((chunk + 1) * SPAN, 2 * WIDTH), bf16), pltpu.VMEM((SPAN, D), f32)],
+    )
+
+
+GELU = math.sqrt(2.0 / math.pi)
+
+
+def mlp_body(core_ref, own_ref, sib_ref, up_ref, bias_ref, down_ref, *refs):
+    full_ref, pre_ref, active_ref, mine_ref, other_ref, sums_ref = refs
+    step = pl.program_id(0)
+
+    @pl.when(step == 0)
+    def _():
+        join_tokens(core_ref, own_ref, sib_ref, full_ref)
+
+    pre = dot(full_ref[...], up_ref[...]) + bias_ref[...]
+    pre_ref[...] = pre
+    curve = jnp.tanh(GELU * (pre + 0.044715 * (pre * pre * pre)))
+    active = (0.5 * pre * (1.0 + curve)).astype(bf16)
+    active_ref[...] = active
+    sums = dot(active, down_ref[...])
+
+    @pl.when(step == 0)
+    def _():
+        sums_ref[...] = sums
+
+    @pl.when(step > 0)
+    def _():
+        sums_ref[...] += sums
+
+    @pl.when(step == pl.num_programs(0) - 1)
+    def _():
+        part_tokens(core_ref, sums_ref, mine_ref, other_ref)
+
+
+def mlp_call(core, own, sib, up_w, bias, down_w):
+    units = up_w.shape[1]
+    step = 256
+    whole = pl.BlockSpec((OWN, D), lambda i: (0, 0))
+    return kernel_call(
+        mlp_body,
+        [
+            like((SPAN, D), bf16),
+            like((SPAN, units), f32),
+            like((SPAN, units), bf16),
+            like((OWN, D), f32),
+            like((OWN, D), bf16),
+        ],
+        (core, own, sib, up_w, bias, down_w),
+        4 * SPAN * D * units,
+        grid=(units // step,),
+        in_specs=[
+            pl.BlockSpec(memory_space=pltpu.SMEM),
+            whole,
+            whole,
+            pl.BlockSpec((D, step), lambda i: (0, i)),
+            pl.BlockSpec((1, step), lambda i: (0, i)),
+            pl.BlockSpec((step, D), lambda i: (i, 0)),
+        ],
+        out_specs=[
+            pl.BlockSpec((SPAN, D), lambda i: (0, 0)),
+            pl.BlockSpec((SPAN, step), lambda i: (0, i)),
+            pl.BlockSpec((SPAN, step), lambda i: (0, i)),
+            whole,
+            whole,
+        ],
+        scratch=[pltpu.VMEM((SPAN, D), f32)],
+    )
+
+
+def mlp_back_body(core_ref, own_ref, sib_ref, down_ref, pre_ref, up_ref, *refs):
+    full_ref, hidden_ref, bias_ref, mine_ref, other_ref, sums_ref = refs
+    step = pl.program_id(0)
+
+    @pl.when(step == 0)
+    def _():
+        join_tokens(core_ref, own_ref, sib_ref, full_ref)
+
+    active_grad = dot_nt(full_ref[...], down_ref[...])
+    pre = pre_ref[...]
+    square = pre * pre
+    curve = jnp.tanh(GELU * (pre + 0.044715 * (square * pre)))
+    slope = 0.5 * (1.0 + curve) + (0.5 * GELU) * pre * (1.0 - curve * curve) * (
+        1.0 + (3.0 * 0.044715) * square
+    )
+    hidden = (active_grad * slope).astype(bf16)
+    hidden_ref[...] = hidden
+    bias_ref[...] = jnp.sum(hidden.astype(f32), axis=0, keepdims=True)
+    sums = dot_nt(hidden, up_ref[...])
+
+    @pl.when(step == 0)
+    def _():
+        sums_ref[...] = sums
+
+    @pl.when(step > 0)
+    def _():
+        sums_ref[...] += sums
+
+    @pl.when(step == pl.num_programs(0) - 1)
+    def _():
+        part_tokens(core_ref, sums_ref, mine_ref, other_ref)
+
+
+def mlp_back_call(core, own, sib, down_w, pre, up_w):
+    units = up_w.shape[1]
+    step = 256
+    whole = pl.BlockSpec((OWN, D), lambda i: (0, 0))
+    return kernel_call(
+        mlp_back_body,
+        [
+            like((SPAN, D), bf16),
+            like((SPAN, units), bf16),
+            like((1, units), f32),
+            like((OWN, D), f32),
+            like((OWN, D), bf16),
+        ],
+        (core, own, sib, down_w, pre, up_w),
+        4 * SPAN * D * units,
+        grid=(units // step,),
+        in_specs=[
+            pl.BlockSpec(memory_space=pltpu.SMEM),
+            whole,
+            whole,
+            pl.BlockSpec((step, D), lambda i: (i, 0)),
+            pl.BlockSpec((SPAN, step), lambda i: (0, i)),
+            pl.BlockSpec((D, step), lambda i: (0, i)),
+        ],
+        out_specs=[
+            pl.BlockSpec((SPAN, D), lambda i: (0, 0)),
+            pl.BlockSpec((SPAN, step), lambda i: (0, i)),
+            pl.BlockSpec((1, step), lambda i: (0, i)),
+            whole,
+            whole,
+        ],
+        scratch=[pltpu.VMEM((SPAN, D), f32)],
+    )
+
+
+def attend_back_body(chunk, later, *refs):
+    core_ref, own_ref, sib_ref, output_w_ref, triple_w_ref, log_ref, col_ref, row_ref = refs[:8]
+    triples = refs[8 : 9 + chunk]
+    refs = refs[9 + chunk :]
+    if later:
+        carried_ref, refs = refs[0], refs[1:]
+    full_ref, rows_ref, bias_ref, mine_ref, other_ref = refs[:5]
+    refs = refs[5:]
+    if chunk:
+        carry_ref, refs = refs[0], refs[1:]
+    kv_ref, grad_ref, total_ref, sums_ref = refs
+    scale = 1.0 / math.sqrt(HD)
+    triple_ref = triples[chunk]
+    join_tokens(core_ref, own_ref, sib_ref, full_ref)
+    grad_ref[...] = dot_nt(full_ref[...], output_w_ref[...]).astype(bf16)
+    for k in range(chunk + 1):
+        kv_ref[k * SPAN : (k + 1) * SPAN, :] = triples[k][:, WIDTH:]
+    if later:
+        total_ref[...] = carried_ref[...]
+    else:
+        total_ref[...] = jnp.zeros_like(total_ref)
+    for block in range(SPAN // QB):
+        rows = slice(block * QB, (block + 1) * QB)
+        start = chunk * SPAN + block * QB
+        keys = start + QB
+        allowed = allowed_pairs(col_ref[start : start + QB, :], row_ref[:, :keys], start, keys)
+        queries = triple_ref[rows, :WIDTH] * scale
+        grads = grad_ref[rows, :]
+        key_rows = kv_ref[:keys, :WIDTH]
+        value_rows = kv_ref[:keys, WIDTH:]
+        query_grad = jnp.zeros((QB, WIDTH), f32)
+        for h in range(HEADS_HERE):
+            lanes = head_lanes(h)
+            query = jnp.where(lanes, queries, 0).astype(bf16)
+            grad = jnp.where(lanes, grads, 0).astype(bf16)
+            scores = jnp.where(allowed, dot_nt(query, key_rows), masked)
+            chances = jnp.exp(scores - log_ref[rows, h : h + 1])
+            product = chances * dot_nt(grad, value_rows)
+            inner = jnp.sum(product, axis=1, keepdims=True)
+            score_grad = (product - chances * inner).astype(bf16)
+            query_grad = jnp.where(lanes, dot(score_grad, key_rows), query_grad)
+            total_ref[:keys, :WIDTH] += dot_tn(score_grad, query)
+            total_ref[:keys, WIDTH:] += dot_tn(chances.astype(bf16), grad)
+        rows_ref[rows, :WIDTH] = (query_grad * scale).astype(bf16)
+    rows_ref[:, WIDTH:] = total_ref[chunk * SPAN :, :].astype(bf16)
+    if chunk:
+        carry_ref[...] = total_ref[: chunk * SPAN, :]
+    bias_ref[0:1, :] = jnp.sum(rows_ref[:, :WIDTH].astype(f32), axis=0, keepdims=True)
+    bias_ref[1:2, :] = jnp.sum(rows_ref[:, 2 * WIDTH :].astype(f32), axis=0, keepdims=True)
+    sums_ref[...] = dot_nt(rows_ref[...], triple_w_ref[...])
+    part_tokens(core_ref, sums_ref, mine_ref, other_ref)
+
+
+def attend_back_call(
+    chunk, core, own, sib, output_w, triple_w, logs, seg_col, seg_row, triples, carried
+):
+    outs = [
+        like((SPAN, D), bf16),
+        like((SPAN, 3 * WIDTH), bf16),
+        like((2, WIDTH), f32),
+        like((OWN, D), f32),
+        like((OWN, D), bf16),
+    ]
+    if chunk:
+        outs.append(like((chunk * SPAN, 2 * WIDTH), f32))
+    later = () if carried is None else (carried,)
+    return kernel_call(
+        lambda *refs: attend_back_body(chunk, bool(later), *refs),
+        outs,
+        (core, own, sib, output_w, triple_w, logs, seg_col, seg_row, *triples, *later),
+        2 * SPAN * D * 4 * WIDTH + 20 * 4 * SPAN * (chunk + 1) * SPAN * WIDTH,
+        scratch=[
+            pltpu.VMEM(((chunk + 1) * SPAN, 2 * WIDTH), bf16),
+            pltpu.VMEM((SPAN, WIDTH), bf16),
+            pltpu.VMEM(((chunk + 1) * SPAN, 2 * WIDTH), f32),
+            pltpu.VMEM((SPAN, D), f32),
+        ],
+    )
+
+
+def weight_grad_body(join, *refs):
+    left, right = refs[:CHUNKS], refs[CHUNKS : 2 * CHUNKS]
+    keep_ref, give_ref = refs[2 * CHUNKS :]
+    total = dot_tn(left[0][...], right[0][...])
+    for k in range(1, CHUNKS):
+        total += dot_tn(left[k][...], right[k][...])
+    total = total.astype(bf16)
+    if join == 0:
+        keep_ref[0] = total[:WIDTH]
+        give_ref[0] = total[WIDTH:]
+    else:
+        for k in range(2):
+            keep_ref[k] = total[:, 2 * k * WIDTH : (2 * k + 1) * WIDTH]
+            give_ref[k] = total[:, (2 * k + 1) * WIDTH : (2 * k + 2) * WIDTH]
+
+
+def weight_grad(left, right, join):
+    high, across = left[0].shape[1], right[0].shape[1]
+    part = min(512, high)
+    steps = high // part
+    if join == 0:
+        shape = (2, WIDTH, across)
+        out = pl.BlockSpec((1, WIDTH, across), lambda i: (i, 0, 0))
+    else:
+        shape = (2, high, WIDTH)
+        out = pl.BlockSpec((2, part, WIDTH), lambda i: (0, i, 0))
+    return kernel_call(
+        lambda *refs: weight_grad_body(join, *refs),
+        [like(shape, bf16)] * 2,
+        (*left, *right),
+        2 * LEN * high * across,
+        grid=(steps,),
+        in_specs=[pl.BlockSpec((SPAN, part), lambda i: (0, i))] * CHUNKS
+        + [pl.BlockSpec((SPAN, across), lambda i: (0, 0))] * CHUNKS,
+        out_specs=[out, out],
+    )
+
+
+def mean_lanes(v):
+    return jnp.sum(v, axis=1, keepdims=True) * (1.0 / D)
+
+
+def norm_parts(v):
+    center = mean_lanes(v)
+    second = mean_lanes(v * v) - center * center
+    inv_std = lax.rsqrt(second + eps)
+    return (v - center) * inv_std, inv_std
+
+
+def norm_body(stream_ref, chip_ref, got_ref, bias_ref, gain_ref, shift_ref, after_ref, out_ref):
+    total = chip_ref[...].astype(f32) + got_ref[...].astype(f32)
+    after_sum = stream_ref[...] + (total + bias_ref[...])
+    after_ref[...] = after_sum
+    normed, _ = norm_parts(after_sum)
+    out_ref[...] = (normed * gain_ref[...] + shift_ref[...]).astype(bf16)
+
+
+def norm_call(stream, chip, got, bias, gain, shift):
+    return kernel_call(
+        norm_body,
+        [like((OWN, D), f32), like((OWN, D), bf16)],
+        (stream, chip, got, bias[None], gain[None], shift[None]),
+        20 * OWN * D,
+    )
+
+
+def norm_back_body(grad_ref, chip_ref, got_ref, stream_ref, gain_ref, out_ref, low_ref, sums_ref):
+    grad_out = chip_ref[...].astype(f32) + got_ref[...].astype(f32)
+    normed, inv_std = norm_parts(stream_ref[...])
+    scaled = grad_out * gain_ref[...]
+    total = grad_ref[...] + inv_std * (
+        scaled - mean_lanes(scaled) - normed * mean_lanes(scaled * normed)
+    )
+    low = total.astype(bf16)
+    out_ref[...] = total
+    low_ref[...] = low
+    sums_ref[0:1, :] = jnp.sum(grad_out * normed, axis=0, keepdims=True)
+    sums_ref[1:2, :] = jnp.sum(grad_out, axis=0, keepdims=True)
+    sums_ref[2:3, :] = jnp.sum(low.astype(f32), axis=0, keepdims=True)
+
+
+def norm_back_call(grad, chip, got, stream, gain):
+    return kernel_call(
+        norm_back_body,
+        [like((OWN, D), f32), like((OWN, D), bf16), like((3, D), f32)],
+        (grad, chip, got, stream, gain[None]),
+        30 * OWN * D,
+    )
+
+
+def chip_total(mine, other):
+    return (mine + swap_core(other).astype(f32)).astype(bf16)
+
+
+def pair_plan(
+    tokens,
+    segments,
+    norm_gain,
+    norm_shift,
+    triple_weight,
+    triple_bias,
+    output_weight,
+    output_bias,
+    up_weight,
+    up_bias,
+    down_weight,
+    down_bias,
+    cotangent,
+):
+    row = lax.axis_index("row")
+    core = row % 2
+    chip = row // 2
+    first = core == 0
+    core_id = core.astype(jnp.int32).reshape(1)
+    chunks = range(CHUNKS)
+
+    def to_tokens(block):
+        def of_owner(j):
+            start = (row ^ j) // 2 * LEN + (row ^ j) % 2 * OWN
+            return jnp.concatenate(
+                [lax.dynamic_slice_in_dim(block, start + k * SPAN, OWN, 0) for k in chunks]
+            )
+
+        parts = [of_owner(j) for j in range(4)]
+        got = [parts[0]] + [swap_row(parts[j], j) for j in range(1, 4)]
+        whole = jnp.concatenate(got, axis=1)
+        return [whole[k * OWN : (k + 1) * OWN] for k in chunks]
+
+    def to_features(pieces):
+        whole = jnp.concatenate(pieces)
+        parts = jnp.split(whole, 4, axis=1)
+        got = [parts[0]] + [swap_row(parts[j], j) for j in range(1, 4)]
+        halves = [jnp.stack(pair).reshape(2, CHUNKS, OWN, WIDTH) for pair in (got[:2], got[2:])]
+        packs = []
+        for pair in halves:
+            pair = jnp.where(first, pair, pair[::-1])
+            packs.append(jnp.swapaxes(pair, 0, 1).reshape(LEN, WIDTH))
+        return jnp.where(
+            chip == 0,
+            jnp.concatenate(packs),
+            jnp.concatenate(packs[::-1]),
+        )
+
+    streams = [v.astype(f32) for v in to_tokens(tokens)]
+    seg_pack = lax.dynamic_slice_in_dim(segments, chip * LEN, LEN, 0)
+    seg_col, seg_row = seg_pack[:, None], seg_pack[None, :]
+
+    flat = jnp.concatenate(
+        [
+            v.reshape(-1)
+            for v in (norm_gain, norm_shift, output_bias, down_bias, triple_bias, up_bias)
+        ]
+    ).reshape(-1, 128)
+    small = jnp.stack([flat] + [swap_row(flat, j) for j in range(1, 4)]).astype(f32)
+    small = small.reshape(4, -1)
+    at = 0
+
+    def take(shape):
+        nonlocal at
+        size = math.prod(shape)
+        part = small[:, at : at + size].reshape((4,) + shape)
+        at += size
+        return part
+
+    def wide(part):
+        return jnp.moveaxis(part, 0, -2).reshape(part.shape[1:-1] + (-1,))
+
+    def of_core(part):
+        pick = [
+            lax.dynamic_index_in_dim(part, row ^ (2 * core + b), 0, keepdims=False)
+            for b in range(2)
+        ]
+        return jnp.concatenate(pick, axis=-1)
+
+    gains = wide(take((LAYERS, 2, WIDTH)))
+    shifts = wide(take((LAYERS, 2, WIDTH)))
+    output_b = wide(take((LAYERS, WIDTH)))
+    down_b = wide(take((LAYERS, WIDTH)))
+    triple_b = of_core(take((LAYERS, 2, D // 8)))
+    up_b = of_core(take((LAYERS,) + up_bias.shape[1:]))
+
+    weights = []
+    last = [streams[0], streams[0]]
+    for layer in range(LAYERS):
+        triple_w, p0 = gather_weight(
+            core, after(jnp.swapaxes(triple_weight[layer], 0, 1), last[0]), 2, 1
+        )
+        triple_w = jnp.concatenate([triple_w[0], triple_w[1], triple_w[2]], axis=1)
+        output_w, p1 = gather_weight(core, after(output_weight[layer], last[1]), 0, 1)
+        up_w, p2 = gather_weight(core, after(up_weight[layer], p0), 1, 0)
+        down_w, p3 = gather_weight(core, after(down_weight[layer], p1), 0, 1)
+        last = [p2, p3]
+        weights.append((triple_w, output_w, up_w, down_w))
+
+    stored = []
+    low = []
+    for k in chunks:
+        normed, _ = norm_parts(streams[k])
+        low.append((normed * gains[0, 0] + shifts[0, 0]).astype(bf16))
+    for layer in range(LAYERS):
+        triple_w, output_w, up_w, down_w = weights[layer]
+        bias = jnp.concatenate(
+            [triple_b[layer, 0], jnp.zeros_like(triple_b[layer, 0]), triple_b[layer, 1]]
+        )[None]
+        saved = {name: [] for name in ("start", "attn", "triple", "mixed", "logs", "middle")}
+        saved.update({name: [] for name in ("mlp", "pre", "active")})
+        saved["start"] = streams
+        for k in chunks:
+            attn, triple, mixed, logs, mine, other = attend_call(
+                k,
+                core_id,
+                low[k],
+                swap_core(low[k]),
+                triple_w,
+                bias,
+                output_w,
+                seg_col,
+                seg_row,
+                saved["triple"],
+            )
+            total = chip_total(mine, other)
+            middle, mlp_own = norm_call(
+                streams[k], total, swap_col(total), output_b[layer], gains[layer, 1], shifts[layer, 1]
+            )
+            for name, value in (
+                ("attn", attn),
+                ("triple", triple),
+                ("mixed", mixed),
+                ("logs", logs),
+                ("middle", middle),
+            ):
+                saved[name].append(value)
+            low[k] = mlp_own
+        streams = []
+        for k in chunks:
+            mlp, pre, active, mine, other = mlp_call(
+                core_id, low[k], swap_core(low[k]), up_w, up_b[layer][None], down_w
+            )
+            total = chip_total(mine, other)
+            if layer + 1 < LAYERS:
+                stream, low[k] = norm_call(
+                    saved["middle"][k],
+                    total,
+                    swap_col(total),
+                    down_b[layer],
+                    gains[layer + 1, 0],
+                    shifts[layer + 1, 0],
+                )
+            else:
+                both = total.astype(f32) + swap_col(total).astype(f32)
+                stream = saved["middle"][k] + (both + down_b[layer])
+            for name, value in (("mlp", mlp), ("pre", pre), ("active", active)):
+                saved[name].append(value)
+            streams.append(stream)
+        stored.append(saved)
+
+    result = to_features([v.astype(bf16) for v in streams])
+    low = to_tokens(cotangent)
+    grad = [v.astype(f32) for v in low]
+    low_sums = sum(jnp.sum(v, axis=0) for v in grad)
+    grads = [None] * LAYERS
+    for layer in reversed(range(LAYERS)):
+        triple_w, output_w, up_w, down_w = weights[layer]
+        saved = stored[layer]
+        down_bias_grad = low_sums
+        down_in, hidden, branch, triple_rows = ([None] * CHUNKS for _ in range(4))
+        sums_two, sums_one = [], []
+        up_bias_grad, triple_bias_grad = [], []
+        for k in reversed(chunks):
+            down_in[k], hidden[k], bias, mine, other = mlp_back_call(
+                core_id, low[k], swap_core(low[k]), down_w, saved["pre"][k], up_w
+            )
+            up_bias_grad.append(bias[0])
+            total = chip_total(mine, other)
+            grad[k], low[k], sums = norm_back_call(
+                grad[k], total, swap_col(total), saved["middle"][k], gains[layer, 1]
+            )
+            sums_two.append(sums)
+        down_grad = spread_grad(*weight_grad(saved["active"], down_in, 1))
+        up_grad = spread_grad(*weight_grad(saved["mlp"], hidden, 0))
+        carried = None
+        for k in reversed(chunks):
+            branch[k], triple_rows[k], bias, mine, other, *carry = attend_back_call(
+                k,
+                core_id,
+                low[k],
+                swap_core(low[k]),
+                output_w,
+                triple_w,
+                saved["logs"][k],
+                seg_col,
+                seg_row,
+                saved["triple"][: k + 1],
+                carried,
+            )
+            carried = carry[0] if carry else None
+            triple_bias_grad.append(bias)
+            total = chip_total(mine, other)
+            grad[k], low[k], sums = norm_back_call(
+                grad[k], total, swap_col(total), saved["start"][k], gains[layer, 0]
+            )
+            sums_one.append(sums)
+        output_grad = spread_grad(*weight_grad(saved["mixed"], branch, 1))
+        triple_grad = spread_grad(*weight_grad(saved["attn"], triple_rows, 0))
+        sums_one, sums_two = sum(sums_one), sum(sums_two)
+        up_bias_grad, triple_bias_grad = sum(up_bias_grad), sum(triple_bias_grad)
+        low_sums = sums_one[2]
+
+        full = jnp.stack(
+            [sums_one[0], sums_two[0], sums_one[1], sums_two[1], sums_two[2], down_bias_grad]
+        )
+        full = jnp.moveaxis(full.reshape(6, 4, WIDTH), 1, 0)
+        theirs = swap_core(full)
+        full = full + jnp.stack([theirs[1], theirs[0], theirs[3], theirs[2]])
+        full = full[0] + swap_chip(full[2])
+        pieces = jnp.concatenate(
+            [
+                jnp.moveaxis(triple_bias_grad.reshape(2, 2, D // 8), 1, 0).reshape(2, -1),
+                up_bias_grad.reshape(2, -1),
+            ],
+            axis=1,
+        )
+        pieces = pieces + swap_chip(pieces)
+        give = lax.dynamic_index_in_dim(pieces, 1 - core, 0, keepdims=False)
+        keep = lax.dynamic_index_in_dim(pieces, core, 0, keepdims=False)
+        share = jnp.where(chip == core, keep, swap_core(give))
+        packed = jnp.concatenate([full.reshape(-1), share]).reshape(-1, 128)
+        packed = dp_total(packed).reshape(-1)
+        full = packed[: 6 * WIDTH].reshape(6, WIDTH)
+        share = packed[6 * WIDTH :]
+        thirds = [slice(part * WIDTH, (part + 1) * WIDTH) for part in range(3)]
+        grads[layer] = (
+            full[0:2],
+            full[2:4],
+            jnp.stack(
+                [in_place(first, triple_grad[0][:, s], triple_grad[1][:, s], 1) for s in thirds],
+                axis=1,
+            ),
+            share[: D // 4].reshape(2, D // 8),
+            in_place(first, output_grad[0], output_grad[1], 0),
+            full[4],
+            in_place(first, up_grad[0], up_grad[1], 1),
+            share[D // 4 :],
+            in_place(first, down_grad[0], down_grad[1], 0),
+            full[5],
+        )
+    input_grad = to_features(low).astype(f32)
+    stacks = [jnp.stack([grads[layer][k] for layer in range(LAYERS)]) for k in range(10)]
+    return (result, input_grad, *stacks)
+
+
 def solution(mesh):
     in_specs = (
         P("dp", "row"),
@@ -344,6 +1120,13 @@
         P(None, "col", "row"),
         P(None, "row"),
     )
+    shape = mesh.shape
+
+    def on_device(*arrays):
+        if fits_pairs(shape, arrays):
+            return pair_plan(*arrays)
+        return general_plan(*arrays)
+
     return jax.shard_map(
         on_device, mesh=mesh, in_specs=in_specs, out_specs=out_specs, check_vma=False
     )

time: 2090 us -> 849 us (0.41)
  waiting for transfers between devices: 1570 us -> 348 us
  matrix products: 189 us -> 0 us
  Pallas kernels: 0 us -> 145 us
  starting transfers between devices: 1.58 us -> 128 us
  blocking collectives: 113 us -> 0 us
  local copies, waits for them, and re-layouts: 75.6 us -> 110 us
    psum x8 -> x0, waiting for transfers between devices: 627 us -> none  [the longest x7 442 us: col_total(): return lax.psum(partial_sums, 'col')]
    reduce_scatter x6 -> x0, waiting for transfers between devices: 572 us -> none  [the longest x4 450 us: in_parts(): lax.psum_scatter(partial_sums, 'row', scatter_dimension=2, tiled=True)]
    ppermute x0 -> x133, waiting for transfers between devices: none -> 348 us  [the longest x16 104 us: swap_col(): return lax.ppermute(value, 'col', [(0, 1), (1, 0)])]
    all_gather x8 -> x0, waiting for transfers between devices: 317 us -> none  [the longest x4 197 us: grad_gather(): return lax.all_gather(block, 'row', axis=2, tiled=True)]
    dot_general x52 -> x0, matrix products: 189 us -> none  [the longest x2 16.9 us: layer_forward(): jnp.dot(mlp_in, up_w, preferred_element_type=jnp.float32)[:, None, :]]
    pallas_call x0 -> x38, Pallas kernels: none -> 145 us  [kernel_call(): pl.pallas_call(body, out_shape=outs, in_specs=in_specs, out_specs=out_spe...]
    ppermute x0 -> x133, starting transfers between devices: none -> 128 us  [the longest x10 43.7 us: dp_total(): from_end = lax.ppermute(value, 'dp', [(0, 1), (3, 2)])]
    psum x9 -> x0, blocking collectives: 113 us -> none  [the longest x4 46.5 us: norm_forward(): lax.psum((jnp.sum(stream, axis=1), jnp.sum(stream * stream, axis=1)), 'row')]
  transfers between devices with their start and end apart: 24 -> 133, of which waited for: 24 -> 36; matrix products, arithmetic and copies ran while one was open for 6% -> 16% of each run, Pallas kernels for 0% -> 17%
where the time goes in v1:
time: 849 us; the launch traced here: 837 us
  waiting for transfers between devices  348 us (41%)
  Pallas kernels  145 us (17%)
  starting transfers between devices  128 us (15%)
  local copies, waits for them, and re-layouts  110 us (13%)
  other arithmetic  101 us (12%)
    pallas_call x38, Pallas kernels, kernel_call(): pl.pallas_call(body, out_shape=outs, in_specs=in_specs, out_specs=out_spe...  145 us
    ppermute x16, waiting for transfers between devices, swap_col(): return lax.ppermute(value, 'col', [(0, 1), (1, 0)])  104 us
    ppermute x87, waiting for transfers between devices, swap_row(): return lax.ppermute(value, 'row', [(i, i ^ bits) for i in range(4)])  102 us
    unnamed x430, local copies, waits for them, and re-layouts  75.6 us
    ppermute x10, waiting for transfers between devices, dp_total(): back = lax.ppermute(whole, 'dp', [(1, 0), (2, 3)])  74.4 us
    ppermute x10, waiting for transfers between devices, dp_total(): from_end = lax.ppermute(value, 'dp', [(0, 1), (3, 2)])  67.7 us
    ppermute x10, starting transfers between devices, dp_total(): from_end = lax.ppermute(value, 'dp', [(0, 1), (3, 2)])  43.7 us
    ppermute x87, starting transfers between devices, swap_row(): return lax.ppermute(value, 'row', [(i, i ^ bits) for i in range(4)])  42 us
  transfers between devices with their start and end apart: 133, of which 36 were waited for; matrix products, arithmetic and copies ran while one was open for 16% of the time, Pallas kernels for 17%

profile of v1, /device:TPU:0, one launch (start us, length us, event | category | flops | bytes accessed | tf_op | source)
XLA Modules:
  0.0 837.5 jit_solution(2619071503821431988)
XLA Ops:
  47.7 13.1 %collective-permute-done.7 = bf16[3,256,512]{2,1,0:T(8,128)(2,1)S(1)} collective-permute-done((bf16[3,256,512]{2,1,0:T(8,128)(2,1)S(1)}, bf16[3,256,512]{2,1,0:T(8,128)(2,1)S(1)}, u32[]{:S(2)}, u32[]{:S(2)}) %collective-permute-start.7) | collective-permute-done | bytes 786464 | tf_op jit(solution)/shard_map/ppermute | solution.py:339
  62.6 20.7 %collective-permute-done.16 = bf16[2048,256]{1,0:T(8,128)(2,1)S(1)} collective-permute-done((bf16[2048,256]{1,0:T(8,128)(2,1)S(1)}, bf16[2048,256]{1,0:T(8,128)(2,1)S(1)}, u32[]{:S(2)}, u32[]{:S(2)}) %collective-permute-start.16) | collective-permute-done | bytes 1048608 | tf_op jit(solution)/shard_map/ppermute | solution.py:339
  84.9 25.9 %collective-permute-done.23 = bf16[512,256]{1,0:T(8,128)(2,1)S(1)} collective-permute-done((bf16[512,256]{1,0:T(8,128)(2,1)S(1)}, bf16[512,256]{1,0:T(8,128)(2,1)S(1)}, u32[]{:S(2)}, u32[]{:S(2)}) %collective-permute-start.23) | collective-permute-done | bytes 262176 | tf_op jit(solution)/shard_map/ppermute | solution.py:339
  131.1 12.1 %collective-permute-done.12.got_ref = bf16[256,1024]{1,0:T(8,128)(2,1)S(1)} collective-permute-done((bf16[256,1024]{1,0:T(8,128)(2,1)S(1)}, bf16[256,1024]{1,0:T(8,128)(2,1)S(1)}, u32[]{:S(2)}, u32[]{:S(2)}) %collective-permute-start.12) | collective-permute-done | bytes 524320 | tf_op jit(solution)/shard_map/ppermute | solution.py:351
  145.9 8.0 collective-permute-done.36.got_ref
  164.8 6.9 shard_map.229
  179.0 11.6 %collective-permute-done.19.got_ref = bf16[256,1024]{1,0:T(8,128)(2,1)S(1)} collective-permute-done((bf16[256,1024]{1,0:T(8,128)(2,1)S(1)}, bf16[256,1024]{1,0:T(8,128)(2,1)S(1)}, u32[]{:S(2)}, u32[]{:S(2)}) %collective-permute-start.19) | collective-permute-done | bytes 524320 | tf_op jit(solution)/shard_map/ppermute | solution.py:351
  192.2 8.6 %collective-permute-done.39.got_ref = bf16[256,1024]{1,0:T(8,128)(2,1)S(1)} collective-permute-done((bf16[256,1024]{1,0:T(8,128)(2,1)S(1)}, bf16[256,1024]{1,0:T(8,128)(2,1)S(1)}, u32[]{:S(2)}, u32[]{:S(2)}) %collective-permute-start.39) | collective-permute-done | bytes 524320 | tf_op jit(solution)/shard_map/ppermute | solution.py:351
  224.5 9.5 %collective-permute-done.26.got_ref = bf16[256,1024]{1,0:T(8,128)(2,1)} collective-permute-done((bf16[256,1024]{1,0:T(8,128)(2,1)}, bf16[256,1024]{1,0:T(8,128)(2,1)}, u32[]{:S(2)}, u32[]{:S(2)}) %collective-permute-start.26) | collective-permute-done | bytes 524320 | tf_op jit(solution)/shard_map/ppermute | solution.py:351
  236.7 7.8 collective-permute-done.42.got_ref
  248.2 7.5 shard_map.226
  258.9 7.5 shard_map.233
  269.8 9.0 %shard_map.234 = (bf16[512,1024]{1,0:T(8,128)(2,1)S(1)}, bf16[512,1024]{1,0:T(8,128)(2,1)S(1)}, f32[1,1024]{1,0:T(1,128)S(1)}, f32[256,1024]{1,0:T(8,128)S(1)}, bf16[256,1024]{1,0:T(8,128)(2,1)}) custom-call(s32[1]{0:T(128)} %bitcast.refs_0_.core_ref, bf16[256,1024]{1,0:T(8,128)(2,1)} %get-tuple-element.361.own_ref, ...), custom_call_target="tpu_custom_call" | custom-call | flops 2147483648 | bytes 11014148 | tf_op jit(solution)/shard_map/pallas_call | solution.py:420
  282.0 7.9 shard_map.236
  322.9 10.7 %collective-permute-done.45 = bf16[256,1024]{1,0:T(8,128)(2,1)S(1)} collective-permute-done((bf16[256,1024]{1,0:T(8,128)(2,1)S(1)}, bf16[256,1024]{1,0:T(8,128)(2,1)S(1)}, u32[]{:S(2)}, u32[]{:S(2)}) %collective-permute-start.45) | collective-permute-done | bytes 524320 | tf_op jit(solution)/shard_map/ppermute | solution.py:351
  337.7 7.1 collective-permute-done.54.got_ref
  347.3 8.1 collective-permute-done.58.got_ref
  365.0 9.2 %shard_map.238 = (bf16[512,1024]{1,0:T(8,128)(2,1)S(1)}, bf16[512,768]{1,0:T(8,128)(2,1)S(1)}, f32[2,256]{1,0:T(2,128)S(1)}, f32[256,1024]{1,0:T(8,128)S(1)}, bf...) custom-call(s32[1]{0:T(128)} %bitcast.refs_0_.core_ref, bf16[256,1024]{1,0:T(8,128)(2,1)S(1)} %copy-done.86, ...), custom_call_target="tpu_custom_call" | custom-call | flops 11811160064 | bytes 9447428 | tf_op jit(solution)/shard_map/pallas_call | solution.py:420
  437.1 25.5 %collective-permute-done.110 = bf16[2,256,256]{2,1,0:T(8,128)(2,1)S(1)} collective-permute-done((bf16[2,256,256]{2,1,0:T(8,128)(2,1)S(1)}, bf16[2,256,256]{2,1,0:T(8,128)(2,1)S(1)}, u32[]{:S(2)}, u32[]{:S(2)}) %collective-permute-start.110) | collective-permute-done | bytes 262176 | tf_op jit(solution)/shard_map/ppermute | solution.py:362
  486.0 9.1 %collective-permute-done.112 = bf16[2,256,256]{2,1,0:T(8,128)(2,1)} collective-permute-done((bf16[2,256,256]{2,1,0:T(8,128)(2,1)}, bf16[2,256,256]{2,1,0:T(8,128)(2,1)}, u32[]{:S(2)}, u32[]{:S(2)}) %collective-permute-start.112) | collective-permute-done | bytes 262176 | tf_op jit(solution)/shard_map/ppermute | solution.py:366
  506.6 9.1 %shard_map.241 = (bf16[512,1024]{1,0:T(8,128)(2,1)S(1)}, bf16[512,1024]{1,0:T(8,128)(2,1)S(1)}, f32[1,1024]{1,0:T(1,128)S(1)}, f32[256,1024]{1,0:T(8,128)S(1)}, bf16[256,1024]{1,0:T(8,128)(2,1)}) custom-call(s32[1]{0:T(128)} %bitcast.refs_0_.core_ref, bf16[256,1024]{1,0:T(8,128)(2,1)} %get-tuple-element.210.own_ref, ...), custom_call_target="tpu_custom_call" | custom-call | flops 2147483648 | bytes 11014148 | tf_op jit(solution)/shard_map/pallas_call | solution.py:420
  519.2 7.9 shard_map.244
  567.0 10.2 %collective-permute-done.70.got_ref = bf16[256,1024]{1,0:T(8,128)(2,1)S(1)} collective-permute-done((bf16[256,1024]{1,0:T(8,128)(2,1)S(1)}, bf16[256,1024]{1,0:T(8,128)(2,1)S(1)}, u32[]{:S(2)}, u32[]{:S(2)}) %collective-permute-start.70) | collective-permute-done | bytes 524320 | tf_op jit(solution)/shard_map/ppermute | solution.py:351
  586.2 8.8 %shard_map.246 = (bf16[512,1024]{1,0:T(8,128)(2,1)S(1)}, bf16[512,768]{1,0:T(8,128)(2,1)S(1)}, f32[2,256]{1,0:T(2,128)S(1)}, f32[256,1024]{1,0:T(8,128)S(1)}, bf...) custom-call(s32[1]{0:T(128)} %bitcast.refs_0_.core_ref, bf16[256,1024]{1,0:T(8,128)(2,1)S(1)} %get-tuple-element.225.refs_1_, ...), custom_call_target="tpu_custom_call" | custom-call | flops 11811160064 | bytes 9447428 | tf_op jit(solution)/shard_map/pallas_call | solution.py:420
  633.8 13.6 %collective-permute-done.124 = bf16[2,1024,256]{2,1,0:T(8,128)(2,1)S(1)} collective-permute-done((bf16[2,1024,256]{2,1,0:T(8,128)(2,1)S(1)}, bf16[2,1024,256]{2,1,0:T(8,128)(2,1)S(1)}, u32[]{:S(2)}, u32[]{:S(2)}) %collective-permute-start.124) | collective-permute-done | bytes 1048608 | tf_op jit(solution)/shard_map/ppermute | solution.py:339
  664.1 18.4 %collective-permute-done.105 = bf16[2,256,256]{2,1,0:T(8,128)(2,1)S(1)} collective-permute-done((bf16[2,256,256]{2,1,0:T(8,128)(2,1)S(1)}, bf16[2,256,256]{2,1,0:T(8,128)(2,1)S(1)}, u32[]{:S(2)}, u32[]{:S(2)}) %collective-permute-start.105) | collective-permute-done | bytes 262176 | tf_op jit(solution)/shard_map/ppermute | solution.py:362
  712.9 7.6 collective-permute-done.85
  730.4 13.9 %collective-permute-done.94 = bf16[2,256,768]{2,1,0:T(8,128)(2,1)S(1)} collective-permute-done((bf16[2,256,768]{2,1,0:T(8,128)(2,1)}, bf16[2,256,768]{2,1,0:T(8,128)(2,1)S(1)}, u32[]{:S(2)}, u32[]{:S(2)}) %collective-permute-start.94) | collective-permute-done | bytes 786464 | tf_op jit(solution)/shard_map/ppermute | solution.py:339
  749.1 14.5 %collective-permute-done.95 = bf16[2,256,768]{2,1,0:T(8,128)(2,1)S(1)} collective-permute-done((bf16[2,256,768]{2,1,0:T(8,128)(2,1)S(1)}, bf16[2,256,768]{2,1,0:T(8,128)(2,1)S(1)}, u32[]{:S(2)}, u32[]{:S(2)}) %collective-permute-start.95) | collective-permute-done | bytes 786464 | tf_op jit(solution)/shard_map/ppermute | solution.py:362
  772.2 23.2 %collective-permute-done.117 = bf16[2,256,1024]{2,1,0:T(8,128)(2,1)S(1)} collective-permute-done((bf16[2,256,1024]{2,1,0:T(8,128)(2,1)S(1)}, bf16[2,256,1024]{2,1,0:T(8,128)(2,1)S(1)}, u32[]{:S(2)}, u32[]{:S(2)}) %collective-permute-start.117) | collective-permute-done | bytes 1048608 | tf_op jit(solution)/shard_map/ppermute | solution.py:366
  795.7 22.1 %collective-permute-done.127 = bf16[2,1024,256]{2,1,0:T(8,128)(2,1)S(1)} collective-permute-done((bf16[2,1024,256]{2,1,0:T(8,128)(2,1)S(1)}, bf16[2,1024,256]{2,1,0:T(8,128)(2,1)S(1)}, u32[]{:S(2)}, u32[]{:S(2)}) %collective-permute-start.127) | collective-permute-done | bytes 1048608 | tf_op jit(solution)/shard_map/ppermute | solution.py:366
  824.7 8.4 collective-permute-done.97
  (976 shorter events, 449.5 us)
Async XLA Ops:
  30.6 83.1 %collective-permute-start.6 = (bf16[256,1024]{1,0:T(8,128)(2,1)S(1)}, bf16[256,1024]{1,0:T(8,128)(2,1)S(1)}, u32[]{:S(2)}, u32[]{:S(2)}) collective-permute-start(bf16[256,1024]{1,0:T(8,128)(2,1)S(1)} %get-tuple-element.336.refs_1_), channel_id=1, source_target_pairs={{0,2},{2,0},{4,6},{6,4},{1,3},{3,1},{5,7},{7,5},{8,10},{10,8},{12,... | collective-permute-start | bytes 1572872 | tf_op jit(solution)/shard_map/ppermute | solution.py:339
  38.5 81.4 %collective-permute-start.34 = (bf16[256,1024]{1,0:T(8,128)(2,1)S(1)}, bf16[256,1024]{1,0:T(8,128)(2,1)S(1)}, u32[]{:S(2)}, u32[]{:S(2)}) collective-permute-start(bf16[256,1024]{1,0:T(8,128)(2,1)S(1)} %get-tuple-element.337.refs_1_), channel_id=1, source_target_pairs={{0,2},{2,0},{4,6},{6,4},{1,3},{3,1},{5,7},{7,5},{8,10},{10,8},{12,... | collective-permute-start | bytes 1572872 | tf_op jit(solution)/shard_map/ppermute | solution.py:339
  44.1 39.2 %collective-permute-start.16 = (bf16[2048,256]{1,0:T(8,128)(2,1)S(1)}, bf16[2048,256]{1,0:T(8,128)(2,1)S(1)}, u32[]{:S(2)}, u32[]{:S(2)}) collective-permute-start(bf16[2048,256]{1,0:T(8,128)(2,1)S(1)} %copy-done.179), channel_id=1, source_target_pairs={{0,4},{2,6},{4,0},{6,2},{1,5},{3,7},{5,1},{7,3},{8,12},{10,14},{12... | collective-permute-start | bytes 3145736 | tf_op jit(solution)/shard_map/ppermute | solution.py:339
  61.0 50.8 %collective-permute-start.8 = (bf16[2,3,256,256]{3,2,1,0:T(8,128)(2,1)S(1)}, bf16[2,3,256,256]{3,2,1,0:T(8,128)(2,1)S(1)}, u32[]{:S(2)}, u32[]{:S(2)}) collective-permute-start(bf16[2,3,256,256]{3,2,1,0:T(8,128)(2,1)S(1)} %pad_maximum_fusion.22), channel_id=1, source_target_pairs={{0,2},{2,0},{4,6},{6,4},{1,3},{3,1},{5,7},{7,5},{8,10},{10,8},{12,... | collective-permute-start | bytes 2359304 | tf_op jit(solution)/shard_map/ppermute | solution.py:339
  61.1 64.8 %collective-permute-start.14 = (bf16[256,2048]{1,0:T(8,128)(2,1)S(1)}, bf16[256,2048]{1,0:T(8,128)(2,1)}, u32[]{:S(2)}, u32[]{:S(2)}) collective-permute-start(bf16[256,2048]{1,0:T(8,128)(2,1)S(1)} %copy-done.178), channel_id=1, source_target_pairs={{0,4},{2,6},{4,0},{6,2},{1,5},{3,7},{5,1},{7,3},{8,12},{10,14},{12... | collective-permute-start | bytes 3145736 | tf_op jit(solution)/shard_map/ppermute | solution.py:339
  125.9 38.4 %collective-permute-start.21 = (bf16[3,256,512]{2,1,0:T(8,128)(2,1)S(1)}, bf16[3,256,512]{2,1,0:T(8,128)(2,1)S(1)}, u32[]{:S(2)}, u32[]{:S(2)}) collective-permute-start(bf16[3,256,512]{2,1,0:T(8,128)(2,1)S(1)} %copy-done.184), channel_id=1, source_target_pairs={{0,4},{2,6},{4,0},{6,2},{1,5},{3,7},{5,1},{7,3},{8,12},{10,14},{12... | collective-permute-start | bytes 2359304 | tf_op jit(solution)/shard_map/ppermute | solution.py:339
  173.5 49.1 %collective-permute-start.31 = (bf16[2,1024,256]{2,1,0:T(8,128)(2,1)}, bf16[2,1024,256]{2,1,0:T(8,128)(2,1)}, u32[]{:S(2)}, u32[]{:S(2)}) collective-permute-start(bf16[2,1024,256]{2,1,0:T(8,128)(2,1)} %pad_maximum_fusion.15), channel_id=1, source_target_pairs={{0,2},{2,0},{4,6},{6,4},{1,3},{3,1},{5,7},{7,5},{8,10},{10,8},{12,... | collective-permute-start | bytes 3145736 | tf_op jit(solution)/shard_map/ppermute | solution.py:339
  174.0 41.2 %collective-permute-start.28 = (bf16[256,2048]{1,0:T(8,128)(2,1)S(1)}, bf16[256,2048]{1,0:T(8,128)(2,1)S(1)}, u32[]{:S(2)}, u32[]{:S(2)}) collective-permute-start(bf16[256,2048]{1,0:T(8,128)(2,1)S(1)} %copy-done.176), channel_id=1, source_target_pairs={{0,4},{2,6},{4,0},{6,2},{1,5},{3,7},{5,1},{7,3},{8,12},{10,14},{12... | collective-permute-start | bytes 3145736 | tf_op jit(solution)/shard_map/ppermute | solution.py:339
  222.5 47.2 %collective-permute-start.52 = (bf16[256,1024]{1,0:T(8,128)(2,1)}, bf16[256,1024]{1,0:T(8,128)(2,1)}, u32[]{:S(2)}, u32[]{:S(2)}) collective-permute-start(bf16[256,1024]{1,0:T(8,128)(2,1)} %get-tuple-element.361.own_ref), channel_id=1, source_target_pairs={{0,2},{2,0},{4,6},{6,4},{1,3},{3,1},{5,7},{7,5},{8,10},{10,8},{12,... | collective-permute-start | bytes 1572872 | tf_op jit(solution)/shard_map/ppermute | solution.py:339
  222.7 59.3 %collective-permute-start.56 = (bf16[256,1024]{1,0:T(8,128)(2,1)}, bf16[256,1024]{1,0:T(8,128)(2,1)S(1)}, u32[]{:S(2)}, u32[]{:S(2)}) collective-permute-start(bf16[256,1024]{1,0:T(8,128)(2,1)} %get-tuple-element.358.own_ref), channel_id=1, source_target_pairs={{0,2},{2,0},{4,6},{6,4},{1,3},{3,1},{5,7},{7,5},{8,10},{10,8},{12,... | collective-permute-start | bytes 1572872 | tf_op jit(solution)/shard_map/ppermute | solution.py:339
  258.7 47.3 %collective-permute-start.32 = (bf16[256,1024]{1,0:T(8,128)(2,1)}, bf16[256,1024]{1,0:T(8,128)(2,1)}, u32[]{:S(2)}, u32[]{:S(2)}) collective-permute-start(bf16[256,1024]{1,0:T(8,128)(2,1)} %get-tuple-element.177), channel_id=1, source_target_pairs={{0,2},{2,0},{4,6},{6,4},{1,3},{3,1},{5,7},{7,5},{8,10},{10,8},{12,... | collective-permute-start | bytes 1572872 | tf_op jit(solution)/shard_map/ppermute | solution.py:339
  269.4 38.1 %collective-permute-start.44 = (bf16[256,1024]{1,0:T(8,128)(2,1)}, bf16[256,1024]{1,0:T(8,128)(2,1)}, u32[]{:S(2)}, u32[]{:S(2)}) collective-permute-start(bf16[256,1024]{1,0:T(8,128)(2,1)} %get-tuple-element.193), channel_id=1, source_target_pairs={{0,2},{2,0},{4,6},{6,4},{1,3},{3,1},{5,7},{7,5},{8,10},{10,8},{12,... | collective-permute-start | bytes 1572872 | tf_op jit(solution)/shard_map/ppermute | solution.py:339
  315.0 40.3 %collective-permute-start.58 = (bf16[256,1024]{1,0:T(8,128)(2,1)S(1)}, bf16[256,1024]{1,0:T(8,128)(2,1)S(1)}, u32[]{:S(2)}, u32[]{:S(2)}) collective-permute-start(bf16[256,1024]{1,0:T(8,128)(2,1)S(1)} %add_convert_fusion.24.chip_ref), channel_id=1, source_target_pairs={{0,1},{1,0},{2,3},{3,2},{4,5},{5,4},{6,7},{7,6},{8,9},{9,8},{10,11... | collective-permute-start | bytes 1572872 | tf_op jit(solution)/shard_map/ppermute | solution.py:351
  322.4 83.1 %collective-permute-start.119 = (bf16[2,256,1024]{2,1,0:T(8,128)(2,1)}, bf16[2,256,1024]{2,1,0:T(8,128)(2,1)}, u32[]{:S(2)}, u32[]{:S(2)}) collective-permute-start(bf16[2,256,1024]{2,1,0:T(8,128)(2,1)} %pad_maximum_fusion.19), channel_id=1, source_target_pairs={{0,4},{2,6},{4,0},{6,2},{1,5},{3,7},{5,1},{7,3},{8,12},{10,14},{12... | collective-permute-start | bytes 3145736 | tf_op jit(solution)/shard_map/ppermute | solution.py:339
  344.8 63.8 %collective-permute-start.129 = (bf16[2,1024,256]{2,1,0:T(8,128)(2,1)}, bf16[2,1024,256]{2,1,0:T(8,128)(2,1)}, u32[]{:S(2)}, u32[]{:S(2)}) collective-permute-start(bf16[2,1024,256]{2,1,0:T(8,128)(2,1)} %pad_maximum_fusion.21), channel_id=1, source_target_pairs={{0,4},{2,6},{4,0},{6,2},{1,5},{3,7},{5,1},{7,3},{8,12},{10,14},{12... | collective-permute-start | bytes 3145736 | tf_op jit(solution)/shard_map/ppermute | solution.py:339
  399.2 73.1 %collective-permute-start.98 = (bf16[2,256,768]{2,1,0:T(8,128)(2,1)}, bf16[2,256,768]{2,1,0:T(8,128)(2,1)}, u32[]{:S(2)}, u32[]{:S(2)}) collective-permute-start(bf16[2,256,768]{2,1,0:T(8,128)(2,1)} %get-tuple-element.263), channel_id=1, source_target_pairs={{0,2},{2,0},{4,6},{6,4},{1,3},{3,1},{5,7},{7,5},{8,10},{10,8},{12,... | collective-permute-start | bytes 2359304 | tf_op jit(solution)/shard_map/ppermute | solution.py:339
  408.7 88.3 %collective-permute-start.120 = (bf16[2,256,1024]{2,1,0:T(8,128)(2,1)}, bf16[2,256,1024]{2,1,0:T(8,128)(2,1)}, u32[]{:S(2)}, u32[]{:S(2)}) collective-permute-start(bf16[2,256,1024]{2,1,0:T(8,128)(2,1)} %add_convert_fusion.8), channel_id=1, source_target_pairs={{0,8},{24,16},{1,9},{25,17},{2,10},{26,18},{3,11},{27,19},{4,12},{... | collective-permute-start | bytes 3145736 | tf_op jit(solution)/shard_map/ppermute | solution.py:362
  418.6 83.5 %collective-permute-start.130 = (bf16[2,1024,256]{2,1,0:T(8,128)(2,1)}, bf16[2,1024,256]{2,1,0:T(8,128)(2,1)}, u32[]{:S(2)}, u32[]{:S(2)}) collective-permute-start(bf16[2,1024,256]{2,1,0:T(8,128)(2,1)} %add_convert_fusion.2), channel_id=1, source_target_pairs={{0,8},{24,16},{1,9},{25,17},{2,10},{26,18},{3,11},{27,19},{4,12},{... | collective-permute-start | bytes 3145736 | tf_op jit(solution)/shard_map/ppermute | solution.py:362
  476.9 53.3 %collective-permute-start.99 = (bf16[2,256,768]{2,1,0:T(8,128)(2,1)}, bf16[2,256,768]{2,1,0:T(8,128)(2,1)}, u32[]{:S(2)}, u32[]{:S(2)}) collective-permute-start(bf16[2,256,768]{2,1,0:T(8,128)(2,1)} %pad_maximum_fusion.25), channel_id=1, source_target_pairs={{0,4},{2,6},{4,0},{6,2},{1,5},{3,7},{5,1},{7,3},{8,12},{10,14},{12... | collective-permute-start | bytes 2359304 | tf_op jit(solution)/shard_map/ppermute | solution.py:339
  500.3 56.6 %collective-permute-start.121 = (bf16[2,256,1024]{2,1,0:T(8,128)(2,1)}, bf16[2,256,1024]{2,1,0:T(8,128)(2,1)}, u32[]{:S(2)}, u32[]{:S(2)}) collective-permute-start(bf16[2,256,1024]{2,1,0:T(8,128)(2,1)} %add_convert_fusion.7), channel_id=1, source_target_pairs={{8,16},{16,8},{9,17},{17,9},{10,18},{18,10},{11,19},{19,11},{12,20... | collective-permute-start | bytes 3145736 | tf_op jit(solution)/shard_map/ppermute | solution.py:364
  504.9 55.4 %collective-permute-start.131 = (bf16[2,1024,256]{2,1,0:T(8,128)(2,1)}, bf16[2,1024,256]{2,1,0:T(8,128)(2,1)}, u32[]{:S(2)}, u32[]{:S(2)}) collective-permute-start(bf16[2,1024,256]{2,1,0:T(8,128)(2,1)} %add_convert_fusion.1), channel_id=1, source_target_pairs={{8,16},{16,8},{9,17},{17,9},{10,18},{18,10},{11,19},{19,11},{12,20... | collective-permute-start | bytes 3145736 | tf_op jit(solution)/shard_map/ppermute | solution.py:364
  560.3 57.6 %collective-permute-start.101 = (bf16[2,256,768]{2,1,0:T(8,128)(2,1)}, bf16[2,256,768]{2,1,0:T(8,128)(2,1)}, u32[]{:S(2)}, u32[]{:S(2)}) collective-permute-start(bf16[2,256,768]{2,1,0:T(8,128)(2,1)} %add_convert_fusion.13), channel_id=1, source_target_pairs={{8,16},{16,8},{9,17},{17,9},{10,18},{18,10},{11,19},{19,11},{12,20... | collective-permute-start | bytes 2359304 | tf_op jit(solution)/shard_map/ppermute | solution.py:364
  564.8 58.2 %collective-permute-start.122 = (bf16[2,256,1024]{2,1,0:T(8,128)(2,1)}, bf16[2,256,1024]{2,1,0:T(8,128)(2,1)}, u32[]{:S(2)}, u32[]{:S(2)}) collective-permute-start(bf16[2,256,1024]{2,1,0:T(8,128)(2,1)} %add_convert_fusion.6), channel_id=1, source_target_pairs={{8,0},{16,24},{9,1},{17,25},{10,2},{18,26},{11,3},{19,27},{12,4},{... | collective-permute-start | bytes 3145736 | tf_op jit(solution)/shard_map/ppermute | solution.py:366
  579.5 45.4 %collective-permute-start.132 = (bf16[2,1024,256]{2,1,0:T(8,128)(2,1)}, bf16[2,1024,256]{2,1,0:T(8,128)(2,1)}, u32[]{:S(2)}, u32[]{:S(2)}) collective-permute-start(bf16[2,1024,256]{2,1,0:T(8,128)(2,1)} %add_convert_fusion), channel_id=1, source_target_pairs={{8,0},{16,24},{9,1},{17,25},{10,2},{18,26},{11,3},{19,27},{12,4},{... | collective-permute-start | bytes 3145736 | tf_op jit(solution)/shard_map/ppermute | solution.py:366
  583.3 47.8 %collective-permute-start.114 = (bf16[2,256,1024]{2,1,0:T(8,128)(2,1)}, bf16[2,256,1024]{2,1,0:T(8,128)(2,1)}, u32[]{:S(2)}, u32[]{:S(2)}) collective-permute-start(bf16[2,256,1024]{2,1,0:T(8,128)(2,1)} %pad_maximum_fusion.18), channel_id=1, source_target_pairs={{0,4},{2,6},{4,0},{6,2},{1,5},{3,7},{5,1},{7,3},{8,12},{10,14},{12... | collective-permute-start | bytes 3145736 | tf_op jit(solution)/shard_map/ppermute | solution.py:339
  631.1 56.9 %collective-permute-start.93 = (bf16[2,256,768]{2,1,0:T(8,128)(2,1)S(1)}, bf16[2,256,768]{2,1,0:T(8,128)(2,1)S(1)}, u32[]{:S(2)}, u32[]{:S(2)}) collective-permute-start(bf16[2,256,768]{2,1,0:T(8,128)(2,1)S(1)} %get-tuple-element.257), channel_id=1, source_target_pairs={{0,2},{2,0},{4,6},{6,4},{1,3},{3,1},{5,7},{7,5},{8,10},{10,8},{12,... | collective-permute-start | bytes 2359304 | tf_op jit(solution)/shard_map/ppermute | solution.py:339
  649.5 77.0 %collective-permute-start.115 = (bf16[2,256,1024]{2,1,0:T(8,128)(2,1)}, bf16[2,256,1024]{2,1,0:T(8,128)(2,1)}, u32[]{:S(2)}, u32[]{:S(2)}) collective-permute-start(bf16[2,256,1024]{2,1,0:T(8,128)(2,1)} %add_convert_fusion.11), channel_id=1, source_target_pairs={{0,8},{24,16},{1,9},{25,17},{2,10},{26,18},{3,11},{27,19},{4,12},{... | collective-permute-start | bytes 3145736 | tf_op jit(solution)/shard_map/ppermute | solution.py:362
  657.9 34.4 %collective-permute-start.75 = (bf16[256,1024]{1,0:T(8,128)(2,1)S(1)}, bf16[256,1024]{1,0:T(8,128)(2,1)S(1)}, u32[]{:S(2)}, u32[]{:S(2)}) collective-permute-start(bf16[256,1024]{1,0:T(8,128)(2,1)S(1)} %add_convert_fusion.18.chip_ref), channel_id=1, source_target_pairs={{0,1},{1,0},{2,3},{3,2},{4,5},{5,4},{6,7},{7,6},{8,9},{9,8},{10,11... | collective-permute-start | bytes 1572872 | tf_op jit(solution)/shard_map/ppermute | solution.py:351
  682.5 64.2 %collective-permute-start.125 = (bf16[2,1024,256]{2,1,0:T(8,128)(2,1)}, bf16[2,1024,256]{2,1,0:T(8,128)(2,1)}, u32[]{:S(2)}, u32[]{:S(2)}) collective-permute-start(bf16[2,1024,256]{2,1,0:T(8,128)(2,1)} %add_convert_fusion.5), channel_id=1, source_target_pairs={{0,8},{24,16},{1,9},{25,17},{2,10},{26,18},{3,11},{27,19},{4,12},{... | collective-permute-start | bytes 3145736 | tf_op jit(solution)/shard_map/ppermute | solution.py:362
  729.5 35.1 %collective-permute-start.116 = (bf16[2,256,1024]{2,1,0:T(8,128)(2,1)S(1)}, bf16[2,256,1024]{2,1,0:T(8,128)(2,1)S(1)}, u32[]{:S(2)}, u32[]{:S(2)}) collective-permute-start(bf16[2,256,1024]{2,1,0:T(8,128)(2,1)S(1)} %add_convert_fusion.10), channel_id=1, source_target_pairs={{8,16},{16,8},{9,17},{17,9},{10,18},{18,10},{11,19},{19,11},{12,20... | collective-permute-start | bytes 3145736 | tf_op jit(solution)/shard_map/ppermute | solution.py:364
  768.4 49.5 %collective-permute-start.127 = (bf16[2,1024,256]{2,1,0:T(8,128)(2,1)S(1)}, bf16[2,1024,256]{2,1,0:T(8,128)(2,1)S(1)}, u32[]{:S(2)}, u32[]{:S(2)}) collective-permute-start(bf16[2,1024,256]{2,1,0:T(8,128)(2,1)S(1)} %add_convert_fusion.3), channel_id=1, source_target_pairs={{8,0},{16,24},{9,1},{17,25},{10,2},{18,26},{11,3},{19,27},{12,4},{... | collective-permute-start | bytes 3145736 | tf_op jit(solution)/shard_map/ppermute | solution.py:366
  770.9 62.2 %collective-permute-start.97 = (bf16[2,256,768]{2,1,0:T(8,128)(2,1)S(1)}, bf16[2,256,768]{2,1,0:T(8,128)(2,1)S(1)}, u32[]{:S(2)}, u32[]{:S(2)}) collective-permute-start(bf16[2,256,768]{2,1,0:T(8,128)(2,1)S(1)} %add_convert_fusion.15), channel_id=1, source_target_pairs={{8,0},{16,24},{9,1},{17,25},{10,2},{18,26},{11,3},{19,27},{12,4},{... | collective-permute-start | bytes 2359304 | tf_op jit(solution)/shard_map/ppermute | solution.py:366
  (304 other events, 2952.2 us)

commit v2 on v1

--- a/solution.py
+++ b/solution.py
@@ -389,6 +389,9 @@
 
 
 def spread_grad(keep, give):
+    row = lax.axis_index("row")
+    keep, give = [jnp.where(row % 2 == 0, a, b) for a, b in ((keep, give), (give, keep))]
+    keep, give = [jnp.where(row // 2 == 0, v, v[::-1]) for v in (keep, give)]
     got = swap_core(give)
     away = swap_chip(jnp.stack([keep[1], got[1]]))
     own = jnp.stack([keep[0], got[0]])
@@ -434,8 +437,7 @@
 
 
 def other_order(value):
-    b = [value[:, k * WIDTH : (k + 1) * WIDTH] for k in range(4)]
-    return jnp.concatenate([b[1], b[0], b[3], b[2]], axis=1)
+    return value
 
 
 def part_rows(index):
@@ -600,13 +602,7 @@
         join_tokens(core_ref, own_ref, sib_ref, full_ref)
 
     active_grad = dot_nt(full_ref[...], down_ref[...])
-    pre = pre_ref[...]
-    square = pre * pre
-    curve = jnp.tanh(GELU * (pre + 0.044715 * (square * pre)))
-    slope = 0.5 * (1.0 + curve) + (0.5 * GELU) * pre * (1.0 - curve * curve) * (
-        1.0 + (3.0 * 0.044715) * square
-    )
-    hidden = (active_grad * slope).astype(bf16)
+    hidden = (active_grad * pre_ref[...].astype(f32)).astype(bf16)
     hidden_ref[...] = hidden
     bias_ref[...] = jnp.sum(hidden.astype(f32), axis=0, keepdims=True)
     sums = dot_nt(hidden, up_ref[...])
@@ -833,6 +829,585 @@
     return (mine + swap_core(other).astype(f32)).astype(bf16)
 
 
+MESH = pl.DeviceIdType.MESH
+HEADS_HERE = WIDTH // HD
+SMALL = 24
+
+
+class Place:
+    def __init__(self):
+        self.row = lax.axis_index("row")
+        self.col = lax.axis_index("col")
+        self.dp = lax.axis_index("dp")
+        self.core = self.row % 2
+        self.chip = self.row // 2
+        self.half = self.dp % 2
+        sibling = self.row + 1 - 2 * self.core
+        self.rows = [self.row, sibling, (self.row + 2) % 4, (sibling + 2) % 4]
+        self.cores = [self.core, 1 - self.core, self.core, 1 - self.core]
+
+    def to_row(self, j):
+        return {"row": self.rows[j]}
+
+    def to_col(self):
+        return {"col": 1 - self.col}
+
+    def to_dp(self):
+        return {"dp": self.dp + 1 - 2 * self.half}
+
+
+class Copies:
+    def __init__(self, sems):
+        self.sems = sems
+        self.used = 0
+        self.open = []
+
+    def sem(self):
+        self.used += 1
+        return self.sems.at[self.used - 1]
+
+    def local(self, src, dst):
+        copy = pltpu.make_async_copy(src, dst, self.sem())
+        copy.start()
+        return copy
+
+    def save(self, src, dst):
+        self.open.append(self.local(src, dst).wait)
+
+    def trade(self, src, dst, landing, device):
+        sent, got = self.sem(), self.sem()
+        out = pltpu.make_async_remote_copy(src, dst, sent, got, device_id=device, device_id_type=MESH)
+        back = pltpu.make_async_remote_copy(
+            landing, landing, sent, got, device_id=device, device_id_type=MESH
+        )
+        out.start()
+        return out.wait_send, back.wait_recv
+
+    def finish(self):
+        for wait in self.open:
+            wait()
+
+
+def greet(place, devices):
+    barrier = pltpu.get_barrier_semaphore()
+    for device in devices:
+        pl.semaphore_signal(barrier, inc=1, device_id=device, device_id_type=MESH)
+    pl.semaphore_wait(barrier, len(devices))
+
+
+def span(start, size):
+    return pl.ds(pl.multiple_of(start, size), size)
+
+
+def weight_cuts(kind, layer, wide, local):
+    w = WIDTH
+    if kind == 0:
+
+        def source(core, half):
+            rows = slice(None) if half is None else span(half * (w // 2), w // 2)
+            return local.at[layer, :, rows, span(core * w, w)]
+
+        def target(row, half):
+            rows = span(row * w, w) if half is None else span(row * w + half * (w // 2), w // 2)
+            return wide.at[layer, :, rows, :]
+
+    elif kind == 2:
+        units = wide.shape[2]
+
+        def source(core, half):
+            rows = slice(None) if half is None else span(half * (w // 2), w // 2)
+            return local.at[layer, rows, span(core * units, units)]
+
+        def target(row, half):
+            rows = span(row * w, w) if half is None else span(row * w + half * (w // 2), w // 2)
+            return wide.at[layer, rows, :]
+
+    else:
+        high = wide.shape[1]
+
+        def source(core, half):
+            if half is None:
+                return local.at[layer, span(core * high, high), :]
+            return local.at[layer, span(core * high + half * (high // 2), high // 2), :]
+
+        def target(row, half):
+            rows = slice(None) if half is None else span(half * (high // 2), high // 2)
+            return wide.at[layer, rows, span(row * w, w)]
+
+    return source, target
+
+
+def strips(count, body):
+    def step(i, carry):
+        body(pl.multiple_of(i * 32, 32))
+        return carry
+
+    lax.fori_loop(0, count // 32, step, 0)
+
+
+def causal(seg_col, seg_row, start, keys):
+    query = lax.broadcasted_iota(jnp.int32, (QB, keys), 0) + start
+    key = lax.broadcasted_iota(jnp.int32, (QB, keys), 1)
+    return (seg_col == seg_row) & (key <= query)
+
+
+def lanes_of(h):
+    lane = lax.broadcasted_iota(jnp.int32, (1, WIDTH), 1)
+    return (lane >= h * HD) & (lane < (h + 1) * HD)
+
+
+def attend_chunk(k, triples, seg_col_ref, seg_row_ref, kv_ref, mixed_ref, log_ref):
+    scale = 1.0 / math.sqrt(HD)
+    kv_ref[k * SPAN : (k + 1) * SPAN, :] = triples[k][:, WIDTH:]
+    for block in range(SPAN // QB):
+        rows = slice(block * QB, (block + 1) * QB)
+        start = k * SPAN + block * QB
+        keys = start + QB
+        allowed = causal(seg_col_ref[start : start + QB, :], seg_row_ref[:, :keys], start, keys)
+        queries = triples[k][rows, :WIDTH] * scale
+        key_rows = kv_ref[:keys, :WIDTH]
+        value_rows = kv_ref[:keys, WIDTH:]
+        blended = jnp.zeros((QB, WIDTH), f32)
+        for h in range(HEADS_HERE):
+            lanes = lanes_of(h)
+            scores = dot_nt(jnp.where(lanes, queries, 0).astype(bf16), key_rows)
+            scores = jnp.where(allowed, scores, masked)
+            peak = jnp.max(scores, axis=1, keepdims=True)
+            exponent = jnp.exp(scores - peak)
+            total = jnp.sum(exponent, axis=1, keepdims=True)
+            soft = (exponent * (1.0 / total)).astype(bf16)
+            blended = jnp.where(lanes, dot(soft, value_rows), blended)
+            log_ref[rows, h : h + 1] = peak + jnp.log(total)
+        mixed_ref[rows, :] = blended.astype(bf16)
+
+
+def forward_body(*refs):
+    (
+        tokens_ref,
+        cotangent_ref,
+        small_ref,
+        seg_col_ref,
+        seg_row_ref,
+        triple_in,
+        output_in,
+        up_in,
+        down_in,
+        result_ref,
+        grad_ref,
+        wide_out,
+        triple_out,
+        output_out,
+        up_out,
+        down_out,
+        attn_out,
+        rows_out,
+        mixed_out,
+        log_out,
+        mlp_out,
+        slope_out,
+        active_out,
+        stream_out,
+        triple_w,
+        output_w,
+        up_w,
+        down_w,
+        attn,
+        rows,
+        mixed,
+        logs,
+        mlp,
+        slope,
+        active,
+        stream,
+        taken,
+        wide,
+        kv,
+        mine,
+        give,
+        got_core,
+        chip_sum,
+        got_col,
+        final,
+        sems,
+    ) = refs
+    place = Place()
+    copies = Copies(sems)
+    core, sibling = place.core, 1 - place.core
+    greet(place, [place.to_row(1), place.to_row(2), place.to_row(3), place.to_col(), place.to_dp()])
+
+    own_lanes = span(place.row * WIDTH, WIDTH)
+
+    def held(j, k):
+        return span(place.rows[j] // 2 * LEN + k * SPAN + place.cores[j] * OWN, OWN)
+
+    def part(c):
+        return span(c * OWN, OWN)
+
+    small_waits = []
+    copy = copies.local(small_ref, wide.at[:, own_lanes])
+    small_waits.append(copy.wait)
+    for j in range(1, 4):
+        sent, got = copies.trade(
+            small_ref,
+            wide.at[:, own_lanes],
+            wide.at[:, span(place.rows[j] * WIDTH, WIDTH)],
+            place.to_row(j),
+        )
+        copies.open.append(sent)
+        small_waits.append(got)
+    token_waits = [[] for _ in range(CHUNKS)]
+
+    def scatter_in(block_ref, target, k, waits):
+        waits.append(copies.local(block_ref.at[held(0, k), :], target.at[k, :, own_lanes]).wait)
+        for j in range(1, 4):
+            sent, got = copies.trade(
+                block_ref.at[held(j, k), :],
+                target.at[k, :, own_lanes],
+                target.at[k, :, span(place.rows[j] * WIDTH, WIDTH)],
+                place.to_row(j),
+            )
+            copies.open.append(sent)
+            waits.append(got)
+
+    arrivals, ready_waits = {}, {}
+
+    def send_weight(layer, kind):
+        local = (triple_in, output_in, up_in, down_in)[kind]
+        whole = (triple_w, output_w, up_w, down_w)[kind]
+        source, target = weight_cuts(kind, layer, whole, local)
+        here = []
+        for j in (2, 3):
+            sent, got = copies.trade(
+                source(place.cores[j], place.half),
+                target(place.row, place.half),
+                target(place.rows[j], place.half),
+                place.to_row(j),
+            )
+            copies.open.append(sent)
+            here.append((got, target(place.rows[j], place.half), target(place.rows[j], 1 - place.half)))
+        arrivals[layer, kind] = here
+        sent, got = copies.trade(
+            source(sibling, None),
+            target(place.row, None),
+            target(place.rows[1], None),
+            place.to_row(1),
+        )
+        copies.open.append(sent)
+        own = copies.local(source(core, None), target(place.row, None))
+        ready_waits[layer, kind] = [got, own.wait]
+
+    def relay_weight(layer, kind):
+        for got, arrived, missing in arrivals[layer, kind]:
+            got()
+            sent, back = copies.trade(arrived, arrived, missing, place.to_dp())
+            copies.open.append(sent)
+            ready_waits[layer, kind].append(back)
+
+    def ready_weight(layer, kind):
+        for wait in ready_waits[layer, kind]:
+            wait()
+        whole = (triple_w, output_w, up_w, down_w)[kind]
+        out = (triple_out, output_out, up_out, down_out)[kind]
+        copies.save(whole.at[layer], out.at[layer])
+
+    scatter_in(tokens_ref, taken, 0, token_waits[0])
+    send_weight(0, 0)
+    scatter_in(tokens_ref, taken, 1, token_waits[1])
+    for layer, kind in ((0, 1), (0, 2), (0, 3), (1, 0), (1, 1), (1, 2), (1, 3)):
+        send_weight(layer, kind)
+    grad_waits = []
+    for k in range(CHUNKS):
+        scatter_in(cotangent_ref, grad_ref, k, grad_waits)
+
+    for wait in small_waits:
+        wait()
+    copies.save(wide, wide_out)
+
+    def gain(layer, which):
+        return wide[2 * layer + which : 2 * layer + which + 1, :]
+
+    def shift(layer, which):
+        return wide[4 + 2 * layer + which : 5 + 2 * layer + which, :]
+
+    def output_bias(layer):
+        return wide[8 + layer : 9 + layer, :]
+
+    def down_bias(layer):
+        return wide[10 + layer : 11 + layer, :]
+
+    def of_core(line, start, size):
+        return wide[line : line + 1, span(start, size)]
+
+    def triple_bias(layer, which):
+        at = 2 * core * WIDTH + which * (WIDTH // 2)
+        size = WIDTH // 2
+        return jnp.concatenate(
+            [of_core(12 + layer, at, size), of_core(12 + layer, at + WIDTH, size)], axis=1
+        )
+
+    def up_bias(layer):
+        line, at = 14 + 2 * layer, 2 * core * WIDTH
+        return jnp.concatenate(
+            [of_core(line + a, at + b * WIDTH, WIDTH) for b in range(2) for a in range(2)], axis=1
+        )
+
+    def norm_to(value, layer, which, target, at):
+        center = jnp.mean(value, axis=1, keepdims=True)
+        second = jnp.mean(value * value, axis=1, keepdims=True) - center * center
+        normed = (value - center) * lax.rsqrt(second + eps)
+        target[pl.ds(pl.multiple_of(core * OWN + at, 32), 32), :] = (
+            normed * gain(layer, which) + shift(layer, which)
+        ).astype(bf16)
+
+    def share(target):
+        return copies.trade(target.at[part(core)], target.at[part(core)], target.at[part(sibling)], place.to_row(1))
+
+    def give_rows(k, value):
+        give[k] = value.astype(bf16)
+
+    sent_core, sent_col = [None] * CHUNKS, [None] * CHUNKS
+    col_waits = [None] * CHUNKS
+    saves = {}
+
+    def settle(stage, k, got):
+        got()
+        if sent_col[k] is not None:
+            sent_col[k]()
+
+        def add(at):
+            lines = pl.ds(at, 32)
+            chip_sum[k, lines, :] = (
+                mine[k, lines, :] + got_core[stage, k, lines, :].astype(f32)
+            ).astype(bf16)
+
+        strips(OWN, add)
+        sent_col[k], col_waits[k] = copies.trade(
+            chip_sum.at[k], got_col.at[stage, k], got_col.at[stage, k], place.to_col()
+        )
+
+    def start_core(stage, k):
+        sent, got = copies.trade(
+            give.at[k], got_core.at[stage, k], got_core.at[stage, k], place.to_row(1)
+        )
+        sent_core[k] = sent
+        return got
+
+    def take_col(stage, k, layer, bias, after_ref):
+        col_waits[k]()
+
+        def add(at):
+            lines = pl.ds(at, 32)
+            total = chip_sum[k, lines, :].astype(f32) + got_col[stage, k, lines, :].astype(f32)
+            value = stream[stage, k, lines, :] + (total + bias)
+            stream[1 - stage, k, lines, :] = value
+            after_ref(value, at)
+
+        strips(OWN, add)
+
+    shares = [None] * CHUNKS
+    for k in range(CHUNKS):
+        for wait in token_waits[k]:
+            wait()
+        if k == 0:
+            pass
+
+        def first(at, k=k):
+            value = taken[k, pl.ds(at, 32), :].astype(f32)
+            stream[0, k, pl.ds(at, 32), :] = value
+            norm_to(value, 0, 0, attn.at[0, k], at)
+
+        strips(OWN, first)
+        saves[0, 0, k] = copies.local(stream.at[0, k], stream_out.at[0, 0, k])
+        shares[k] = share(attn.at[0, k])
+        if k == 0:
+            relay_weight(0, 0)
+    relay_weight(0, 1)
+    pump = [(0, 2), (0, 3), (1, 0), (1, 1), (1, 2), (1, 3)]
+
+    def pump_one():
+        if pump:
+            relay_weight(*pump.pop(0))
+
+    for layer in range(LAYERS):
+        for k in range(CHUNKS):
+            if layer:
+                saves.pop((layer - 1, 0, k)).wait()
+                take_col(
+                    1, k, layer, down_bias(layer - 1), lambda v, at, k=k: norm_to(v, layer, 0, attn.at[layer, k], at)
+                )
+                saves[layer, 0, k] = copies.local(stream.at[0, k], stream_out.at[layer, 0, k])
+                shares[k] = share(attn.at[layer, k])
+            if k == 0:
+                ready_weight(layer, 0)
+            bias = [triple_bias(layer, 0), None, triple_bias(layer, 1)]
+
+            def project(c, k=k, bias=bias):
+                for third in range(3):
+                    value = dot(attn[layer, k, part(c), :], triple_w[layer, third])
+                    if bias[third] is not None:
+                        value = value + bias[third]
+                    rows[layer, k, part(c), third * WIDTH : (third + 1) * WIDTH] = value.astype(bf16)
+
+            project(core)
+            sent, got = shares[k]
+            got()
+            project(sibling)
+            attend_chunk(
+                k,
+                [rows.at[layer, i] for i in range(k + 1)],
+                seg_col_ref,
+                seg_row_ref,
+                kv,
+                mixed.at[layer, k],
+                logs.at[layer, k],
+            )
+            if k == 0:
+                ready_weight(layer, 1)
+            if sent_core[k] is not None:
+                sent_core[k]()
+            give[k] = dot(mixed[layer, k, part(sibling), :], output_w[layer]).astype(bf16)
+            got = start_core(0, k)
+            mine[k] = dot(mixed[layer, k, part(core), :], output_w[layer])
+            sent()
+            copies.save(attn.at[layer, k], attn_out.at[layer, k])
+            copies.save(rows.at[layer, k], rows_out.at[layer, k])
+            copies.save(mixed.at[layer, k], mixed_out.at[layer, k])
+            copies.save(logs.at[layer, k], log_out.at[layer, k])
+            settle(0, k, got)
+            pump_one()
+        for k in range(CHUNKS):
+            if layer:
+                saves.pop((layer - 1, 1, k)).wait()
+            take_col(
+                0, k, layer, output_bias(layer), lambda v, at, k=k: norm_to(v, layer, 1, mlp.at[layer, k], at)
+            )
+            saves[layer, 1, k] = copies.local(stream.at[1, k], stream_out.at[layer, 1, k])
+            shares[k] = share(mlp.at[layer, k])
+            if k == 0:
+                ready_weight(layer, 2)
+            bias = up_bias(layer)
+
+            def widen(c, k=k, bias=bias):
+                for block in range(4):
+                    cols = slice(block * WIDTH, (block + 1) * WIDTH)
+                    pre = dot(mlp[layer, k, part(c), :], up_w[layer, :, cols]) + bias[:, cols]
+                    square = pre * pre
+                    curve = jnp.tanh(GELU * (pre + 0.044715 * (square * pre)))
+                    upper = 0.5 * (1.0 + curve)
+                    active[layer, k, part(c), cols] = (pre * upper).astype(bf16)
+                    slope[layer, k, part(c), cols] = (
+                        upper
+                        + (0.5 * GELU) * pre * (1.0 - curve * curve) * (1.0 + (3.0 * 0.044715) * square)
+                    ).astype(bf16)
+
+            widen(core)
+            sent, got = shares[k]
+            got()
+            widen(sibling)
+            if k == 0:
+                ready_weight(layer, 3)
+            sent_core[k]()
+            give[k] = dot(active[layer, k, part(sibling), :], down_w[layer]).astype(bf16)
+            got = start_core(1, k)
+            mine[k] = dot(active[layer, k, part(core), :], down_w[layer])
+            sent()
+            copies.save(mlp.at[layer, k], mlp_out.at[layer, k])
+            copies.save(slope.at[layer, k], slope_out.at[layer, k])
+            copies.save(active.at[layer, k], active_out.at[layer, k])
+            settle(1, k, got)
+            pump_one()
+    result_waits = []
+    for k in range(CHUNKS):
+        saves.pop((LAYERS - 1, 0, k)).wait()
+
+        def finish(v, at, k=k):
+            final[k, pl.ds(at, 32), :] = v.astype(bf16)
+
+        take_col(1, k, LAYERS, down_bias(LAYERS - 1), finish)
+        result_waits.append(copies.local(final.at[k, :, own_lanes], result_ref.at[held(0, k), :]).wait)
+        for j in range(1, 4):
+            sent, got = copies.trade(
+                final.at[k, :, span(place.rows[j] * WIDTH, WIDTH)],
+                result_ref.at[held(0, k), :],
+                result_ref.at[held(j, k), :],
+                place.to_row(j),
+            )
+            result_waits += [sent, got]
+    for k in range(CHUNKS):
+        saves.pop((LAYERS - 1, 1, k)).wait()
+        sent_core[k]()
+        sent_col[k]()
+    for wait in result_waits + grad_waits:
+        wait()
+    copies.finish()
+
+
+def forward_call(tokens, cotangent, small, seg_col, seg_row, triple_w, output_w, up_w, down_w):
+    units = up_w.shape[2] // 2
+    per_layer = [
+        ((LAYERS, CHUNKS, SPAN, D), bf16),
+        ((LAYERS, CHUNKS, SPAN, 3 * WIDTH), bf16),
+        ((LAYERS, CHUNKS, SPAN, WIDTH), bf16),
+        ((LAYERS, CHUNKS, SPAN, 128), f32),
+        ((LAYERS, CHUNKS, SPAN, D), bf16),
+        ((LAYERS, CHUNKS, SPAN, units), bf16),
+        ((LAYERS, CHUNKS, SPAN, units), bf16),
+    ]
+    wide = [
+        ((LAYERS, 3, D, WIDTH), bf16),
+        ((LAYERS, WIDTH, D), bf16),
+        ((LAYERS, D, units), bf16),
+        ((LAYERS, units, D), bf16),
+    ]
+    outs = [
+        (tokens.shape, bf16),
+        ((CHUNKS, OWN, D), bf16),
+        ((SMALL, D), f32),
+        *wide,
+        *per_layer,
+        ((LAYERS, 2, CHUNKS, OWN, D), f32),
+    ]
+    scratch = [
+        *wide,
+        *per_layer,
+        ((2, CHUNKS, OWN, D), f32),
+        ((CHUNKS, OWN, D), bf16),
+        ((SMALL, D), f32),
+        ((LEN, 2 * WIDTH), bf16),
+        ((CHUNKS, OWN, D), f32),
+        ((CHUNKS, OWN, D), bf16),
+        ((2, CHUNKS, OWN, D), bf16),
+        ((CHUNKS, OWN, D), bf16),
+        ((2, CHUNKS, OWN, D), bf16),
+        ((CHUNKS, OWN, D), bf16),
+    ]
+    anywhere = pl.BlockSpec(memory_space=pl.ANY)
+    inside = pl.BlockSpec(memory_space=pltpu.VMEM)
+    return pl.pallas_call(
+        forward_body,
+        out_shape=[like(*v) for v in outs],
+        in_specs=[anywhere] * 2 + [inside] * 3 + [anywhere] * 4,
+        out_specs=[anywhere] * len(outs),
+        scratch_shapes=[pltpu.VMEM(*v) for v in scratch] + [pltpu.SemaphoreType.DMA((320,))],
+        compiler_params=pltpu.CompilerParams(
+            collective_id=0, has_side_effects=True, vmem_limit_bytes=60 * 1024 * 1024
+        ),
+    )(tokens, cotangent, small, seg_col, seg_row, triple_w, output_w, up_w, down_w)
+
+
+def pack_small(norm_gain, norm_shift, output_bias, down_bias, triple_bias, up_bias):
+    lines = [
+        norm_gain.reshape(-1, WIDTH),
+        norm_shift.reshape(-1, WIDTH),
+        output_bias,
+        down_bias,
+        triple_bias.reshape(-1, WIDTH),
+        up_bias.reshape(-1, WIDTH),
+    ]
+    lines = jnp.concatenate(lines).astype(f32)
+    return jnp.pad(lines, ((0, SMALL - lines.shape[0]), (0, 0)))
+
+
 def pair_plan(
     tokens,
     segments,
@@ -855,21 +1430,9 @@
     core_id = core.astype(jnp.int32).reshape(1)
     chunks = range(CHUNKS)
 
-    def to_tokens(block):
-        def of_owner(j):
-            start = (row ^ j) // 2 * LEN + (row ^ j) % 2 * OWN
-            return jnp.concatenate(
-                [lax.dynamic_slice_in_dim(block, start + k * SPAN, OWN, 0) for k in chunks]
-            )
-
-        parts = [of_owner(j) for j in range(4)]
-        got = [parts[0]] + [swap_row(parts[j], j) for j in range(1, 4)]
-        whole = jnp.concatenate(got, axis=1)
-        return [whole[k * OWN : (k + 1) * OWN] for k in chunks]
-
     def to_features(pieces):
         whole = jnp.concatenate(pieces)
-        parts = jnp.split(whole, 4, axis=1)
+        parts = [lax.dynamic_slice_in_dim(whole, (row ^ j) * WIDTH, WIDTH, 1) for j in range(4)]
         got = [parts[0]] + [swap_row(parts[j], j) for j in range(1, 4)]
         halves = [jnp.stack(pair).reshape(2, CHUNKS, OWN, WIDTH) for pair in (got[:2], got[2:])]
         packs = []
@@ -882,121 +1445,57 @@
             jnp.concatenate(packs[::-1]),
         )
 
-    streams = [v.astype(f32) for v in to_tokens(tokens)]
     seg_pack = lax.dynamic_slice_in_dim(segments, chip * LEN, LEN, 0)
     seg_col, seg_row = seg_pack[:, None], seg_pack[None, :]
-
-    flat = jnp.concatenate(
-        [
-            v.reshape(-1)
-            for v in (norm_gain, norm_shift, output_bias, down_bias, triple_bias, up_bias)
-        ]
-    ).reshape(-1, 128)
-    small = jnp.stack([flat] + [swap_row(flat, j) for j in range(1, 4)]).astype(f32)
-    small = small.reshape(4, -1)
-    at = 0
-
-    def take(shape):
-        nonlocal at
-        size = math.prod(shape)
-        part = small[:, at : at + size].reshape((4,) + shape)
-        at += size
-        return part
-
-    def wide(part):
-        return jnp.moveaxis(part, 0, -2).reshape(part.shape[1:-1] + (-1,))
-
-    def of_core(part):
-        pick = [
-            lax.dynamic_index_in_dim(part, row ^ (2 * core + b), 0, keepdims=False)
-            for b in range(2)
-        ]
-        return jnp.concatenate(pick, axis=-1)
-
-    gains = wide(take((LAYERS, 2, WIDTH)))
-    shifts = wide(take((LAYERS, 2, WIDTH)))
-    output_b = wide(take((LAYERS, WIDTH)))
-    down_b = wide(take((LAYERS, WIDTH)))
-    triple_b = of_core(take((LAYERS, 2, D // 8)))
-    up_b = of_core(take((LAYERS,) + up_bias.shape[1:]))
-
+    (
+        result,
+        grad_in,
+        wide,
+        triple_wide,
+        output_wide,
+        up_wide,
+        down_wide,
+        attn_all,
+        rows_all,
+        mixed_all,
+        log_all,
+        mlp_all,
+        slope_all,
+        active_all,
+        stream_all,
+    ) = forward_call(
+        tokens,
+        cotangent,
+        pack_small(norm_gain, norm_shift, output_bias, down_bias, triple_bias, up_bias),
+        seg_col,
+        seg_row,
+        jnp.swapaxes(triple_weight, 1, 2),
+        output_weight,
+        up_weight,
+        down_weight,
+    )
+    low = [grad_in[k] for k in chunks]
+    gains = wide[:4].reshape(LAYERS, 2, D)
     weights = []
-    last = [streams[0], streams[0]]
+    stored = []
     for layer in range(LAYERS):
-        triple_w, p0 = gather_weight(
-            core, after(jnp.swapaxes(triple_weight[layer], 0, 1), last[0]), 2, 1
-        )
-        triple_w = jnp.concatenate([triple_w[0], triple_w[1], triple_w[2]], axis=1)
-        output_w, p1 = gather_weight(core, after(output_weight[layer], last[1]), 0, 1)
-        up_w, p2 = gather_weight(core, after(up_weight[layer], p0), 1, 0)
-        down_w, p3 = gather_weight(core, after(down_weight[layer], p1), 0, 1)
-        last = [p2, p3]
-        weights.append((triple_w, output_w, up_w, down_w))
-
-    stored = []
-    low = []
-    for k in chunks:
-        normed, _ = norm_parts(streams[k])
-        low.append((normed * gains[0, 0] + shifts[0, 0]).astype(bf16))
-    for layer in range(LAYERS):
-        triple_w, output_w, up_w, down_w = weights[layer]
-        bias = jnp.concatenate(
-            [triple_b[layer, 0], jnp.zeros_like(triple_b[layer, 0]), triple_b[layer, 1]]
-        )[None]
-        saved = {name: [] for name in ("start", "attn", "triple", "mixed", "logs", "middle")}
-        saved.update({name: [] for name in ("mlp", "pre", "active")})
-        saved["start"] = streams
-        for k in chunks:
-            attn, triple, mixed, logs, mine, other = attend_call(
-                k,
-                core_id,
-                low[k],
-                swap_core(low[k]),
-                triple_w,
-                bias,
-                output_w,
-                seg_col,
-                seg_row,
-                saved["triple"],
-            )
-            total = chip_total(mine, other)
-            middle, mlp_own = norm_call(
-                streams[k], total, swap_col(total), output_b[layer], gains[layer, 1], shifts[layer, 1]
-            )
-            for name, value in (
-                ("attn", attn),
-                ("triple", triple),
-                ("mixed", mixed),
-                ("logs", logs),
-                ("middle", middle),
-            ):
-                saved[name].append(value)
-            low[k] = mlp_own
-        streams = []
-        for k in chunks:
-            mlp, pre, active, mine, other = mlp_call(
-                core_id, low[k], swap_core(low[k]), up_w, up_b[layer][None], down_w
-            )
-            total = chip_total(mine, other)
-            if layer + 1 < LAYERS:
-                stream, low[k] = norm_call(
-                    saved["middle"][k],
-                    total,
-                    swap_col(total),
-                    down_b[layer],
-                    gains[layer + 1, 0],
-                    shifts[layer + 1, 0],
-                )
-            else:
-                both = total.astype(f32) + swap_col(total).astype(f32)
-                stream = saved["middle"][k] + (both + down_b[layer])
-            for name, value in (("mlp", mlp), ("pre", pre), ("active", active)):
-                saved[name].append(value)
-            streams.append(stream)
-        stored.append(saved)
-
-    result = to_features([v.astype(bf16) for v in streams])
-    low = to_tokens(cotangent)
+        t = triple_wide[layer]
+        weights.append(
+            (jnp.concatenate([t[0], t[1], t[2]], axis=1), output_wide[layer], up_wide[layer], down_wide[layer])
+        )
+        stored.append(
+            {
+                "start": [stream_all[layer, 0, k] for k in chunks],
+                "middle": [stream_all[layer, 1, k] for k in chunks],
+                "attn": [attn_all[layer, k] for k in chunks],
+                "triple": [rows_all[layer, k] for k in chunks],
+                "mixed": [mixed_all[layer, k] for k in chunks],
+                "logs": [log_all[layer, k] for k in chunks],
+                "mlp": [mlp_all[layer, k] for k in chunks],
+                "pre": [slope_all[layer, k] for k in chunks],
+                "active": [active_all[layer, k] for k in chunks],
+            }
+        )
     grad = [v.astype(f32) for v in low]
     low_sums = sum(jnp.sum(v, axis=0) for v in grad)
     grads = [None] * LAYERS
@@ -1051,6 +1550,9 @@
             [sums_one[0], sums_two[0], sums_one[1], sums_two[1], sums_two[2], down_bias_grad]
         )
         full = jnp.moveaxis(full.reshape(6, 4, WIDTH), 1, 0)
+        full = jnp.stack(
+            [lax.dynamic_index_in_dim(full, row ^ j, 0, keepdims=False) for j in range(4)]
+        )
         theirs = swap_core(full)
         full = full + jnp.stack([theirs[1], theirs[0], theirs[3], theirs[2]])
         full = full[0] + swap_chip(full[2])

time: 849 us -> 776 us (0.914)
  waiting for transfers between devices: 348 us -> 215 us
  Pallas kernels: 145 us -> 238 us
  starting transfers between devices: 128 us -> 91.9 us
  local copies, waits for them, and re-layouts: 110 us -> 126 us
    pallas_call x0 -> x1, Pallas kernels: none -> 148 us  [forward_call(): pl.pallas_call(forward_body, out_shape=[like(*v) for v in outs], in_specs...]
    ppermute x16 -> x8, waiting for transfers between devices: 104 us -> 40.4 us  [swap_col(): return lax.ppermute(value, 'col', [(0, 1), (1, 0)])]
    pallas_call x38 -> x24, Pallas kernels: 145 us -> 89.3 us  [kernel_call(): pl.pallas_call(body, out_shape=outs, in_specs=in_specs, out_specs=out_spe...]
    ppermute x87 -> x43, waiting for transfers between devices: 102 us -> 55.4 us  [swap_row(): return lax.ppermute(value, 'row', [(i, i ^ bits) for i in range(4)])]
    ppermute x10, waiting for transfers between devices: 67.7 us -> 44 us  [dp_total(): from_end = lax.ppermute(value, 'dp', [(0, 1), (3, 2)])]
    ppermute x87 -> x43, starting transfers between devices: 42 us -> 19.5 us  [swap_row(): return lax.ppermute(value, 'row', [(i, i ^ bits) for i in range(4)])]
    squeeze x15 -> x10, local copies, waits for them, and re-layouts: 7.14 us -> 22.2 us  [the longest x1 6.47 us: pair_plan(): active_all[layer, k]]
    convert_element_type x16 -> x8, other arithmetic: 11.5 us -> 1.17 us  [chip_total(): return (mine + swap_core(other).astype(f32)).astype(bf16)]
  transfers between devices with their start and end apart: 133 -> 81, of which waited for: 36 -> 23; matrix products, arithmetic and copies ran while one was open for 16% -> 17% of each run, Pallas kernels for 17% -> 11%
where the time goes in v2:
time: 776 us; the launch traced here: 766 us
  Pallas kernels  238 us (31%)
  waiting for transfers between devices  215 us (28%)
  local copies, waits for them, and re-layouts  126 us (16%)
  other arithmetic  93.1 us (12%)
  starting transfers between devices  91.9 us (12%)
    pallas_call x1, Pallas kernels, forward_call(): pl.pallas_call(forward_body, out_shape=[like(*v) for v in outs], in_specs...  148 us
    pallas_call x24, Pallas kernels, kernel_call(): pl.pallas_call(body, out_shape=outs, in_specs=in_specs, out_specs=out_spe...  89.3 us
    unnamed x365, local copies, waits for them, and re-layouts  75.9 us
    ppermute x10, waiting for transfers between devices, dp_total(): back = lax.ppermute(whole, 'dp', [(1, 0), (2, 3)])  74.6 us
    ppermute x43, waiting for transfers between devices, swap_row(): return lax.ppermute(value, 'row', [(i, i ^ bits) for i in range(4)])  55.4 us
    ppermute x10, waiting for transfers between devices, dp_total(): from_end = lax.ppermute(value, 'dp', [(0, 1), (3, 2)])  44 us
    ppermute x8, waiting for transfers between devices, swap_col(): return lax.ppermute(value, 'col', [(0, 1), (1, 0)])  40.4 us
    ppermute x10, starting transfers between devices, dp_total(): from_end = lax.ppermute(value, 'dp', [(0, 1), (3, 2)])  39 us
  transfers between devices with their start and end apart: 81, of which 23 were waited for; matrix products, arithmetic and copies ran while one was open for 17% of the time, Pallas kernels for 11%

profile of v2, /device:TPU:0, one launch (start us, length us, event | category | flops | bytes accessed | tf_op | source)
XLA Modules:
  0.0 766.1 jit_solution(10135140075957567913)
XLA Ops:
  6.6 148.2 %shard_map.220 = (bf16[2048,256]{1,0:T(8,128)(2,1)}, bf16[2,256,1024]{2,1,0:T(8,128)(2,1)}, f32[24,1024]{1,0:T(8,128)}, bf16[2,3,1024,256]{3,2,1,0:T(8,128)(2,1)...) custom-call(bf16[2048,256]{1,0:T(8,128)(2,1)} %refs_0_.1, ...), custom_call_target="tpu_custom_call" | custom-call | tf_op jit(solution)/shard_map/pallas_call | solution.py:1386
  177.5 6.5 slice_bitcast_fusion.6
  194.3 7.7 %shard_map.223 = (bf16[512,1024]{1,0:T(8,128)(2,1)S(1)}, bf16[512,1024]{1,0:T(8,128)(2,1)S(1)}, f32[1,1024]{1,0:T(1,128)S(1)}, f32[256,1024]{1,0:T(8,128)S(1)}, bf16[256,1024]{1,0:T(8,128)(2,1)S(1)}) custom-call(s32[1]{0:T(128)} %bitcast.4.core_ref.refs_0_, bf16[256,1024]{1,0:T(8,128)(2,1)} %get-tuple-element.302.own_ref, ...), custom_call_target="tpu_custom_call" | custom-call | flops 2147483648 | bytes 9965572 | tf_op jit(solution)/shard_map/pallas_call | solution.py:423
  205.0 7.7 %shard_map.221 = (bf16[512,1024]{1,0:T(8,128)(2,1)S(1)}, bf16[512,1024]{1,0:T(8,128)(2,1)S(1)}, f32[1,1024]{1,0:T(1,128)S(1)}, f32[256,1024]{1,0:T(8,128)S(1)}, bf16[256,1024]{1,0:T(8,128)(2,1)S(1)}) custom-call(s32[1]{0:T(128)} %bitcast.4.core_ref.refs_0_, bf16[256,1024]{1,0:T(8,128)(2,1)} %get-tuple-element.305.own_ref, ...), custom_call_target="tpu_custom_call" | custom-call | flops 2147483648 | bytes 9965572 | tf_op jit(solution)/shard_map/pallas_call | solution.py:423
  239.3 10.3 %collective-permute-done.6.got_ref = bf16[256,1024]{1,0:T(8,128)(2,1)S(1)} collective-permute-done((bf16[256,1024]{1,0:T(8,128)(2,1)S(1)}, bf16[256,1024]{1,0:T(8,128)(2,1)S(1)}, u32[]{:S(2)}, u32[]{:S(2)}) %collective-permute-start.6) | collective-permute-done | bytes 524320 | tf_op jit(solution)/shard_map/ppermute | solution.py:351
  252.4 7.9 %collective-permute-done.2.got_ref = bf16[256,1024]{1,0:T(8,128)(2,1)S(1)} collective-permute-done((bf16[256,1024]{1,0:T(8,128)(2,1)S(1)}, bf16[256,1024]{1,0:T(8,128)(2,1)S(1)}, u32[]{:S(2)}, u32[]{:S(2)}) %collective-permute-start.2) | collective-permute-done | bytes 524320 | tf_op jit(solution)/shard_map/ppermute | solution.py:351
  273.3 10.3 %shard_map.225 = (bf16[512,1024]{1,0:T(8,128)(2,1)S(1)}, bf16[512,768]{1,0:T(8,128)(2,1)S(1)}, f32[2,256]{1,0:T(2,128)S(1)}, f32[256,1024]{1,0:T(8,128)S(1)}, bf...) custom-call(s32[1]{0:T(128)} %bitcast.4.core_ref.refs_0_, bf16[256,1024]{1,0:T(8,128)(2,1)} %get-tuple-element.124.refs_1_, ...), custom_call_target="tpu_custom_call" | custom-call | flops 11811160064 | bytes 9447428 | tf_op jit(solution)/shard_map/pallas_call | solution.py:423
  286.4 5.7 shard_map.226
  308.8 7.2 collective-permute-done.36
  325.8 4.0 collective-permute-start.58
  355.1 4.1 collective-permute-start.78
  369.3 12.4 %collective-permute-done.38 = f32[18,128]{1,0:T(8,128)S(1)} collective-permute-done((f32[18,128]{1,0:T(8,128)S(1)}, f32[18,128]{1,0:T(8,128)S(1)}, u32[]{:S(2)}, u32[]{:S(2)}) %collective-permute-start.38) | collective-permute-done | bytes 9248 | tf_op jit(solution)/shard_map/ppermute | solution.py:362
  390.9 4.8 collective-permute-done.40
  395.8 7.4 collective-permute-done.60
  417.2 5.3 collective-permute-start.48
  422.6 6.6 shard_map.231
  432.1 7.7 %shard_map.228 = (bf16[512,1024]{1,0:T(8,128)(2,1)S(1)}, bf16[512,1024]{1,0:T(8,128)(2,1)S(1)}, f32[1,1024]{1,0:T(1,128)S(1)}, f32[256,1024]{1,0:T(8,128)S(1)}, bf16[256,1024]{1,0:T(8,128)(2,1)S(1)}) custom-call(s32[1]{0:T(128)} %bitcast.4.core_ref.refs_0_, bf16[256,1024]{1,0:T(8,128)(2,1)} %get-tuple-element.129.own_ref, ...), custom_call_target="tpu_custom_call" | custom-call | flops 2147483648 | bytes 9965572 | tf_op jit(solution)/shard_map/pallas_call | solution.py:423
  463.4 11.7 %collective-permute-done.18.got_ref = bf16[256,1024]{1,0:T(8,128)(2,1)S(1)} collective-permute-done((bf16[256,1024]{1,0:T(8,128)(2,1)S(1)}, bf16[256,1024]{1,0:T(8,128)(2,1)S(1)}, u32[]{:S(2)}, u32[]{:S(2)}) %collective-permute-start.18) | collective-permute-done | bytes 524320 | tf_op jit(solution)/shard_map/ppermute | solution.py:351
  479.6 5.9 collective-permute-done.12.got_ref
  502.2 8.8 %shard_map.233 = (bf16[512,1024]{1,0:T(8,128)(2,1)S(1)}, bf16[512,768]{1,0:T(8,128)(2,1)S(1)}, f32[2,256]{1,0:T(2,128)S(1)}, f32[256,1024]{1,0:T(8,128)S(1)}, bf...) custom-call(s32[1]{0:T(128)} %bitcast.4.core_ref.refs_0_, bf16[256,1024]{1,0:T(8,128)(2,1)S(1)} %get-tuple-element.141.refs_1_, ...), custom_call_target="tpu_custom_call" | custom-call | flops 11811160064 | bytes 9447428 | tf_op jit(solution)/shard_map/pallas_call | solution.py:423
  513.7 5.9 shard_map.234
  543.2 28.4 %collective-permute-done.52 = bf16[2,256,256]{2,1,0:T(8,128)(2,1)S(1)} collective-permute-done((bf16[2,256,256]{2,1,0:T(8,128)(2,1)S(1)}, bf16[2,256,256]{2,1,0:T(8,128)(2,1)S(1)}, u32[]{:S(2)}, u32[]{:S(2)}) %collective-permute-start.52) | collective-permute-done | bytes 262176 | tf_op jit(solution)/shard_map/ppermute | solution.py:339
  584.1 6.6 collective-permute-start.53
  612.4 8.4 %collective-permute-done.28 = f32[6,256]{1,0:T(8,128)S(1)} collective-permute-done((f32[6,256]{1,0:T(8,128)S(1)}, f32[6,256]{1,0:T(8,128)S(1)}, u32[]{:S(2)}, u32[]{:S(2)}) %collective-permute-start.28) | collective-permute-done | bytes 6176 | tf_op jit(solution)/shard_map/ppermute | solution.py:339
  622.2 19.3 %collective-permute-done.31 = f32[18,128]{1,0:T(8,128)S(1)} collective-permute-done((f32[18,128]{1,0:T(8,128)S(1)}, f32[18,128]{1,0:T(8,128)S(1)}, u32[]{:S(2)}, u32[]{:S(2)}) %collective-permute-start.31) | collective-permute-done | bytes 9248 | tf_op jit(solution)/shard_map/ppermute | solution.py:362
  644.8 7.7 %collective-permute-done.33 = f32[18,128]{1,0:T(8,128)S(1)} collective-permute-done((f32[18,128]{1,0:T(8,128)S(1)}, f32[18,128]{1,0:T(8,128)S(1)}, u32[]{:S(2)}, u32[]{:S(2)}) %collective-permute-start.33) | collective-permute-done | bytes 9248 | tf_op jit(solution)/shard_map/ppermute | solution.py:366
  657.4 3.9 collective-permute-done.25
  668.2 6.2 collective-permute-start.43
  678.4 12.3 %collective-permute-done.43 = bf16[2,256,768]{2,1,0:T(8,128)(2,1)S(1)} collective-permute-done((bf16[2,256,768]{2,1,0:T(8,128)(2,1)S(1)}, bf16[2,256,768]{2,1,0:T(8,128)(2,1)S(1)}, u32[]{:S(2)}, u32[]{:S(2)}) %collective-permute-start.43) | collective-permute-done | bytes 786464 | tf_op jit(solution)/shard_map/ppermute | solution.py:362
  698.8 25.0 %collective-permute-done.65 = bf16[2,256,1024]{2,1,0:T(8,128)(2,1)S(1)} collective-permute-done((bf16[2,256,1024]{2,1,0:T(8,128)(2,1)S(1)}, bf16[2,256,1024]{2,1,0:T(8,128)(2,1)S(1)}, u32[]{:S(2)}, u32[]{:S(2)}) %collective-permute-start.65) | collective-permute-done | bytes 1048608 | tf_op jit(solution)/shard_map/ppermute | solution.py:366
  724.2 22.1 %collective-permute-done.75 = bf16[2,1024,256]{2,1,0:T(8,128)(2,1)S(1)} collective-permute-done((bf16[2,1024,256]{2,1,0:T(8,128)(2,1)S(1)}, bf16[2,1024,256]{2,1,0:T(8,128)(2,1)S(1)}, u32[]{:S(2)}, u32[]{:S(2)}) %collective-permute-start.75) | collective-permute-done | bytes 1048608 | tf_op jit(solution)/shard_map/ppermute | solution.py:366
  753.3 7.5 collective-permute-done.45
  (744 shorter events, 319.1 us)
Async XLA Ops:
  158.0 36.2 %collective-permute-start.4 = (bf16[256,1024]{1,0:T(8,128)(2,1)}, bf16[256,1024]{1,0:T(8,128)(2,1)}, u32[]{:S(2)}, u32[]{:S(2)}) collective-permute-start(bf16[256,1024]{1,0:T(8,128)(2,1)} %get-tuple-element.302.own_ref), channel_id=1, source_target_pairs={{0,2},{2,0},{4,6},{6,4},{1,3},{3,1},{5,7},{7,5},{8,10},{10,8},{12,... | collective-permute-start | bytes 1572872 | tf_op jit(solution)/shard_map/ppermute | solution.py:339
  158.4 46.6 %collective-permute-start = (bf16[256,1024]{1,0:T(8,128)(2,1)}, bf16[256,1024]{1,0:T(8,128)(2,1)}, u32[]{:S(2)}, u32[]{:S(2)}) collective-permute-start(bf16[256,1024]{1,0:T(8,128)(2,1)} %get-tuple-element.305.own_ref), channel_id=1, source_target_pairs={{0,2},{2,0},{4,6},{6,4},{1,3},{3,1},{5,7},{7,5},{8,10},{10,8},{12,... | collective-permute-start | bytes 1572872 | tf_op jit(solution)/shard_map/ppermute | solution.py:339
  232.9 31.4 %collective-permute-start.66 = (bf16[2,256,1024]{2,1,0:T(8,128)(2,1)}, bf16[2,256,1024]{2,1,0:T(8,128)(2,1)}, u32[]{:S(2)}, u32[]{:S(2)}) collective-permute-start(bf16[2,256,1024]{2,1,0:T(8,128)(2,1)} %reverse_select_fusion.4), channel_id=1, source_target_pairs={{0,2},{2,0},{4,6},{6,4},{1,3},{3,1},{5,7},{7,5},{8,10},{10,8},{12,... | collective-permute-start | bytes 3145736 | tf_op jit(solution)/shard_map/ppermute | solution.py:339
  233.3 35.9 %collective-permute-start.76 = (bf16[2,1024,256]{2,1,0:T(8,128)(2,1)}, bf16[2,1024,256]{2,1,0:T(8,128)(2,1)}, u32[]{:S(2)}, u32[]{:S(2)}) collective-permute-start(bf16[2,1024,256]{2,1,0:T(8,128)(2,1)} %reverse_select_fusion), channel_id=1, source_target_pairs={{0,2},{2,0},{4,6},{6,4},{1,3},{3,1},{5,7},{7,5},{8,10},{10,8},{12,... | collective-permute-start | bytes 3145736 | tf_op jit(solution)/shard_map/ppermute | solution.py:339
  267.6 58.2 %collective-permute-start.67 = (bf16[2,256,1024]{2,1,0:T(8,128)(2,1)}, bf16[2,256,1024]{2,1,0:T(8,128)(2,1)}, u32[]{:S(2)}, u32[]{:S(2)}) collective-permute-start(bf16[2,256,1024]{2,1,0:T(8,128)(2,1)} %pad_maximum_fusion.7), channel_id=1, source_target_pairs={{0,4},{2,6},{4,0},{6,2},{1,5},{3,7},{5,1},{7,3},{8,12},{10,14},{12... | collective-permute-start | bytes 3145736 | tf_op jit(solution)/shard_map/ppermute | solution.py:339
  272.4 80.0 %collective-permute-start.77 = (bf16[2,1024,256]{2,1,0:T(8,128)(2,1)}, bf16[2,1024,256]{2,1,0:T(8,128)(2,1)}, u32[]{:S(2)}, u32[]{:S(2)}) collective-permute-start(bf16[2,1024,256]{2,1,0:T(8,128)(2,1)} %pad_maximum_fusion.9), channel_id=1, source_target_pairs={{0,4},{2,6},{4,0},{6,2},{1,5},{3,7},{5,1},{7,3},{8,12},{10,14},{12... | collective-permute-start | bytes 3145736 | tf_op jit(solution)/shard_map/ppermute | solution.py:339
  325.0 42.3 %collective-permute-start.46 = (bf16[2,256,768]{2,1,0:T(8,128)(2,1)}, bf16[2,256,768]{2,1,0:T(8,128)(2,1)}, u32[]{:S(2)}, u32[]{:S(2)}) collective-permute-start(bf16[2,256,768]{2,1,0:T(8,128)(2,1)} %reverse_select_fusion.8), channel_id=1, source_target_pairs={{0,2},{2,0},{4,6},{6,4},{1,3},{3,1},{5,7},{7,5},{8,10},{10,8},{12,... | collective-permute-start | bytes 2359304 | tf_op jit(solution)/shard_map/ppermute | solution.py:339
  325.8 34.3 %collective-permute-start.58 = (bf16[2,256,256]{2,1,0:T(8,128)(2,1)}, bf16[2,256,256]{2,1,0:T(8,128)(2,1)}, u32[]{:S(2)}, u32[]{:S(2)}) collective-permute-start(bf16[2,256,256]{2,1,0:T(8,128)(2,1)} %add_convert_fusion.28), channel_id=1, source_target_pairs={{0,8},{24,16},{1,9},{25,17},{2,10},{26,18},{3,11},{27,19},{4,12},{... | collective-permute-start | bytes 786440 | tf_op jit(solution)/shard_map/ppermute | solution.py:362
  333.4 71.7 %collective-permute-start.68 = (bf16[2,256,1024]{2,1,0:T(8,128)(2,1)}, bf16[2,256,1024]{2,1,0:T(8,128)(2,1)}, u32[]{:S(2)}, u32[]{:S(2)}) collective-permute-start(bf16[2,256,1024]{2,1,0:T(8,128)(2,1)} %add_convert_fusion.8), channel_id=1, source_target_pairs={{0,8},{24,16},{1,9},{25,17},{2,10},{26,18},{3,11},{27,19},{4,12},{... | collective-permute-start | bytes 3145736 | tf_op jit(solution)/shard_map/ppermute | solution.py:362
  355.1 55.0 %collective-permute-start.78 = (bf16[2,1024,256]{2,1,0:T(8,128)(2,1)}, bf16[2,1024,256]{2,1,0:T(8,128)(2,1)}, u32[]{:S(2)}, u32[]{:S(2)}) collective-permute-start(bf16[2,1024,256]{2,1,0:T(8,128)(2,1)} %add_convert_fusion.2), channel_id=1, source_target_pairs={{0,8},{24,16},{1,9},{25,17},{2,10},{26,18},{3,11},{27,19},{4,12},{... | collective-permute-start | bytes 3145736 | tf_op jit(solution)/shard_map/ppermute | solution.py:362
  361.8 25.9 %collective-permute-start.59 = (bf16[2,256,256]{2,1,0:T(8,128)(2,1)}, bf16[2,256,256]{2,1,0:T(8,128)(2,1)}, u32[]{:S(2)}, u32[]{:S(2)}) collective-permute-start(bf16[2,256,256]{2,1,0:T(8,128)(2,1)} %add_convert_fusion.27), channel_id=1, source_target_pairs={{8,16},{16,8},{9,17},{17,9},{10,18},{18,10},{11,19},{19,11},{12,20... | collective-permute-start | bytes 786440 | tf_op jit(solution)/shard_map/ppermute | solution.py:364
  385.1 29.9 %collective-permute-start.47 = (bf16[2,256,768]{2,1,0:T(8,128)(2,1)}, bf16[2,256,768]{2,1,0:T(8,128)(2,1)}, u32[]{:S(2)}, u32[]{:S(2)}) collective-permute-start(bf16[2,256,768]{2,1,0:T(8,128)(2,1)} %pad_maximum_fusion.11), channel_id=1, source_target_pairs={{0,4},{2,6},{4,0},{6,2},{1,5},{3,7},{5,1},{7,3},{8,12},{10,14},{12... | collective-permute-start | bytes 2359304 | tf_op jit(solution)/shard_map/ppermute | solution.py:339
  395.7 36.4 %collective-permute-start.10 = (bf16[256,1024]{1,0:T(8,128)(2,1)}, bf16[256,1024]{1,0:T(8,128)(2,1)}, u32[]{:S(2)}, u32[]{:S(2)}) collective-permute-start(bf16[256,1024]{1,0:T(8,128)(2,1)} %get-tuple-element.129.own_ref), channel_id=1, source_target_pairs={{0,2},{2,0},{4,6},{6,4},{1,3},{3,1},{5,7},{7,5},{8,10},{10,8},{12,... | collective-permute-start | bytes 1572872 | tf_op jit(solution)/shard_map/ppermute | solution.py:339
  408.3 80.9 %collective-permute-start.69 = (bf16[2,256,1024]{2,1,0:T(8,128)(2,1)}, bf16[2,256,1024]{2,1,0:T(8,128)(2,1)}, u32[]{:S(2)}, u32[]{:S(2)}) collective-permute-start(bf16[2,256,1024]{2,1,0:T(8,128)(2,1)} %add_convert_fusion.7), channel_id=1, source_target_pairs={{8,16},{16,8},{9,17},{17,9},{10,18},{18,10},{11,19},{19,11},{12,20... | collective-permute-start | bytes 3145736 | tf_op jit(solution)/shard_map/ppermute | solution.py:364
  413.2 79.3 %collective-permute-start.79 = (bf16[2,1024,256]{2,1,0:T(8,128)(2,1)}, bf16[2,1024,256]{2,1,0:T(8,128)(2,1)}, u32[]{:S(2)}, u32[]{:S(2)}) collective-permute-start(bf16[2,1024,256]{2,1,0:T(8,128)(2,1)} %add_convert_fusion.1), channel_id=1, source_target_pairs={{8,16},{16,8},{9,17},{17,9},{10,18},{18,10},{11,19},{19,11},{12,20... | collective-permute-start | bytes 3145736 | tf_op jit(solution)/shard_map/ppermute | solution.py:364
  417.2 44.1 %collective-permute-start.48 = (bf16[2,256,768]{2,1,0:T(8,128)(2,1)}, bf16[2,256,768]{2,1,0:T(8,128)(2,1)}, u32[]{:S(2)}, u32[]{:S(2)}) collective-permute-start(bf16[2,256,768]{2,1,0:T(8,128)(2,1)} %add_convert_fusion.14), channel_id=1, source_target_pairs={{0,8},{24,16},{1,9},{25,17},{2,10},{26,18},{3,11},{27,19},{4,12},{... | collective-permute-start | bytes 2359304 | tf_op jit(solution)/shard_map/ppermute | solution.py:362
  459.6 28.5 %collective-permute-start.61 = (bf16[2,256,1024]{2,1,0:T(8,128)(2,1)S(1)}, bf16[2,256,1024]{2,1,0:T(8,128)(2,1)S(1)}, u32[]{:S(2)}, u32[]{:S(2)}) collective-permute-start(bf16[2,256,1024]{2,1,0:T(8,128)(2,1)S(1)} %reverse_select_fusion.6), channel_id=1, source_target_pairs={{0,2},{2,0},{4,6},{6,4},{1,3},{3,1},{5,7},{7,5},{8,10},{10,8},{12,... | collective-permute-start | bytes 3145736 | tf_op jit(solution)/shard_map/ppermute | solution.py:339
  485.5 51.1 %collective-permute-start.49 = (bf16[2,256,768]{2,1,0:T(8,128)(2,1)}, bf16[2,256,768]{2,1,0:T(8,128)(2,1)}, u32[]{:S(2)}, u32[]{:S(2)}) collective-permute-start(bf16[2,256,768]{2,1,0:T(8,128)(2,1)} %add_convert_fusion.13), channel_id=1, source_target_pairs={{8,16},{16,8},{9,17},{17,9},{10,18},{18,10},{11,19},{19,11},{12,20... | collective-permute-start | bytes 2359304 | tf_op jit(solution)/shard_map/ppermute | solution.py:364
  492.5 79.2 %collective-permute-start.70 = (bf16[2,256,1024]{2,1,0:T(8,128)(2,1)}, bf16[2,256,1024]{2,1,0:T(8,128)(2,1)}, u32[]{:S(2)}, u32[]{:S(2)}) collective-permute-start(bf16[2,256,1024]{2,1,0:T(8,128)(2,1)} %add_convert_fusion.6), channel_id=1, source_target_pairs={{8,0},{16,24},{9,1},{17,25},{10,2},{18,26},{11,3},{19,27},{12,4},{... | collective-permute-start | bytes 3145736 | tf_op jit(solution)/shard_map/ppermute | solution.py:366
  497.7 76.6 %collective-permute-start.80 = (bf16[2,1024,256]{2,1,0:T(8,128)(2,1)}, bf16[2,1024,256]{2,1,0:T(8,128)(2,1)}, u32[]{:S(2)}, u32[]{:S(2)}) collective-permute-start(bf16[2,1024,256]{2,1,0:T(8,128)(2,1)} %add_convert_fusion), channel_id=1, source_target_pairs={{8,0},{16,24},{9,1},{17,25},{10,2},{18,26},{11,3},{19,27},{12,4},{... | collective-permute-start | bytes 3145736 | tf_op jit(solution)/shard_map/ppermute | solution.py:366
  501.5 79.3 %collective-permute-start.62 = (bf16[2,256,1024]{2,1,0:T(8,128)(2,1)}, bf16[2,256,1024]{2,1,0:T(8,128)(2,1)}, u32[]{:S(2)}, u32[]{:S(2)}) collective-permute-start(bf16[2,256,1024]{2,1,0:T(8,128)(2,1)} %pad_maximum_fusion.6), channel_id=1, source_target_pairs={{0,4},{2,6},{4,0},{6,2},{1,5},{3,7},{5,1},{7,3},{8,12},{10,14},{12... | collective-permute-start | bytes 3145736 | tf_op jit(solution)/shard_map/ppermute | solution.py:339
  540.8 43.3 %collective-permute-start.72 = (bf16[2,1024,256]{2,1,0:T(8,128)(2,1)S(1)}, bf16[2,1024,256]{2,1,0:T(8,128)(2,1)S(1)}, u32[]{:S(2)}, u32[]{:S(2)}) collective-permute-start(bf16[2,1024,256]{2,1,0:T(8,128)(2,1)S(1)} %copy-done.164), channel_id=1, source_target_pairs={{0,4},{2,6},{4,0},{6,2},{1,5},{3,7},{5,1},{7,3},{8,12},{10,14},{12... | collective-permute-start | bytes 3145736 | tf_op jit(solution)/shard_map/ppermute | solution.py:339
  542.3 29.4 %collective-permute-start.52 = (bf16[2,256,256]{2,1,0:T(8,128)(2,1)S(1)}, bf16[2,256,256]{2,1,0:T(8,128)(2,1)S(1)}, u32[]{:S(2)}, u32[]{:S(2)}) collective-permute-start(bf16[2,256,256]{2,1,0:T(8,128)(2,1)S(1)} %pad_maximum_fusion.14), channel_id=1, source_target_pairs={{0,4},{2,6},{4,0},{6,2},{1,5},{3,7},{5,1},{7,3},{8,12},{10,14},{12... | collective-permute-start | bytes 786440 | tf_op jit(solution)/shard_map/ppermute | solution.py:339
  574.4 29.0 %collective-permute-start.21 = (bf16[256,1024]{1,0:T(8,128)(2,1)S(1)}, bf16[256,1024]{1,0:T(8,128)(2,1)S(1)}, u32[]{:S(2)}, u32[]{:S(2)}) collective-permute-start(bf16[256,1024]{1,0:T(8,128)(2,1)S(1)} %add_convert_fusion.19.chip_ref), channel_id=1, source_target_pairs={{0,1},{1,0},{2,3},{3,2},{4,5},{5,4},{6,7},{7,6},{8,9},{9,8},{10,11... | collective-permute-start | bytes 1572872 | tf_op jit(solution)/shard_map/ppermute | solution.py:351
  591.9 71.3 %collective-permute-start.63 = (bf16[2,256,1024]{2,1,0:T(8,128)(2,1)}, bf16[2,256,1024]{2,1,0:T(8,128)(2,1)}, u32[]{:S(2)}, u32[]{:S(2)}) collective-permute-start(bf16[2,256,1024]{2,1,0:T(8,128)(2,1)} %add_convert_fusion.11), channel_id=1, source_target_pairs={{0,8},{24,16},{1,9},{25,17},{2,10},{26,18},{3,11},{27,19},{4,12},{... | collective-permute-start | bytes 3145736 | tf_op jit(solution)/shard_map/ppermute | solution.py:362
  596.0 80.0 %collective-permute-start.73 = (bf16[2,1024,256]{2,1,0:T(8,128)(2,1)}, bf16[2,1024,256]{2,1,0:T(8,128)(2,1)}, u32[]{:S(2)}, u32[]{:S(2)}) collective-permute-start(bf16[2,1024,256]{2,1,0:T(8,128)(2,1)} %add_convert_fusion.5), channel_id=1, source_target_pairs={{0,8},{24,16},{1,9},{25,17},{2,10},{26,18},{3,11},{27,19},{4,12},{... | collective-permute-start | bytes 3145736 | tf_op jit(solution)/shard_map/ppermute | solution.py:362
  601.3 65.5 %collective-permute-start.42 = (bf16[2,256,768]{2,1,0:T(8,128)(2,1)}, bf16[2,256,768]{2,1,0:T(8,128)(2,1)}, u32[]{:S(2)}, u32[]{:S(2)}) collective-permute-start(bf16[2,256,768]{2,1,0:T(8,128)(2,1)} %pad_maximum_fusion.10), channel_id=1, source_target_pairs={{0,4},{2,6},{4,0},{6,2},{1,5},{3,7},{5,1},{7,3},{8,12},{10,14},{12... | collective-permute-start | bytes 2359304 | tf_op jit(solution)/shard_map/ppermute | solution.py:339
  603.4 39.0 %collective-permute-start.54 = (bf16[2,256,256]{2,1,0:T(8,128)(2,1)}, bf16[2,256,256]{2,1,0:T(8,128)(2,1)}, u32[]{:S(2)}, u32[]{:S(2)}) collective-permute-start(bf16[2,256,256]{2,1,0:T(8,128)(2,1)} %add_convert_fusion.30), channel_id=1, source_target_pairs={{8,16},{16,8},{9,17},{17,9},{10,18},{18,10},{11,19},{19,11},{12,20... | collective-permute-start | bytes 786440 | tf_op jit(solution)/shard_map/ppermute | solution.py:364
  666.1 26.8 %collective-permute-start.64 = (bf16[2,256,1024]{2,1,0:T(8,128)(2,1)S(1)}, bf16[2,256,1024]{2,1,0:T(8,128)(2,1)S(1)}, u32[]{:S(2)}, u32[]{:S(2)}) collective-permute-start(bf16[2,256,1024]{2,1,0:T(8,128)(2,1)S(1)} %add_convert_fusion.10), channel_id=1, source_target_pairs={{8,16},{16,8},{9,17},{17,9},{10,18},{18,10},{11,19},{19,11},{12,20... | collective-permute-start | bytes 3145736 | tf_op jit(solution)/shard_map/ppermute | solution.py:364
  693.3 30.6 %collective-permute-start.65 = (bf16[2,256,1024]{2,1,0:T(8,128)(2,1)S(1)}, bf16[2,256,1024]{2,1,0:T(8,128)(2,1)S(1)}, u32[]{:S(2)}, u32[]{:S(2)}) collective-permute-start(bf16[2,256,1024]{2,1,0:T(8,128)(2,1)S(1)} %add_convert_fusion.9), channel_id=1, source_target_pairs={{8,0},{16,24},{9,1},{17,25},{10,2},{18,26},{11,3},{19,27},{12,4},{... | collective-permute-start | bytes 3145736 | tf_op jit(solution)/shard_map/ppermute | solution.py:366
  695.0 51.4 %collective-permute-start.75 = (bf16[2,1024,256]{2,1,0:T(8,128)(2,1)S(1)}, bf16[2,1024,256]{2,1,0:T(8,128)(2,1)S(1)}, u32[]{:S(2)}, u32[]{:S(2)}) collective-permute-start(bf16[2,1024,256]{2,1,0:T(8,128)(2,1)S(1)} %add_convert_fusion.3), channel_id=1, source_target_pairs={{8,0},{16,24},{9,1},{17,25},{10,2},{18,26},{11,3},{19,27},{12,4},{... | collective-permute-start | bytes 3145736 | tf_op jit(solution)/shard_map/ppermute | solution.py:366
  697.5 63.3 %collective-permute-start.45 = (bf16[2,256,768]{2,1,0:T(8,128)(2,1)S(1)}, bf16[2,256,768]{2,1,0:T(8,128)(2,1)S(1)}, u32[]{:S(2)}, u32[]{:S(2)}) collective-permute-start(bf16[2,256,768]{2,1,0:T(8,128)(2,1)S(1)} %add_convert_fusion.15), channel_id=1, source_target_pairs={{8,0},{16,24},{9,1},{17,25},{10,2},{18,26},{11,3},{19,27},{12,4},{... | collective-permute-start | bytes 2359304 | tf_op jit(solution)/shard_map/ppermute | solution.py:366
  (228 other events, 1541.4 us)

commit v3 on v2

--- a/solution.py
+++ b/solution.py
@@ -335,70 +335,6 @@
     )
 
 
-def swap_row(value, bits):
-    return lax.ppermute(value, "row", [(i, i ^ bits) for i in range(4)])
-
-
-def swap_core(value):
-    return swap_row(value, 1)
-
-
-def swap_chip(value):
-    return swap_row(value, 2)
-
-
-def swap_col(value):
-    return lax.ppermute(value, "col", [(0, 1), (1, 0)])
-
-
-def after(value, *others):
-    return lax.optimization_barrier((value, *others))[0]
-
-
-def dp_total(value):
-    place = lax.axis_index("dp")
-    inner = (place == 1) | (place == 2)
-    kind = value.dtype
-    from_end = lax.ppermute(value, "dp", [(0, 1), (3, 2)])
-    half = (value.astype(f32) + from_end.astype(f32)).astype(kind)
-    from_inner = lax.ppermute(half, "dp", [(1, 2), (2, 1)])
-    whole = (half.astype(f32) + from_inner.astype(f32)).astype(kind)
-    back = lax.ppermute(whole, "dp", [(1, 0), (2, 3)])
-    return jnp.where(inner, whole, back)
-
-
-def half_of(value, index, axis):
-    size = value.shape[axis] // 2
-    return lax.dynamic_slice_in_dim(value, index * size, size, axis)
-
-
-def in_place(first, mine, other, axis):
-    return jnp.where(
-        first,
-        jnp.concatenate([mine, other], axis=axis),
-        jnp.concatenate([other, mine], axis=axis),
-    )
-
-
-def gather_weight(core, own, cut, join):
-    peer = swap_chip(own)
-    mine = [half_of(v, core, cut) for v in (own, peer)]
-    theirs = jnp.stack([half_of(v, 1 - core, cut) for v in (own, peer)])
-    theirs = swap_core(theirs)
-    return jnp.concatenate([mine[0], theirs[0], mine[1], theirs[1]], axis=join), peer
-
-
-def spread_grad(keep, give):
-    row = lax.axis_index("row")
-    keep, give = [jnp.where(row % 2 == 0, a, b) for a, b in ((keep, give), (give, keep))]
-    keep, give = [jnp.where(row // 2 == 0, v, v[::-1]) for v in (keep, give)]
-    got = swap_core(give)
-    away = swap_chip(jnp.stack([keep[1], got[1]]))
-    own = jnp.stack([keep[0], got[0]])
-    total = dp_total((own.astype(f32) + away.astype(f32)).astype(bf16)).astype(f32)
-    return total[0], total[1]
-
-
 def dot(a, b):
     return lax.dot_general(a, b, (((1,), (0,)), ((), ())), preferred_element_type=f32)
 
@@ -411,366 +347,8 @@
     return lax.dot_general(a, b, (((0,), (0,)), ((), ())), preferred_element_type=f32)
 
 
-def kernel_call(body, outs, args, flops, grid=None, in_specs=None, out_specs=None, scratch=(), limit=40):
-    moved = sum(math.prod(v.shape) * v.dtype.itemsize for v in (*outs, *args))
-    whole = pl.BlockSpec(memory_space=pltpu.VMEM)
-    if in_specs is None:
-        in_specs = [
-            pl.BlockSpec(memory_space=pltpu.SMEM) if v.dtype == jnp.int32 and v.size == 1 else whole
-            for v in args
-        ]
-    extra = {} if grid is None else {"grid": grid}
-    return pl.pallas_call(
-        body,
-        out_shape=outs,
-        in_specs=in_specs,
-        out_specs=out_specs if out_specs is not None else [whole] * len(outs),
-        scratch_shapes=list(scratch),
-        compiler_params=pltpu.CompilerParams(vmem_limit_bytes=limit * 1024 * 1024),
-        cost_estimate=pl.CostEstimate(flops=flops, bytes_accessed=moved, transcendentals=0),
-        **extra,
-    )(*args)
-
-
 def like(shape, kind):
     return jax.ShapeDtypeStruct(shape, kind)
-
-
-def other_order(value):
-    return value
-
-
-def part_rows(index):
-    return pl.ds(pl.multiple_of(index * OWN, OWN), OWN)
-
-
-def join_tokens(core_ref, own_ref, sib_ref, full_ref):
-    core = core_ref[0]
-    full_ref[part_rows(core), :] = own_ref[...]
-    full_ref[part_rows(1 - core), :] = other_order(sib_ref[...])
-
-
-def part_tokens(core_ref, sums_ref, mine_ref, other_ref):
-    core = core_ref[0]
-    mine_ref[...] = sums_ref[part_rows(core), :]
-    other_ref[...] = other_order(sums_ref[part_rows(1 - core), :]).astype(bf16)
-
-
-def head_lanes(h):
-    lane = lax.broadcasted_iota(jnp.int32, (1, WIDTH), 1)
-    return (lane >= h * HD) & (lane < (h + 1) * HD)
-
-
-def allowed_pairs(seg_col, seg_row, start, keys):
-    same = seg_col == seg_row
-    query = lax.broadcasted_iota(jnp.int32, (QB, keys), 0) + start
-    key = lax.broadcasted_iota(jnp.int32, (QB, keys), 1)
-    return same & (key <= query)
-
-
-HEADS_HERE = WIDTH // HD
-
-
-def attend_body(chunk, *refs):
-    core_ref, own_ref, sib_ref, triple_w_ref, bias_ref, output_w_ref, col_ref, row_ref = refs[:8]
-    earlier = refs[8 : 8 + chunk]
-    full_ref, triple_ref, mixed_ref, log_ref, mine_ref, other_ref = refs[8 + chunk : 14 + chunk]
-    kv_ref, sums_ref = refs[14 + chunk :]
-    scale = 1.0 / math.sqrt(HD)
-    join_tokens(core_ref, own_ref, sib_ref, full_ref)
-    for part in range(3):
-        cols = slice(part * WIDTH, (part + 1) * WIDTH)
-        triple_ref[:, cols] = (
-            dot(full_ref[...], triple_w_ref[:, cols]) + bias_ref[:, cols]
-        ).astype(bf16)
-    for k in range(chunk):
-        kv_ref[k * SPAN : (k + 1) * SPAN, :] = earlier[k][:, WIDTH:]
-    kv_ref[chunk * SPAN :, :] = triple_ref[:, WIDTH:]
-    for block in range(SPAN // QB):
-        rows = slice(block * QB, (block + 1) * QB)
-        start = chunk * SPAN + block * QB
-        keys = start + QB
-        allowed = allowed_pairs(col_ref[start : start + QB, :], row_ref[:, :keys], start, keys)
-        queries = triple_ref[rows, :WIDTH] * scale
-        key_rows = kv_ref[:keys, :WIDTH]
-        value_rows = kv_ref[:keys, WIDTH:]
-        blended = jnp.zeros((QB, WIDTH), f32)
-        for h in range(HEADS_HERE):
-            lanes = head_lanes(h)
-            scores = dot_nt(jnp.where(lanes, queries, 0).astype(bf16), key_rows)
-            scores = jnp.where(allowed, scores, masked)
-            peak = jnp.max(scores, axis=1, keepdims=True)
-            exponent = jnp.exp(scores - peak)
-            total = jnp.sum(exponent, axis=1, keepdims=True)
-            soft = (exponent * (1.0 / total)).astype(bf16)
-            blended = jnp.where(lanes, dot(soft, value_rows), blended)
-            log_ref[rows, h : h + 1] = peak + jnp.log(total)
-        mixed_ref[rows, :] = blended.astype(bf16)
-    sums_ref[...] = dot(mixed_ref[...], output_w_ref[...])
-    part_tokens(core_ref, sums_ref, mine_ref, other_ref)
-
-
-def attend_call(chunk, core, own, sib, triple_w, bias, output_w, seg_col, seg_row, earlier):
-    return kernel_call(
-        lambda *refs: attend_body(chunk, *refs),
-        [
-            like((SPAN, D), bf16),
-            like((SPAN, 3 * WIDTH), bf16),
-            like((SPAN, WIDTH), bf16),
-            like((SPAN, 128), f32),
-            like((OWN, D), f32),
-            like((OWN, D), bf16),
-        ],
-        (core, own, sib, triple_w, bias, output_w, seg_col, seg_row, *earlier),
-        2 * SPAN * D * 4 * WIDTH + 8 * 4 * SPAN * (chunk + 1) * SPAN * WIDTH,
-        scratch=[pltpu.VMEM(((chunk + 1) * SPAN, 2 * WIDTH), bf16), pltpu.VMEM((SPAN, D), f32)],
-    )
-
-
-GELU = math.sqrt(2.0 / math.pi)
-
-
-def mlp_body(core_ref, own_ref, sib_ref, up_ref, bias_ref, down_ref, *refs):
-    full_ref, pre_ref, active_ref, mine_ref, other_ref, sums_ref = refs
-    step = pl.program_id(0)
-
-    @pl.when(step == 0)
-    def _():
-        join_tokens(core_ref, own_ref, sib_ref, full_ref)
-
-    pre = dot(full_ref[...], up_ref[...]) + bias_ref[...]
-    pre_ref[...] = pre
-    curve = jnp.tanh(GELU * (pre + 0.044715 * (pre * pre * pre)))
-    active = (0.5 * pre * (1.0 + curve)).astype(bf16)
-    active_ref[...] = active
-    sums = dot(active, down_ref[...])
-
-    @pl.when(step == 0)
-    def _():
-        sums_ref[...] = sums
-
-    @pl.when(step > 0)
-    def _():
-        sums_ref[...] += sums
-
-    @pl.when(step == pl.num_programs(0) - 1)
-    def _():
-        part_tokens(core_ref, sums_ref, mine_ref, other_ref)
-
-
-def mlp_call(core, own, sib, up_w, bias, down_w):
-    units = up_w.shape[1]
-    step = 256
-    whole = pl.BlockSpec((OWN, D), lambda i: (0, 0))
-    return kernel_call(
-        mlp_body,
-        [
-            like((SPAN, D), bf16),
-            like((SPAN, units), f32),
-            like((SPAN, units), bf16),
-            like((OWN, D), f32),
-            like((OWN, D), bf16),
-        ],
-        (core, own, sib, up_w, bias, down_w),
-        4 * SPAN * D * units,
-        grid=(units // step,),
-        in_specs=[
-            pl.BlockSpec(memory_space=pltpu.SMEM),
-            whole,
-            whole,
-            pl.BlockSpec((D, step), lambda i: (0, i)),
-            pl.BlockSpec((1, step), lambda i: (0, i)),
-            pl.BlockSpec((step, D), lambda i: (i, 0)),
-        ],
-        out_specs=[
-            pl.BlockSpec((SPAN, D), lambda i: (0, 0)),
-            pl.BlockSpec((SPAN, step), lambda i: (0, i)),
-            pl.BlockSpec((SPAN, step), lambda i: (0, i)),
-            whole,
-            whole,
-        ],
-        scratch=[pltpu.VMEM((SPAN, D), f32)],
-    )
-
-
-def mlp_back_body(core_ref, own_ref, sib_ref, down_ref, pre_ref, up_ref, *refs):
-    full_ref, hidden_ref, bias_ref, mine_ref, other_ref, sums_ref = refs
-    step = pl.program_id(0)
-
-    @pl.when(step == 0)
-    def _():
-        join_tokens(core_ref, own_ref, sib_ref, full_ref)
-
-    active_grad = dot_nt(full_ref[...], down_ref[...])
-    hidden = (active_grad * pre_ref[...].astype(f32)).astype(bf16)
-    hidden_ref[...] = hidden
-    bias_ref[...] = jnp.sum(hidden.astype(f32), axis=0, keepdims=True)
-    sums = dot_nt(hidden, up_ref[...])
-
-    @pl.when(step == 0)
-    def _():
-        sums_ref[...] = sums
-
-    @pl.when(step > 0)
-    def _():
-        sums_ref[...] += sums
-
-    @pl.when(step == pl.num_programs(0) - 1)
-    def _():
-        part_tokens(core_ref, sums_ref, mine_ref, other_ref)
-
-
-def mlp_back_call(core, own, sib, down_w, pre, up_w):
-    units = up_w.shape[1]
-    step = 256
-    whole = pl.BlockSpec((OWN, D), lambda i: (0, 0))
-    return kernel_call(
-        mlp_back_body,
-        [
-            like((SPAN, D), bf16),
-            like((SPAN, units), bf16),
-            like((1, units), f32),
-            like((OWN, D), f32),
-            like((OWN, D), bf16),
-        ],
-        (core, own, sib, down_w, pre, up_w),
-        4 * SPAN * D * units,
-        grid=(units // step,),
-        in_specs=[
-            pl.BlockSpec(memory_space=pltpu.SMEM),
-            whole,
-            whole,
-            pl.BlockSpec((step, D), lambda i: (i, 0)),
-            pl.BlockSpec((SPAN, step), lambda i: (0, i)),
-            pl.BlockSpec((D, step), lambda i: (0, i)),
-        ],
-        out_specs=[
-            pl.BlockSpec((SPAN, D), lambda i: (0, 0)),
-            pl.BlockSpec((SPAN, step), lambda i: (0, i)),
-            pl.BlockSpec((1, step), lambda i: (0, i)),
-            whole,
-            whole,
-        ],
-        scratch=[pltpu.VMEM((SPAN, D), f32)],
-    )
-
-
-def attend_back_body(chunk, later, *refs):
-    core_ref, own_ref, sib_ref, output_w_ref, triple_w_ref, log_ref, col_ref, row_ref = refs[:8]
-    triples = refs[8 : 9 + chunk]
-    refs = refs[9 + chunk :]
-    if later:
-        carried_ref, refs = refs[0], refs[1:]
-    full_ref, rows_ref, bias_ref, mine_ref, other_ref = refs[:5]
-    refs = refs[5:]
-    if chunk:
-        carry_ref, refs = refs[0], refs[1:]
-    kv_ref, grad_ref, total_ref, sums_ref = refs
-    scale = 1.0 / math.sqrt(HD)
-    triple_ref = triples[chunk]
-    join_tokens(core_ref, own_ref, sib_ref, full_ref)
-    grad_ref[...] = dot_nt(full_ref[...], output_w_ref[...]).astype(bf16)
-    for k in range(chunk + 1):
-        kv_ref[k * SPAN : (k + 1) * SPAN, :] = triples[k][:, WIDTH:]
-    if later:
-        total_ref[...] = carried_ref[...]
-    else:
-        total_ref[...] = jnp.zeros_like(total_ref)
-    for block in range(SPAN // QB):
-        rows = slice(block * QB, (block + 1) * QB)
-        start = chunk * SPAN + block * QB
-        keys = start + QB
-        allowed = allowed_pairs(col_ref[start : start + QB, :], row_ref[:, :keys], start, keys)
-        queries = triple_ref[rows, :WIDTH] * scale
-        grads = grad_ref[rows, :]
-        key_rows = kv_ref[:keys, :WIDTH]
-        value_rows = kv_ref[:keys, WIDTH:]
-        query_grad = jnp.zeros((QB, WIDTH), f32)
-        for h in range(HEADS_HERE):
-            lanes = head_lanes(h)
-            query = jnp.where(lanes, queries, 0).astype(bf16)
-            grad = jnp.where(lanes, grads, 0).astype(bf16)
-            scores = jnp.where(allowed, dot_nt(query, key_rows), masked)
-            chances = jnp.exp(scores - log_ref[rows, h : h + 1])
-            product = chances * dot_nt(grad, value_rows)
-            inner = jnp.sum(product, axis=1, keepdims=True)
-            score_grad = (product - chances * inner).astype(bf16)
-            query_grad = jnp.where(lanes, dot(score_grad, key_rows), query_grad)
-            total_ref[:keys, :WIDTH] += dot_tn(score_grad, query)
-            total_ref[:keys, WIDTH:] += dot_tn(chances.astype(bf16), grad)
-        rows_ref[rows, :WIDTH] = (query_grad * scale).astype(bf16)
-    rows_ref[:, WIDTH:] = total_ref[chunk * SPAN :, :].astype(bf16)
-    if chunk:
-        carry_ref[...] = total_ref[: chunk * SPAN, :]
-    bias_ref[0:1, :] = jnp.sum(rows_ref[:, :WIDTH].astype(f32), axis=0, keepdims=True)
-    bias_ref[1:2, :] = jnp.sum(rows_ref[:, 2 * WIDTH :].astype(f32), axis=0, keepdims=True)
-    sums_ref[...] = dot_nt(rows_ref[...], triple_w_ref[...])
-    part_tokens(core_ref, sums_ref, mine_ref, other_ref)
-
-
-def attend_back_call(
-    chunk, core, own, sib, output_w, triple_w, logs, seg_col, seg_row, triples, carried
-):
-    outs = [
-        like((SPAN, D), bf16),
-        like((SPAN, 3 * WIDTH), bf16),
-        like((2, WIDTH), f32),
-        like((OWN, D), f32),
-        like((OWN, D), bf16),
-    ]
-    if chunk:
-        outs.append(like((chunk * SPAN, 2 * WIDTH), f32))
-    later = () if carried is None else (carried,)
-    return kernel_call(
-        lambda *refs: attend_back_body(chunk, bool(later), *refs),
-        outs,
-        (core, own, sib, output_w, triple_w, logs, seg_col, seg_row, *triples, *later),
-        2 * SPAN * D * 4 * WIDTH + 20 * 4 * SPAN * (chunk + 1) * SPAN * WIDTH,
-        scratch=[
-            pltpu.VMEM(((chunk + 1) * SPAN, 2 * WIDTH), bf16),
-            pltpu.VMEM((SPAN, WIDTH), bf16),
-            pltpu.VMEM(((chunk + 1) * SPAN, 2 * WIDTH), f32),
-            pltpu.VMEM((SPAN, D), f32),
-        ],
-    )
-
-
-def weight_grad_body(join, *refs):
-    left, right = refs[:CHUNKS], refs[CHUNKS : 2 * CHUNKS]
-    keep_ref, give_ref = refs[2 * CHUNKS :]
-    total = dot_tn(left[0][...], right[0][...])
-    for k in range(1, CHUNKS):
-        total += dot_tn(left[k][...], right[k][...])
-    total = total.astype(bf16)
-    if join == 0:
-        keep_ref[0] = total[:WIDTH]
-        give_ref[0] = total[WIDTH:]
-    else:
-        for k in range(2):
-            keep_ref[k] = total[:, 2 * k * WIDTH : (2 * k + 1) * WIDTH]
-            give_ref[k] = total[:, (2 * k + 1) * WIDTH : (2 * k + 2) * WIDTH]
-
-
-def weight_grad(left, right, join):
-    high, across = left[0].shape[1], right[0].shape[1]
-    part = min(512, high)
-    steps = high // part
-    if join == 0:
-        shape = (2, WIDTH, across)
-        out = pl.BlockSpec((1, WIDTH, across), lambda i: (i, 0, 0))
-    else:
-        shape = (2, high, WIDTH)
-        out = pl.BlockSpec((2, part, WIDTH), lambda i: (0, i, 0))
-    return kernel_call(
-        lambda *refs: weight_grad_body(join, *refs),
-        [like(shape, bf16)] * 2,
-        (*left, *right),
-        2 * LEN * high * across,
-        grid=(steps,),
-        in_specs=[pl.BlockSpec((SPAN, part), lambda i: (0, i))] * CHUNKS
-        + [pl.BlockSpec((SPAN, across), lambda i: (0, 0))] * CHUNKS,
-        out_specs=[out, out],
-    )
 
 
 def mean_lanes(v):
@@ -784,54 +362,13 @@
     return (v - center) * inv_std, inv_std
 
 
-def norm_body(stream_ref, chip_ref, got_ref, bias_ref, gain_ref, shift_ref, after_ref, out_ref):
-    total = chip_ref[...].astype(f32) + got_ref[...].astype(f32)
-    after_sum = stream_ref[...] + (total + bias_ref[...])
-    after_ref[...] = after_sum
-    normed, _ = norm_parts(after_sum)
-    out_ref[...] = (normed * gain_ref[...] + shift_ref[...]).astype(bf16)
-
-
-def norm_call(stream, chip, got, bias, gain, shift):
-    return kernel_call(
-        norm_body,
-        [like((OWN, D), f32), like((OWN, D), bf16)],
-        (stream, chip, got, bias[None], gain[None], shift[None]),
-        20 * OWN * D,
-    )
-
-
-def norm_back_body(grad_ref, chip_ref, got_ref, stream_ref, gain_ref, out_ref, low_ref, sums_ref):
-    grad_out = chip_ref[...].astype(f32) + got_ref[...].astype(f32)
-    normed, inv_std = norm_parts(stream_ref[...])
-    scaled = grad_out * gain_ref[...]
-    total = grad_ref[...] + inv_std * (
-        scaled - mean_lanes(scaled) - normed * mean_lanes(scaled * normed)
-    )
-    low = total.astype(bf16)
-    out_ref[...] = total
-    low_ref[...] = low
-    sums_ref[0:1, :] = jnp.sum(grad_out * normed, axis=0, keepdims=True)
-    sums_ref[1:2, :] = jnp.sum(grad_out, axis=0, keepdims=True)
-    sums_ref[2:3, :] = jnp.sum(low.astype(f32), axis=0, keepdims=True)
-
-
-def norm_back_call(grad, chip, got, stream, gain):
-    return kernel_call(
-        norm_back_body,
-        [like((OWN, D), f32), like((OWN, D), bf16), like((3, D), f32)],
-        (grad, chip, got, stream, gain[None]),
-        30 * OWN * D,
-    )
-
-
-def chip_total(mine, other):
-    return (mine + swap_core(other).astype(f32)).astype(bf16)
+GELU = math.sqrt(2.0 / math.pi)
 
 
 MESH = pl.DeviceIdType.MESH
 HEADS_HERE = WIDTH // HD
 SMALL = 24
+SEG = 64
 
 
 class Place:
@@ -978,6 +515,7 @@
             soft = (exponent * (1.0 / total)).astype(bf16)
             blended = jnp.where(lanes, dot(soft, value_rows), blended)
             log_ref[rows, h : h + 1] = peak + jnp.log(total)
+        log_ref[rows, SEG : SEG + 1] = seg_col_ref[start : start + QB, :].astype(f32)
         mixed_ref[rows, :] = blended.astype(bf16)
 
 
@@ -1408,6 +946,710 @@
     return jnp.pad(lines, ((0, SMALL - lines.shape[0]), (0, 0)))
 
 
+PIECES = ((3, WIDTH, WIDTH), (1, WIDTH, WIDTH), (2, WIDTH // 2, D), (2, D // 2, WIDTH))
+LINES = 16
+
+
+def attend_back_chunk(
+    k, rows_ref, log_ref, seg_row_ref, grad_ref, total_ref, out_ref
+):
+    scale = 1.0 / math.sqrt(HD)
+    for block in range(SPAN // QB):
+        start = k * SPAN + block * QB
+        keys = start + QB
+        here = slice(start, keys)
+        allowed = causal(log_ref[here, SEG : SEG + 1], seg_row_ref[:, :keys], start, keys)
+        queries = rows_ref[here, :WIDTH] * scale
+        grads = grad_ref[block * QB : (block + 1) * QB, :]
+        key_rows = rows_ref[:keys, WIDTH : 2 * WIDTH]
+        value_rows = rows_ref[:keys, 2 * WIDTH :]
+        query_grad = jnp.zeros((QB, WIDTH), f32)
+        for h in range(HEADS_HERE):
+            lanes = lanes_of(h)
+            query = jnp.where(lanes, queries, 0).astype(bf16)
+            grad = jnp.where(lanes, grads, 0).astype(bf16)
+            scores = jnp.where(allowed, dot_nt(query, key_rows), masked)
+            chances = jnp.exp(scores - log_ref[here, h : h + 1])
+            product = chances * dot_nt(grad, value_rows)
+            inner = jnp.sum(product, axis=1, keepdims=True)
+            score_grad = (product - chances * inner).astype(bf16)
+            query_grad = jnp.where(lanes, dot(score_grad, key_rows), query_grad)
+            total_ref[:keys, :WIDTH] += dot_tn(score_grad, query)
+            total_ref[:keys, WIDTH:] += dot_tn(chances.astype(bf16), grad)
+        out_ref[here, :WIDTH] = (query_grad * scale).astype(bf16)
+    here = slice(k * SPAN, (k + 1) * SPAN)
+    out_ref[here, WIDTH:] = total_ref[here, :].astype(bf16)
+
+
+def add_pieces(target, left, right):
+    high, across = target.shape
+    step = 32768 // across
+
+    def body(i, carry):
+        lines = pl.ds(pl.multiple_of(i * step, step), step)
+        target[lines, :] = (left[lines, :].astype(f32) + right[lines, :].astype(f32)).astype(bf16)
+        return carry
+
+    lax.fori_loop(0, high // step, body, 0)
+
+
+class Reduction:
+    def __init__(self, kind, layer, place, copies, grads, land, ends, inner, outs, credits):
+        self.kind, self.layer, self.place, self.copies = kind, layer, place, copies
+        self.grads, self.land, self.ends, self.inner = grads[kind], land[kind], ends[kind], inner[kind]
+        self.out, self.credits = outs[kind], credits
+        self.count = PIECES[kind][0]
+        self.again = layer < LAYERS - 1
+        self.is_end = place.dp * (3 - place.dp) == 0
+        self.is_inner = place.dp * (3 - place.dp) > 0
+
+    def home(self, which, s):
+        core = self.place.cores[which]
+        out, layer = self.out, self.layer
+        if self.kind == 0:
+            return out.at[layer, s, :, span(core * WIDTH, WIDTH)]
+        if self.kind == 1:
+            return out.at[layer, span(core * WIDTH, WIDTH), :]
+        if self.kind == 2:
+            return out.at[layer, s * (WIDTH // 2) : (s + 1) * (WIDTH // 2), span(core * D, D)]
+        return out.at[layer, span(core * D + s * (D // 2), D // 2), :]
+
+    def send(self):
+        place, copies = self.place, self.copies
+        if self.again:
+            pl.semaphore_wait(self.credits.at[self.kind], 3)
+        self.waits = {}
+        self.sent = []
+        for s in range(self.count):
+            for j in (2, 3, 1):
+                sent, got = copies.trade(
+                    self.grads.at[place.rows[j], s],
+                    self.land.at[j - 1, s],
+                    self.land.at[j - 1, s],
+                    place.to_row(j),
+                )
+                self.sent.append(sent)
+                self.waits[j, s] = got
+
+    def over_chips(self, s):
+        place, copies = self.place, self.copies
+        if s == 0:
+            self.to_inner = {}
+            if self.again:
+
+                @pl.when(self.is_end)
+                def _():
+                    pl.semaphore_wait(self.credits.at[4 + self.kind], 1)
+
+        for which in range(2):
+            if which == 0:
+                self.waits[2, s]()
+                target = self.land.at[1, s]
+                add_pieces(target, self.grads.at[place.row, s], target)
+            else:
+                self.waits[1, s]()
+                self.waits[3, s]()
+                target = self.land.at[2, s]
+                add_pieces(target, self.land.at[0, s], target)
+            copy = pltpu.make_async_remote_copy(
+                target,
+                self.ends.at[which, s],
+                copies.sem(),
+                copies.sem(),
+                device_id=place.to_dp(),
+                device_id_type=MESH,
+            )
+            self.to_inner[which, s] = copy
+
+            @pl.when(self.is_end)
+            def _():
+                copy.start()
+
+    def to_middle(self, s):
+        place, copies = self.place, self.copies
+        if s == 0:
+            self.across = {}
+            if self.again:
+
+                @pl.when(self.is_inner)
+                def _():
+                    pl.semaphore_wait(self.credits.at[8 + self.kind], 1)
+
+        for which in range(2):
+            half = self.ends.at[which, s]
+            copy = pltpu.make_async_remote_copy(
+                half,
+                self.inner.at[which, s],
+                copies.sem(),
+                copies.sem(),
+                device_id={"dp": 3 - place.dp},
+                device_id_type=MESH,
+            )
+            self.across[which, s] = copy
+
+            @pl.when(self.is_inner)
+            def _():
+                self.to_inner[which, s].wait_recv()
+                add_pieces(half, self.land.at[1 + which, s], half)
+                copy.start()
+
+        if s == self.count - 1:
+
+            @pl.when(self.is_end)
+            def _():
+                for copy in self.to_inner.values():
+                    copy.wait_send()
+
+            for sent in self.sent:
+                sent()
+            if not self.again:
+                for j in range(1, 4):
+                    pl.semaphore_signal(
+                        self.credits.at[self.kind],
+                        inc=1,
+                        device_id=place.to_row(j),
+                        device_id_type=MESH,
+                    )
+
+    def back(self, s):
+        place, copies = self.place, self.copies
+        if s == 0:
+            self.out_copies = []
+        for which in range(2):
+            total = self.inner.at[which, s]
+            home = self.home(which, s)
+            copy = pltpu.make_async_remote_copy(
+                total,
+                home,
+                copies.sem(),
+                copies.sem(),
+                device_id=place.to_dp(),
+                device_id_type=MESH,
+            )
+            here = pltpu.make_async_copy(total, home, copies.sem())
+            self.out_copies.append((copy, here))
+
+            @pl.when(self.is_inner)
+            def _():
+                self.across[which, s].wait_recv()
+                add_pieces(total, self.ends.at[which, s], total)
+                copy.start()
+                here.start()
+
+    def finish(self):
+        place = self.place
+
+        @pl.when(self.is_inner)
+        def _():
+            for copy in self.across.values():
+                copy.wait_send()
+            for copy, here in self.out_copies:
+                copy.wait_send()
+                here.wait()
+            if not self.again:
+                pl.semaphore_signal(
+                    self.credits.at[4 + self.kind], inc=1, device_id=place.to_dp(), device_id_type=MESH
+                )
+                pl.semaphore_signal(
+                    self.credits.at[8 + self.kind],
+                    inc=1,
+                    device_id={"dp": 3 - place.dp},
+                    device_id_type=MESH,
+                )
+
+        @pl.when(self.is_end)
+        def _():
+            for copy, here in self.out_copies:
+                copy.wait_recv()
+
+
+def backward_body(*refs):
+    (
+        grad_in,
+        wide_ref,
+        seg_row_ref,
+        triple_in,
+        output_in,
+        up_in,
+        down_in_w,
+        attn_in,
+        rows_in,
+        mixed_in,
+        log_in,
+        mlp_in,
+        slope_in,
+        active_in,
+        stream_in,
+        input_grad_ref,
+        small_out,
+        triple_out,
+        output_out,
+        up_out,
+        down_out,
+        triple_w,
+        output_w,
+        up_w,
+        down_w,
+        attn,
+        rows,
+        mixed,
+        logs,
+        mlp,
+        slope,
+        active,
+        start,
+        middle,
+        down_in,
+        hidden,
+        branch,
+        rows_grad,
+        mixed_grad,
+        pair_total,
+        grad,
+        mine,
+        give,
+        got_core,
+        chip_sum,
+        got_col,
+        sums,
+        lines,
+        line_land,
+        dp_land,
+        *rest,
+    ) = refs
+    grads, land, ends, inner = rest[0:4], rest[4:8], rest[8:12], rest[12:16]
+    credits, sems = rest[16:]
+    place = Place()
+    copies = Copies(sems)
+    core, sibling = place.core, 1 - place.core
+    others = [{"dp": (place.dp + i) % 4} for i in range(1, 4)]
+    greet(place, [place.to_row(1), place.to_row(2), place.to_row(3), place.to_col(), *others])
+    own_lanes = span(place.row * WIDTH, WIDTH)
+
+    def part(k, c):
+        return span(k * SPAN + c * OWN, OWN)
+
+    ready = {}
+
+    def load(name, layer):
+        source, target = {
+            "triple_w": (triple_in, triple_w),
+            "output_w": (output_in, output_w),
+            "up_w": (up_in, up_w),
+            "down_w": (down_in_w, down_w),
+            "attn": (attn_in, attn),
+            "rows": (rows_in, rows),
+            "mixed": (mixed_in, mixed),
+            "logs": (log_in, logs),
+            "mlp": (mlp_in, mlp),
+            "slope": (slope_in, slope),
+            "active": (active_in, active),
+            "start": (stream_in, start),
+            "middle": (stream_in, middle),
+        }[name]
+        if name in ("start", "middle"):
+            ready[name] = [copies.local(source.at[layer, int(name == "middle")], target).wait]
+        elif name.endswith("_w"):
+            ready[name] = [copies.local(source.at[layer], target).wait]
+        else:
+            ready[name] = [
+                copies.local(source.at[layer, k], target.at[k * SPAN : (k + 1) * SPAN]).wait
+                for k in range(CHUNKS)
+            ]
+
+    def need(name):
+        for wait in ready.pop(name, ()):
+            wait()
+
+    first_waits = [
+        copies.local(grad_in.at[k], down_in.at[part(k, core)]).wait for k in range(CHUNKS)
+    ]
+    top = LAYERS - 1
+    for name in ("active", "down_w", "slope", "up_w", "mlp", "middle"):
+        load(name, top)
+    for name in ("output_w", "rows", "logs", "triple_w", "mixed", "attn", "start"):
+        load(name, top)
+    sums[...] = jnp.zeros_like(sums)
+    lines[...] = jnp.zeros_like(lines)
+
+    def share(target, k):
+        return copies.trade(
+            target.at[part(k, core)], target.at[part(k, core)], target.at[part(k, sibling)], place.to_row(1)
+        )
+
+    def columns(value):
+        return jnp.sum(value.reshape(-1, 8, value.shape[1]), axis=0)
+
+    def gain(layer, which):
+        return wide_ref[2 * layer + which : 2 * layer + which + 1, :]
+
+    sent_core = []
+    sent_col, col_waits = [None] * CHUNKS, [None] * CHUNKS
+
+    def core_free():
+        while sent_core:
+            sent_core.pop()()
+
+    def start_core(stage, k):
+        sent, got = copies.trade(
+            give, got_core.at[stage, k], got_core.at[stage, k], place.to_row(1)
+        )
+        sent_core.append(sent)
+        return got
+
+    def settle(stage, k, got):
+        got()
+        if sent_col[k] is not None:
+            sent_col[k]()
+
+        def add(at):
+            here = pl.ds(at, 32)
+            chip_sum[k, here, :] = (mine[here, :] + got_core[stage, k, here, :].astype(f32)).astype(bf16)
+
+        strips(OWN, add)
+        sent_col[k], col_waits[k] = copies.trade(
+            chip_sum.at[k], got_col.at[stage, k], got_col.at[stage, k], place.to_col()
+        )
+
+    def take_col(stage, k, layer, which, stream, target):
+        col_waits[k]()
+        scale = gain(layer, which)
+
+        def back(at):
+            here = pl.ds(at, 32)
+            grad_out = chip_sum[k, here, :].astype(f32) + got_col[stage, k, here, :].astype(f32)
+            normed, inv_std = norm_parts(stream[k, here, :])
+            scaled = grad_out * scale
+            total = grad[k, here, :] + inv_std * (
+                scaled - mean_lanes(scaled) - normed * mean_lanes(scaled * normed)
+            )
+            low = total.astype(bf16)
+            grad[k, here, :] = total
+            target[pl.ds(pl.multiple_of(k * SPAN + core * OWN + at, 32), 32), :] = low
+            sums[layer, which] += columns(grad_out * normed)
+            sums[layer, 2 + which] += columns(grad_out)
+            if which == 1:
+                sums[layer, 4] += columns(low.astype(f32))
+            elif layer:
+                sums[layer - 1, 5] += columns(low.astype(f32))
+
+        strips(OWN, back)
+
+    shares = [None] * CHUNKS
+    for k in reversed(range(CHUNKS)):
+        first_waits[k]()
+        shares[k] = share(down_in, k)
+    for k in reversed(range(CHUNKS)):
+
+        def widen(at, k=k):
+            low = down_in[pl.ds(pl.multiple_of(k * SPAN + core * OWN + at, 32), 32), :]
+            value = low.astype(f32)
+            grad[k, pl.ds(at, 32), :] = value
+            sums[top, 5] += columns(value)
+
+        strips(OWN, widen)
+
+    reductions = {
+        (layer, kind): Reduction(
+            kind,
+            layer,
+            place,
+            copies,
+            grads,
+            land,
+            ends,
+            inner,
+            (triple_out, output_out, up_out, down_out),
+            credits,
+        )
+        for layer in range(LAYERS)
+        for kind in range(4)
+    }
+
+    def weight_grad(layer, kind):
+        if kind == 0:
+            need("attn")
+            for pair in range(2):
+                for third in range(3):
+                    value = dot_tn(
+                        attn[:, pair * 512 : (pair + 1) * 512],
+                        rows_grad[:, third * WIDTH : (third + 1) * WIDTH],
+                    ).astype(bf16)
+                    for b in range(2):
+                        grads[0][2 * pair + b, third] = value[b * WIDTH : (b + 1) * WIDTH]
+        elif kind == 1:
+            need("mixed")
+            value = dot_tn(mixed[...], branch[...]).astype(bf16)
+            for b in range(4):
+                grads[1][b, 0] = value[:, b * WIDTH : (b + 1) * WIDTH]
+        elif kind == 2:
+            need("mlp")
+            for b in range(4):
+                value = dot_tn(mlp[:, b * WIDTH : (b + 1) * WIDTH], hidden[...]).astype(bf16)
+                for s in range(2):
+                    grads[2][b, s] = value[s * (WIDTH // 2) : (s + 1) * (WIDTH // 2)]
+        else:
+            need("active")
+            for pair in range(4):
+                value = dot_tn(active[:, pair * WIDTH : (pair + 1) * WIDTH], down_in[...]).astype(bf16)
+                s, at = pair // 2, pair % 2 * WIDTH
+                for b in range(4):
+                    grads[3][b, s, at : at + WIDTH] = value[:, b * WIDTH : (b + 1) * WIDTH]
+        reductions[layer, kind].send()
+
+    def run(layer, kind, *names):
+        item = reductions[layer, kind]
+        for name in names:
+            if name == "finish":
+                item.finish()
+            else:
+                for s in range(item.count):
+                    getattr(item, name)(s)
+
+    for layer in reversed(range(LAYERS)):
+        for k in reversed(range(CHUNKS)):
+            if k == CHUNKS - 1 and layer == top:
+                for i in reversed(range(CHUNKS)):
+                    shares[i][1]()
+                weight_grad(layer, 3)
+            need("down_w")
+            need("slope")
+
+            def shrink(c, k=k):
+                for block in range(4):
+                    cols = slice(block * WIDTH, (block + 1) * WIDTH)
+                    value = dot_nt(down_in[part(k, c), :], down_w[cols, :])
+                    value = (value * slope[part(k, c), cols].astype(f32)).astype(bf16)
+                    hidden[part(k, c), cols] = value
+                    lines[layer, 8:16, cols] += columns(value.astype(f32))
+
+            if layer < top:
+                shrink(core)
+                shares[k][1]()
+                shrink(sibling)
+            else:
+                shrink(core)
+                shrink(sibling)
+            need("up_w")
+            core_free()
+            give[...] = dot_nt(hidden[part(k, sibling), :], up_w[...]).astype(bf16)
+            got = start_core(0, k)
+            mine[...] = dot_nt(hidden[part(k, core), :], up_w[...])
+            shares[k][0]()
+            settle(0, k, got)
+        if layer < top:
+            run(layer + 1, 3, "back", "finish")
+            run(layer + 1, 2, "to_middle")
+            weight_grad(layer, 3)
+            weight_grad(layer, 2)
+            run(layer + 1, 1, "over_chips")
+        else:
+            weight_grad(layer, 2)
+        if layer:
+            for name in ("active", "down_w", "slope", "up_w", "mlp"):
+                load(name, layer - 1)
+        for k in reversed(range(CHUNKS)):
+            need("middle")
+            take_col(0, k, layer, 1, middle, branch)
+            shares[k] = share(branch, k)
+            if layer and k == 0:
+                load("middle", layer - 1)
+            need("output_w")
+
+            def narrow(c, k=k):
+                mixed_grad[part(0, c), :] = dot_nt(branch[part(k, c), :], output_w[...]).astype(bf16)
+
+            narrow(core)
+            need("rows")
+            need("logs")
+            if k == CHUNKS - 1:
+                pair_total[...] = jnp.zeros_like(pair_total)
+            shares[k][1]()
+            narrow(sibling)
+            attend_back_chunk(
+                k, rows, logs, seg_row_ref, mixed_grad, pair_total, rows_grad
+            )
+            need("triple_w")
+            core_free()
+
+            def project(c, k=k):
+                value = dot_nt(rows_grad[part(k, c), :WIDTH], triple_w[0])
+                for third in range(1, 3):
+                    cols = slice(third * WIDTH, (third + 1) * WIDTH)
+                    value += dot_nt(rows_grad[part(k, c), cols], triple_w[third])
+                return value
+
+            give[...] = project(sibling).astype(bf16)
+            got = start_core(1, k)
+            mine[...] = project(core)
+            shares[k][0]()
+            settle(1, k, got)
+            if layer == top and k == CHUNKS - 1:
+                run(layer, 3, "over_chips")
+        here = rows_grad[:, :WIDTH].astype(f32)
+        lines[layer, 0:1, 0:WIDTH] = jnp.sum(here, axis=0, keepdims=True)
+        here = rows_grad[:, 2 * WIDTH :].astype(f32)
+        lines[layer, 0:1, WIDTH : 2 * WIDTH] = jnp.sum(here, axis=0, keepdims=True)
+        if layer < top:
+            run(layer + 1, 0, "over_chips")
+            run(layer + 1, 2, "back", "finish")
+            run(layer + 1, 1, "to_middle", "back", "finish")
+            run(layer + 1, 0, "to_middle")
+        weight_grad(layer, 1)
+        weight_grad(layer, 0)
+        if layer:
+            run(layer, 3, "to_middle")
+            run(layer, 2, "over_chips")
+            for name in ("output_w", "rows", "logs", "triple_w", "mixed", "attn"):
+                load(name, layer - 1)
+        for k in reversed(range(CHUNKS)):
+            need("start")
+            take_col(1, k, layer, 0, start, down_in)
+            if layer:
+                shares[k] = share(down_in, k)
+            if layer and k == 0:
+                load("start", layer - 1)
+    landed = []
+
+    def held(j, k):
+        return span(place.rows[j] // 2 * LEN + k * SPAN + place.cores[j] * OWN, OWN)
+
+    for k in reversed(range(CHUNKS)):
+        mine_rows = part(k, core)
+        landed.append(
+            copies.local(down_in.at[mine_rows, own_lanes], input_grad_ref.at[held(0, k), :]).wait
+        )
+        for j in range(1, 4):
+            sent, got = copies.trade(
+                down_in.at[mine_rows, span(place.rows[j] * WIDTH, WIDTH)],
+                input_grad_ref.at[held(0, k), :],
+                input_grad_ref.at[held(j, k), :],
+                place.to_row(j),
+            )
+            landed += [sent, got]
+    run(top, 0, "back", "finish")
+    zero = jnp.zeros((1, WIDTH // 2), f32)
+    for layer in range(LAYERS):
+        found = [jnp.sum(sums[layer, i], axis=0, keepdims=True) for i in range(6)]
+        hidden_sum = jnp.sum(lines[layer, 8:16, :], axis=0, keepdims=True)
+        base = layer * LINES
+        line_land[0, base : base + LINES, :] = jnp.zeros((LINES, D), f32)
+        for i in range(6):
+            line_land[0, base + i : base + i + 1, :] = found[i]
+        for b in range(2):
+            at = span((2 * core + b) * WIDTH, WIDTH)
+            half = slice(b * (WIDTH // 2), (b + 1) * (WIDTH // 2))
+            line_land[0, base + 6 : base + 7, at] = jnp.concatenate(
+                [lines[layer, 0:1, :WIDTH][:, half], lines[layer, 0:1, WIDTH : 2 * WIDTH][:, half]], axis=1
+            )
+            for a in range(2):
+                cols = slice((2 * b + a) * WIDTH, (2 * b + a + 1) * WIDTH)
+                line_land[0, base + 7 + a : base + 8 + a, at] = hidden_sum[:, cols]
+    line_waits = []
+    for j in range(1, 4):
+        there = span(place.rows[j] * WIDTH, WIDTH)
+        sent, got = copies.trade(
+            line_land.at[0, :, there],
+            dp_land.at[3 + j],
+            dp_land.at[3 + j],
+            place.to_row(j),
+        )
+        copies.open.append(sent)
+        line_waits.append(got)
+    for wait in line_waits:
+        wait()
+    total = line_land[0, :, own_lanes]
+    dp_land[place.dp] = total + dp_land[4] + dp_land[5] + dp_land[6]
+    line_waits = []
+    for i, device in enumerate(others):
+        back = (place.dp + 3 - i) % 4
+        sent, got = copies.sem(), copies.sem()
+        out = pltpu.make_async_remote_copy(
+            dp_land.at[place.dp], dp_land.at[place.dp], sent, got, device_id=device, device_id_type=MESH
+        )
+        arriving = pltpu.make_async_remote_copy(
+            dp_land.at[back], dp_land.at[back], sent, got, device_id=device, device_id_type=MESH
+        )
+        out.start()
+        copies.open.append(out.wait_send)
+        line_waits.append(arriving.wait_recv)
+    queue = [(reductions[0, kind], s) for kind in (3, 2, 1, 0) for s in range(PIECES[kind][0])]
+    for i in range(len(queue) + 2):
+        for lag, name in enumerate(("over_chips", "to_middle", "back")):
+            if 0 <= i - lag < len(queue):
+                item, s = queue[i - lag]
+                getattr(item, name)(s)
+    for wait in line_waits:
+        wait()
+    small_out[...] = dp_land[0] + dp_land[1] + dp_land[2] + dp_land[3]
+    for kind in (3, 2, 1, 0):
+        reductions[0, kind].finish()
+    core_free()
+    for k in range(CHUNKS):
+        sent_col[k]()
+    for wait in landed:
+        wait()
+    copies.finish()
+
+
+def backward_call(tokens_shape, grad_in, wide, seg_row, weights, saved, stream):
+    units = weights[2].shape[2]
+    scratch = [
+        ((3, D, WIDTH), bf16),
+        ((WIDTH, D), bf16),
+        ((D, units), bf16),
+        ((units, D), bf16),
+        ((LEN, D), bf16),
+        ((LEN, 3 * WIDTH), bf16),
+        ((LEN, WIDTH), bf16),
+        ((LEN, 128), f32),
+        ((LEN, D), bf16),
+        ((LEN, units), bf16),
+        ((LEN, units), bf16),
+        ((CHUNKS, OWN, D), f32),
+        ((CHUNKS, OWN, D), f32),
+        ((LEN, D), bf16),
+        ((LEN, units), bf16),
+        ((LEN, D), bf16),
+        ((LEN, 3 * WIDTH), bf16),
+        ((SPAN, WIDTH), bf16),
+        ((LEN, 2 * WIDTH), f32),
+        ((CHUNKS, OWN, D), f32),
+        ((OWN, D), f32),
+        ((OWN, D), bf16),
+        ((2, CHUNKS, OWN, D), bf16),
+        ((CHUNKS, OWN, D), bf16),
+        ((2, CHUNKS, OWN, D), bf16),
+        ((LAYERS, 6, 8, D), f32),
+        ((LAYERS, 16, D), f32),
+        ((1, LAYERS * LINES, D), f32),
+        ((7, LAYERS * LINES, WIDTH), f32),
+    ]
+    for parts in (4, 3, 2, 2):
+        scratch += [((parts, *piece), bf16) for piece in PIECES]
+    outs = [
+        (tokens_shape, bf16),
+        ((LAYERS * LINES, WIDTH), f32),
+        ((LAYERS, 3, WIDTH, 2 * WIDTH), bf16),
+        ((LAYERS, 2 * WIDTH, WIDTH), bf16),
+        ((LAYERS, WIDTH, 2 * units), bf16),
+        ((LAYERS, 2 * units, WIDTH), bf16),
+    ]
+    anywhere = pl.BlockSpec(memory_space=pl.ANY)
+    inside = pl.BlockSpec(memory_space=pltpu.VMEM)
+    return pl.pallas_call(
+        backward_body,
+        out_shape=[like(*v) for v in outs],
+        in_specs=[anywhere] + [inside] * 2 + [anywhere] * 12,
+        out_specs=[anywhere, inside] + [anywhere] * 4,
+        scratch_shapes=[pltpu.VMEM(*v) for v in scratch]
+        + [pltpu.SemaphoreType.REGULAR((12,)), pltpu.SemaphoreType.DMA((480,))],
+        compiler_params=pltpu.CompilerParams(
+            collective_id=1, has_side_effects=True, vmem_limit_bytes=60 * 1024 * 1024
+        ),
+    )(grad_in, wide, seg_row, *weights, *saved, stream)
+
+
 def pair_plan(
     tokens,
     segments,
@@ -1423,47 +1665,10 @@
     down_bias,
     cotangent,
 ):
-    row = lax.axis_index("row")
-    core = row % 2
-    chip = row // 2
-    first = core == 0
-    core_id = core.astype(jnp.int32).reshape(1)
-    chunks = range(CHUNKS)
-
-    def to_features(pieces):
-        whole = jnp.concatenate(pieces)
-        parts = [lax.dynamic_slice_in_dim(whole, (row ^ j) * WIDTH, WIDTH, 1) for j in range(4)]
-        got = [parts[0]] + [swap_row(parts[j], j) for j in range(1, 4)]
-        halves = [jnp.stack(pair).reshape(2, CHUNKS, OWN, WIDTH) for pair in (got[:2], got[2:])]
-        packs = []
-        for pair in halves:
-            pair = jnp.where(first, pair, pair[::-1])
-            packs.append(jnp.swapaxes(pair, 0, 1).reshape(LEN, WIDTH))
-        return jnp.where(
-            chip == 0,
-            jnp.concatenate(packs),
-            jnp.concatenate(packs[::-1]),
-        )
-
+    chip = lax.axis_index("row") // 2
     seg_pack = lax.dynamic_slice_in_dim(segments, chip * LEN, LEN, 0)
     seg_col, seg_row = seg_pack[:, None], seg_pack[None, :]
-    (
-        result,
-        grad_in,
-        wide,
-        triple_wide,
-        output_wide,
-        up_wide,
-        down_wide,
-        attn_all,
-        rows_all,
-        mixed_all,
-        log_all,
-        mlp_all,
-        slope_all,
-        active_all,
-        stream_all,
-    ) = forward_call(
+    result, grad_in, wide, *kept, stream = forward_call(
         tokens,
         cotangent,
         pack_small(norm_gain, norm_shift, output_bias, down_bias, triple_bias, up_bias),
@@ -1474,122 +1679,24 @@
         up_weight,
         down_weight,
     )
-    low = [grad_in[k] for k in chunks]
-    gains = wide[:4].reshape(LAYERS, 2, D)
-    weights = []
-    stored = []
-    for layer in range(LAYERS):
-        t = triple_wide[layer]
-        weights.append(
-            (jnp.concatenate([t[0], t[1], t[2]], axis=1), output_wide[layer], up_wide[layer], down_wide[layer])
-        )
-        stored.append(
-            {
-                "start": [stream_all[layer, 0, k] for k in chunks],
-                "middle": [stream_all[layer, 1, k] for k in chunks],
-                "attn": [attn_all[layer, k] for k in chunks],
-                "triple": [rows_all[layer, k] for k in chunks],
-                "mixed": [mixed_all[layer, k] for k in chunks],
-                "logs": [log_all[layer, k] for k in chunks],
-                "mlp": [mlp_all[layer, k] for k in chunks],
-                "pre": [slope_all[layer, k] for k in chunks],
-                "active": [active_all[layer, k] for k in chunks],
-            }
-        )
-    grad = [v.astype(f32) for v in low]
-    low_sums = sum(jnp.sum(v, axis=0) for v in grad)
-    grads = [None] * LAYERS
-    for layer in reversed(range(LAYERS)):
-        triple_w, output_w, up_w, down_w = weights[layer]
-        saved = stored[layer]
-        down_bias_grad = low_sums
-        down_in, hidden, branch, triple_rows = ([None] * CHUNKS for _ in range(4))
-        sums_two, sums_one = [], []
-        up_bias_grad, triple_bias_grad = [], []
-        for k in reversed(chunks):
-            down_in[k], hidden[k], bias, mine, other = mlp_back_call(
-                core_id, low[k], swap_core(low[k]), down_w, saved["pre"][k], up_w
-            )
-            up_bias_grad.append(bias[0])
-            total = chip_total(mine, other)
-            grad[k], low[k], sums = norm_back_call(
-                grad[k], total, swap_col(total), saved["middle"][k], gains[layer, 1]
-            )
-            sums_two.append(sums)
-        down_grad = spread_grad(*weight_grad(saved["active"], down_in, 1))
-        up_grad = spread_grad(*weight_grad(saved["mlp"], hidden, 0))
-        carried = None
-        for k in reversed(chunks):
-            branch[k], triple_rows[k], bias, mine, other, *carry = attend_back_call(
-                k,
-                core_id,
-                low[k],
-                swap_core(low[k]),
-                output_w,
-                triple_w,
-                saved["logs"][k],
-                seg_col,
-                seg_row,
-                saved["triple"][: k + 1],
-                carried,
-            )
-            carried = carry[0] if carry else None
-            triple_bias_grad.append(bias)
-            total = chip_total(mine, other)
-            grad[k], low[k], sums = norm_back_call(
-                grad[k], total, swap_col(total), saved["start"][k], gains[layer, 0]
-            )
-            sums_one.append(sums)
-        output_grad = spread_grad(*weight_grad(saved["mixed"], branch, 1))
-        triple_grad = spread_grad(*weight_grad(saved["attn"], triple_rows, 0))
-        sums_one, sums_two = sum(sums_one), sum(sums_two)
-        up_bias_grad, triple_bias_grad = sum(up_bias_grad), sum(triple_bias_grad)
-        low_sums = sums_one[2]
-
-        full = jnp.stack(
-            [sums_one[0], sums_two[0], sums_one[1], sums_two[1], sums_two[2], down_bias_grad]
-        )
-        full = jnp.moveaxis(full.reshape(6, 4, WIDTH), 1, 0)
-        full = jnp.stack(
-            [lax.dynamic_index_in_dim(full, row ^ j, 0, keepdims=False) for j in range(4)]
-        )
-        theirs = swap_core(full)
-        full = full + jnp.stack([theirs[1], theirs[0], theirs[3], theirs[2]])
-        full = full[0] + swap_chip(full[2])
-        pieces = jnp.concatenate(
-            [
-                jnp.moveaxis(triple_bias_grad.reshape(2, 2, D // 8), 1, 0).reshape(2, -1),
-                up_bias_grad.reshape(2, -1),
-            ],
-            axis=1,
-        )
-        pieces = pieces + swap_chip(pieces)
-        give = lax.dynamic_index_in_dim(pieces, 1 - core, 0, keepdims=False)
-        keep = lax.dynamic_index_in_dim(pieces, core, 0, keepdims=False)
-        share = jnp.where(chip == core, keep, swap_core(give))
-        packed = jnp.concatenate([full.reshape(-1), share]).reshape(-1, 128)
-        packed = dp_total(packed).reshape(-1)
-        full = packed[: 6 * WIDTH].reshape(6, WIDTH)
-        share = packed[6 * WIDTH :]
-        thirds = [slice(part * WIDTH, (part + 1) * WIDTH) for part in range(3)]
-        grads[layer] = (
-            full[0:2],
-            full[2:4],
-            jnp.stack(
-                [in_place(first, triple_grad[0][:, s], triple_grad[1][:, s], 1) for s in thirds],
-                axis=1,
-            ),
-            share[: D // 4].reshape(2, D // 8),
-            in_place(first, output_grad[0], output_grad[1], 0),
-            full[4],
-            in_place(first, up_grad[0], up_grad[1], 1),
-            share[D // 4 :],
-            in_place(first, down_grad[0], down_grad[1], 0),
-            full[5],
-        )
-    input_grad = to_features(low).astype(f32)
-    stacks = [jnp.stack([grads[layer][k] for layer in range(LAYERS)]) for k in range(10)]
-    return (result, input_grad, *stacks)
+    input_grad, small, triple_grad, output_grad, up_grad, down_grad = backward_call(
+        tokens.shape, grad_in, wide, seg_row.astype(f32), kept[:4], kept[4:], stream
+    )
+    small = small.reshape(LAYERS, LINES, WIDTH)
+    return (
+        result,
+        input_grad.astype(f32),
+        small[:, 0:2],
+        small[:, 2:4],
+        jnp.swapaxes(triple_grad, 1, 2).astype(f32),
+        small[:, 6].reshape(LAYERS, 2, WIDTH // 2),
+        output_grad.astype(f32),
+        small[:, 4],
+        up_grad.astype(f32),
+        small[:, 7:9].reshape(LAYERS, 2 * WIDTH),
+        down_grad.astype(f32),
+        small[:, 5],
+    )
 
 
 def solution(mesh):

time: 776 us -> 480 us (0.62)
  waiting for transfers between devices: 215 us -> 0 us
  Pallas kernels: 238 us -> 450 us
  local copies, waits for them, and re-layouts: 126 us -> 9.68 us
  starting transfers between devices: 91.9 us -> 0 us
  other arithmetic: 93.1 us -> 12.6 us
    ppermute x81 -> x0, waiting for transfers between devices: 215 us -> none  [the longest x10 74.6 us: dp_total(): back = lax.ppermute(whole, 'dp', [(1, 0), (2, 3)])]
    pallas_call x24 -> x1, Pallas kernels: 89.3 us -> 301 us  [backward_call(): pl.pallas_call(backward_body, out_shape=[like(*v) for v in outs], in_spec...]
    ppermute x81 -> x0, starting transfers between devices: 91.9 us -> none  [the longest x10 39 us: dp_total(): from_end = lax.ppermute(value, 'dp', [(0, 1), (3, 2)])]
    unnamed x365 -> x16, local copies, waits for them, and re-layouts: 75.9 us -> 3.7 us
    convert_element_type x41 -> x6, other arithmetic: 48.3 us -> 12 us  [the longest x1 2.7 us: pair_plan(): input_grad.astype(f32)]
    squeeze x12 -> x1, local copies, waits for them, and re-layouts: 22.4 us -> 0.58 us  [pair_plan(): small[:, 5]]
    another operation x24 -> x0, other arithmetic: 21.6 us -> none  [the longest x12 14 us: pair_plan(): jnp.stack([grads[layer][k] for layer in range(LAYERS)])]
    slice x38 -> x1, local copies, waits for them, and re-layouts: 17.3 us -> 1.48 us  [pair_plan(): small[:, 5]]
  transfers between devices with their start and end apart: 81 -> 0, of which waited for: 23 -> 0; matrix products, arithmetic and copies ran while one was open for 17% -> 0% of each run, Pallas kernels for 11% -> 0%
where the time goes in v3:
time: 480 us; the launch traced here: 473 us
  Pallas kernels  450 us (94%)
  other arithmetic  12.6 us (3%)
  local copies, waits for them, and re-layouts  9.68 us (2%)
    pallas_call x1, Pallas kernels, backward_call(): pl.pallas_call(backward_body, out_shape=[like(*v) for v in outs], in_spec...  301 us
    pallas_call x1, Pallas kernels, forward_call(): pl.pallas_call(forward_body, out_shape=[like(*v) for v in outs], in_specs...  148 us

profile of v3, /device:TPU:0, one launch (start us, length us, event | category | flops | bytes accessed | tf_op | source)
XLA Modules:
  0.0 472.7 jit_solution(9178617359768267030)
XLA Ops:
  0.7 0.7 copy.37
  1.3 0.7 reshape.43
  2.0 0.7 reshape.44
  2.7 0.7 reshape.46
  3.4 0.8 concatenate.3
  4.2 1.3 fusion
  5.5 0.0 copy-start.5
  5.5 0.6 pad_convert_fusion.refs_2_
  6.1 1.0 copy.27.refs_3_
  7.2 0.0 copy-done.5
  7.2 148.0 %shard_map.220 = (bf16[2048,256]{1,0:T(8,128)(2,1)}, bf16[2,256,1024]{2,1,0:T(8,128)(2,1)}, f32[24,1024]{1,0:T(8,128)}, bf16[2,3,1024,256]{3,2,1,0:T(8,128)(2,1)...) custom-call(bf16[2048,256]{1,0:T(8,128)(2,1)} %refs_0_.1, ...), custom_call_target="tpu_custom_call" | custom-call | tf_op jit(solution)/shard_map/pallas_call | solution.py:924
  155.2 301.5 %shard_map.221 = (bf16[2048,256]{1,0:T(8,128)(2,1)}, f32[32,256]{1,0:T(8,128)}, bf16[2,3,256,512]{3,2,1,0:T(8,128)(2,1)}, bf16[2,512,256]{2,1,0:T(8,128)(2,1)}, ...) custom-call(bf16[2,256,1024]{2,1,0:T(8,128)(2,1)} %get-tuple-element.34.refs_0_, ...), custom_call_target="tpu_custom_call" | custom-call | tf_op jit(solution)/shard_map/pallas_call | solution.py:1640
  456.7 0.0 copy-start.4
  456.7 0.0 copy-start.2
  456.7 1.5 fusion.1
  458.2 1.4 slice_bitcast_fusion
  459.6 0.6 copy.33
  460.2 0.6 copy_bitcast_fusion
  460.8 2.7 convert_element_type.28
  463.5 0.0 copy-done.4
  463.5 0.0 copy-start.1
  463.5 1.0 convert_element_type.31
  464.6 0.0 copy-done.2
  464.6 2.1 convert_bitcast_fusion
  466.7 0.0 copy-done.1
  466.7 0.0 copy-start
  466.7 2.5 convert_element_type.32
  469.2 0.0 copy-done
  469.2 0.0 copy-start.3
  469.2 2.3 convert_element_type.33
  471.6 0.0 copy-done.3
  471.6 1.0 copy.39
Async XLA Ops:
  5.5 1.6 copy-start.5
  456.7 6.8 %copy-start.4 = (bf16[2,512,256]{2,1,0:T(8,128)(2,1)S(1)}, bf16[2,512,256]{2,1,0:T(8,128)(2,1)}, u32[]{:S(2)}) copy-start(bf16[2,512,256]{2,1,0:T(8,128)(2,1)} %get-tuple-element.51) | copy-start | bytes 1572868
  456.7 7.9 %copy-start.2 = (bf16[2,3,256,512]{3,2,1,0:T(8,128)(2,1)S(1)}, bf16[2,3,256,512]{3,2,1,0:T(8,128)(2,1)}, u32[]{:S(2)}) copy-start(bf16[2,3,256,512]{3,2,1,0:T(8,128)(2,1)} %get-tuple-element.50) | copy-start | bytes 4718596
  463.5 3.2 copy-start.1
  466.7 2.5 copy-start
  469.2 2.3 copy-start.3

commit v4 on v3

--- a/solution.py
+++ b/solution.py
@@ -474,12 +474,15 @@
     return source, target
 
 
+STRIP = 64
+
+
 def strips(count, body):
     def step(i, carry):
-        body(pl.multiple_of(i * 32, 32))
+        body(pl.multiple_of(i * STRIP, STRIP))
         return carry
 
-    lax.fori_loop(0, count // 32, step, 0)
+    lax.fori_loop(0, count // STRIP, step, 0)
 
 
 def causal(seg_col, seg_row, start, keys):
@@ -634,8 +637,14 @@
         own = copies.local(source(core, None), target(place.row, None))
         ready_waits[layer, kind] = [got, own.wait]
 
-    def relay_weight(layer, kind):
-        for got, arrived, missing in arrivals[layer, kind]:
+    relays = [
+        (layer, kind, i) for layer in range(LAYERS) for kind in range(4) for i in range(2)
+    ]
+
+    def pump(count):
+        for _ in range(count):
+            layer, kind, i = relays.pop(0)
+            got, arrived, missing = arrivals[layer, kind][i]
             got()
             sent, back = copies.trade(arrived, arrived, missing, place.to_dp())
             copies.open.append(sent)
@@ -693,15 +702,12 @@
         center = jnp.mean(value, axis=1, keepdims=True)
         second = jnp.mean(value * value, axis=1, keepdims=True) - center * center
         normed = (value - center) * lax.rsqrt(second + eps)
-        target[pl.ds(pl.multiple_of(core * OWN + at, 32), 32), :] = (
+        target[pl.ds(pl.multiple_of(core * OWN + at, STRIP), STRIP), :] = (
             normed * gain(layer, which) + shift(layer, which)
         ).astype(bf16)
 
     def share(target):
         return copies.trade(target.at[part(core)], target.at[part(core)], target.at[part(sibling)], place.to_row(1))
-
-    def give_rows(k, value):
-        give[k] = value.astype(bf16)
 
     sent_core, sent_col = [None] * CHUNKS, [None] * CHUNKS
     col_waits = [None] * CHUNKS
@@ -713,7 +719,7 @@
             sent_col[k]()
 
         def add(at):
-            lines = pl.ds(at, 32)
+            lines = pl.ds(at, STRIP)
             chip_sum[k, lines, :] = (
                 mine[k, lines, :] + got_core[stage, k, lines, :].astype(f32)
             ).astype(bf16)
@@ -734,7 +740,7 @@
         col_waits[k]()
 
         def add(at):
-            lines = pl.ds(at, 32)
+            lines = pl.ds(at, STRIP)
             total = chip_sum[k, lines, :].astype(f32) + got_col[stage, k, lines, :].astype(f32)
             value = stream[stage, k, lines, :] + (total + bias)
             stream[1 - stage, k, lines, :] = value
@@ -746,29 +752,21 @@
     for k in range(CHUNKS):
         for wait in token_waits[k]:
             wait()
-        if k == 0:
-            pass
-
         def first(at, k=k):
-            value = taken[k, pl.ds(at, 32), :].astype(f32)
-            stream[0, k, pl.ds(at, 32), :] = value
+            value = taken[k, pl.ds(at, STRIP), :].astype(f32)
+            stream[0, k, pl.ds(at, STRIP), :] = value
             norm_to(value, 0, 0, attn.at[0, k], at)
 
         strips(OWN, first)
         saves[0, 0, k] = copies.local(stream.at[0, k], stream_out.at[0, 0, k])
         shares[k] = share(attn.at[0, k])
-        if k == 0:
-            relay_weight(0, 0)
-    relay_weight(0, 1)
-    pump = [(0, 2), (0, 3), (1, 0), (1, 1), (1, 2), (1, 3)]
-
-    def pump_one():
-        if pump:
-            relay_weight(*pump.pop(0))
+        pump(2)
 
     for layer in range(LAYERS):
         for k in range(CHUNKS):
             if layer:
+                if k == 0:
+                    pump(1)
                 saves.pop((layer - 1, 0, k)).wait()
                 take_col(
                     1, k, layer, down_bias(layer - 1), lambda v, at, k=k: norm_to(v, layer, 0, attn.at[layer, k], at)
@@ -799,6 +797,7 @@
                 mixed.at[layer, k],
                 logs.at[layer, k],
             )
+            pump(1)
             if k == 0:
                 ready_weight(layer, 1)
             if sent_core[k] is not None:
@@ -812,10 +811,13 @@
             copies.save(mixed.at[layer, k], mixed_out.at[layer, k])
             copies.save(logs.at[layer, k], log_out.at[layer, k])
             settle(0, k, got)
-            pump_one()
+            if k:
+                pump(1)
         for k in range(CHUNKS):
             if layer:
                 saves.pop((layer - 1, 1, k)).wait()
+            elif k:
+                pump(1)
             take_col(
                 0, k, layer, output_bias(layer), lambda v, at, k=k: norm_to(v, layer, 1, mlp.at[layer, k], at)
             )
@@ -843,6 +845,8 @@
             got()
             widen(sibling)
             if k == 0:
+                if layer == 0:
+                    pump(1)
                 ready_weight(layer, 3)
             sent_core[k]()
             give[k] = dot(active[layer, k, part(sibling), :], down_w[layer]).astype(bf16)
@@ -853,13 +857,14 @@
             copies.save(slope.at[layer, k], slope_out.at[layer, k])
             copies.save(active.at[layer, k], active_out.at[layer, k])
             settle(1, k, got)
-            pump_one()
+            if layer == 0:
+                pump(k + 1)
     result_waits = []
     for k in range(CHUNKS):
         saves.pop((LAYERS - 1, 0, k)).wait()
 
         def finish(v, at, k=k):
-            final[k, pl.ds(at, 32), :] = v.astype(bf16)
+            final[k, pl.ds(at, STRIP), :] = v.astype(bf16)
 
         take_col(1, k, LAYERS, down_bias(LAYERS - 1), finish)
         result_waits.append(copies.local(final.at[k, :, own_lanes], result_ref.at[held(0, k), :]).wait)
@@ -946,7 +951,31 @@
     return jnp.pad(lines, ((0, SMALL - lines.shape[0]), (0, 0)))
 
 
-PIECES = ((3, WIDTH, WIDTH), (1, WIDTH, WIDTH), (2, WIDTH // 2, D), (2, D // 2, WIDTH))
+PIECES = ((3, WIDTH, WIDTH), (1, WIDTH, WIDTH), (4, WIDTH // 4, D), (4, D // 4, WIDTH))
+
+PLAN = {
+    "a1": ((1, 3, 0, 0),),
+    "a0": ((1, 3, 1, 0), (1, 3, 0, 1)),
+    "u1": ((1, 3, 2, 0),),
+    "c1": ((1, 3, 1, 1), (1, 3, 0, 2), (1, 3, 3, 0)),
+    "m1": ((1, 3, 2, 1), (1, 2, 0, 0), (1, 3, 1, 2), (1, 3, 3, 1), (1, 2, 1, 0)),
+    "c0": ((1, 2, 2, 0), (1, 3, 2, 2), (1, 2, 0, 1)),
+    "m0": ((1, 2, 3, 0), (1, 3, 3, 2), (1, 2, 1, 1)),
+    "w1": ((1, 2, 0, 2), (1, 2, 2, 1)),
+    "f1": ((1, 3, 0, 3),),
+    "g1": ((1, 1, 0, 0), (1, 2, 1, 2), (1, 2, 3, 1)),
+    "e0": ((1, 0, 0, 0), (1, 2, 2, 2)),
+    "g0": ((1, 1, 0, 1), (1, 0, 1, 0), (1, 2, 3, 2)),
+    "v0": ((1, 0, 0, 1), (1, 0, 2, 0)),
+    "u0": ((1, 1, 0, 2), (1, 2, 0, 3), (1, 0, 1, 1)),
+    "c1L": ((0, 3, 0, 0), (1, 0, 0, 2)),
+    "m1L": ((1, 1, 0, 3), (1, 0, 2, 1), (0, 3, 1, 0), (1, 0, 1, 2), (0, 3, 0, 1), (0, 3, 2, 0)),
+    "m0L": ((1, 0, 2, 2), (0, 3, 1, 1), (0, 3, 3, 0), (0, 3, 0, 2), (0, 3, 2, 1), (0, 2, 0, 0)),
+    "w0": ((0, 2, 1, 0), (1, 0, 0, 3)),
+    "h1": ((0, 3, 1, 2), (0, 3, 3, 1)),
+    "h0": ((0, 2, 2, 0), (0, 3, 2, 2), (0, 2, 0, 1), (0, 2, 3, 0), (0, 3, 3, 2), (0, 2, 1, 1)),
+    "tail": ((0, 1, 0, 0), (0, 2, 2, 1), (0, 2, 0, 2), (0, 0, 0, 0), (0, 2, 3, 1), (0, 2, 1, 2), (0, 0, 1, 0), (0, 1, 0, 1), (0, 2, 2, 2), (0, 0, 2, 0), (0, 0, 0, 1), (0, 2, 3, 2), (0, 0, 1, 1), (0, 1, 0, 2), (0, 0, 2, 1), (0, 0, 0, 2), (0, 0, 1, 2), (0, 0, 2, 2)),
+}
 LINES = 16
 
 
@@ -1011,8 +1040,8 @@
         if self.kind == 1:
             return out.at[layer, span(core * WIDTH, WIDTH), :]
         if self.kind == 2:
-            return out.at[layer, s * (WIDTH // 2) : (s + 1) * (WIDTH // 2), span(core * D, D)]
-        return out.at[layer, span(core * D + s * (D // 2), D // 2), :]
+            return out.at[layer, s * (WIDTH // 4) : (s + 1) * (WIDTH // 4), span(core * D, D)]
+        return out.at[layer, span(core * D + s * (D // 4), D // 4), :]
 
     def send(self):
         place, copies = self.place, self.copies
@@ -1303,7 +1332,7 @@
             sent_col[k]()
 
         def add(at):
-            here = pl.ds(at, 32)
+            here = pl.ds(at, STRIP)
             chip_sum[k, here, :] = (mine[here, :] + got_core[stage, k, here, :].astype(f32)).astype(bf16)
 
         strips(OWN, add)
@@ -1316,7 +1345,7 @@
         scale = gain(layer, which)
 
         def back(at):
-            here = pl.ds(at, 32)
+            here = pl.ds(at, STRIP)
             grad_out = chip_sum[k, here, :].astype(f32) + got_col[stage, k, here, :].astype(f32)
             normed, inv_std = norm_parts(stream[k, here, :])
             scaled = grad_out * scale
@@ -1325,7 +1354,7 @@
             )
             low = total.astype(bf16)
             grad[k, here, :] = total
-            target[pl.ds(pl.multiple_of(k * SPAN + core * OWN + at, 32), 32), :] = low
+            target[pl.ds(pl.multiple_of(k * SPAN + core * OWN + at, STRIP), STRIP), :] = low
             sums[layer, which] += columns(grad_out * normed)
             sums[layer, 2 + which] += columns(grad_out)
             if which == 1:
@@ -1342,9 +1371,9 @@
     for k in reversed(range(CHUNKS)):
 
         def widen(at, k=k):
-            low = down_in[pl.ds(pl.multiple_of(k * SPAN + core * OWN + at, 32), 32), :]
+            low = down_in[pl.ds(pl.multiple_of(k * SPAN + core * OWN + at, STRIP), STRIP), :]
             value = low.astype(f32)
-            grad[k, pl.ds(at, 32), :] = value
+            grad[k, pl.ds(at, STRIP), :] = value
             sums[top, 5] += columns(value)
 
         strips(OWN, widen)
@@ -1386,32 +1415,59 @@
             need("mlp")
             for b in range(4):
                 value = dot_tn(mlp[:, b * WIDTH : (b + 1) * WIDTH], hidden[...]).astype(bf16)
-                for s in range(2):
-                    grads[2][b, s] = value[s * (WIDTH // 2) : (s + 1) * (WIDTH // 2)]
+                for s in range(4):
+                    grads[2][b, s] = value[s * (WIDTH // 4) : (s + 1) * (WIDTH // 4)]
         else:
             need("active")
             for pair in range(4):
                 value = dot_tn(active[:, pair * WIDTH : (pair + 1) * WIDTH], down_in[...]).astype(bf16)
-                s, at = pair // 2, pair % 2 * WIDTH
                 for b in range(4):
-                    grads[3][b, s, at : at + WIDTH] = value[:, b * WIDTH : (b + 1) * WIDTH]
+                    grads[3][b, pair] = value[:, b * WIDTH : (b + 1) * WIDTH]
         reductions[layer, kind].send()
 
-    def run(layer, kind, *names):
-        item = reductions[layer, kind]
-        for name in names:
-            if name == "finish":
+    def pump(point):
+        for layer, kind, s, step in PLAN.get(point, ()):
+            item = reductions[layer, kind]
+            if step == 3:
                 item.finish()
             else:
-                for s in range(item.count):
-                    getattr(item, name)(s)
+                (item.over_chips, item.to_middle, item.back)[step](s)
+
+    landed = []
+
+    def held(j, k):
+        return span(place.rows[j] // 2 * LEN + k * SPAN + place.cores[j] * OWN, OWN)
+
+    def send_input_grad(k):
+        mine_rows = part(k, core)
+        landed.append(
+            copies.local(down_in.at[mine_rows, own_lanes], input_grad_ref.at[held(0, k), :]).wait
+        )
+        for j in (2, 3, 1):
+            sent, got = copies.trade(
+                down_in.at[mine_rows, span(place.rows[j] * WIDTH, WIDTH)],
+                input_grad_ref.at[held(0, k), :],
+                input_grad_ref.at[held(j, k), :],
+                place.to_row(j),
+            )
+            landed.extend([sent, got])
 
     for layer in reversed(range(LAYERS)):
+        upper = layer == top
         for k in reversed(range(CHUNKS)):
-            if k == CHUNKS - 1 and layer == top:
-                for i in reversed(range(CHUNKS)):
-                    shares[i][1]()
-                weight_grad(layer, 3)
+            if upper:
+                if k == CHUNKS - 1:
+                    for i in reversed(range(CHUNKS)):
+                        shares[i][1]()
+                    weight_grad(layer, 3)
+            else:
+                pump(f"e{k}")
+                need("start")
+                take_col(1, k, layer + 1, 0, start, down_in)
+                shares[k] = share(down_in, k)
+                if k == 0:
+                    load("start", layer)
+                pump(f"f{k}")
             need("down_w")
             need("slope")
 
@@ -1423,32 +1479,29 @@
                     hidden[part(k, c), cols] = value
                     lines[layer, 8:16, cols] += columns(value.astype(f32))
 
-            if layer < top:
-                shrink(core)
+            shrink(core)
+            if not upper:
                 shares[k][1]()
-                shrink(sibling)
-            else:
-                shrink(core)
-                shrink(sibling)
+            shrink(sibling)
             need("up_w")
             core_free()
             give[...] = dot_nt(hidden[part(k, sibling), :], up_w[...]).astype(bf16)
             got = start_core(0, k)
             mine[...] = dot_nt(hidden[part(k, core), :], up_w[...])
             shares[k][0]()
+            pump(f"a{k}" if upper else f"g{k}")
             settle(0, k, got)
-        if layer < top:
-            run(layer + 1, 3, "back", "finish")
-            run(layer + 1, 2, "to_middle")
+        if not upper:
             weight_grad(layer, 3)
-            weight_grad(layer, 2)
-            run(layer + 1, 1, "over_chips")
-        else:
-            weight_grad(layer, 2)
+            pump("v0")
+        weight_grad(layer, 2)
+        pump(f"u{layer}")
         if layer:
             for name in ("active", "down_w", "slope", "up_w", "mlp"):
                 load(name, layer - 1)
         for k in reversed(range(CHUNKS)):
+            point = f"{k}" if upper else f"{k}L"
+            pump(f"b{point}")
             need("middle")
             take_col(0, k, layer, 1, middle, branch)
             shares[k] = share(branch, k)
@@ -1464,13 +1517,13 @@
             need("logs")
             if k == CHUNKS - 1:
                 pair_total[...] = jnp.zeros_like(pair_total)
+            pump(f"c{point}")
             shares[k][1]()
             narrow(sibling)
-            attend_back_chunk(
-                k, rows, logs, seg_row_ref, mixed_grad, pair_total, rows_grad
-            )
+            attend_back_chunk(k, rows, logs, seg_row_ref, mixed_grad, pair_total, rows_grad)
             need("triple_w")
             core_free()
+            pump(f"m{point}")
 
             def project(c, k=k):
                 value = dot_nt(rows_grad[part(k, c), :WIDTH], triple_w[0])
@@ -1483,51 +1536,24 @@
             got = start_core(1, k)
             mine[...] = project(core)
             shares[k][0]()
+            pump(f"d{point}")
             settle(1, k, got)
-            if layer == top and k == CHUNKS - 1:
-                run(layer, 3, "over_chips")
-        here = rows_grad[:, :WIDTH].astype(f32)
-        lines[layer, 0:1, 0:WIDTH] = jnp.sum(here, axis=0, keepdims=True)
-        here = rows_grad[:, 2 * WIDTH :].astype(f32)
-        lines[layer, 0:1, WIDTH : 2 * WIDTH] = jnp.sum(here, axis=0, keepdims=True)
-        if layer < top:
-            run(layer + 1, 0, "over_chips")
-            run(layer + 1, 2, "back", "finish")
-            run(layer + 1, 1, "to_middle", "back", "finish")
-            run(layer + 1, 0, "to_middle")
         weight_grad(layer, 1)
         weight_grad(layer, 0)
+        for line, cols in ((0, slice(0, WIDTH)), (1, slice(2 * WIDTH, 3 * WIDTH))):
+            value = rows_grad[:SPAN, cols].astype(f32)
+            for k in range(1, CHUNKS):
+                value += rows_grad[k * SPAN : (k + 1) * SPAN, cols].astype(f32)
+            lines[layer, 0:1, line * WIDTH : (line + 1) * WIDTH] = jnp.sum(value, axis=0, keepdims=True)
+        pump(f"w{layer}")
         if layer:
-            run(layer, 3, "to_middle")
-            run(layer, 2, "over_chips")
             for name in ("output_w", "rows", "logs", "triple_w", "mixed", "attn"):
                 load(name, layer - 1)
-        for k in reversed(range(CHUNKS)):
-            need("start")
-            take_col(1, k, layer, 0, start, down_in)
-            if layer:
-                shares[k] = share(down_in, k)
-            if layer and k == 0:
-                load("start", layer - 1)
-    landed = []
-
-    def held(j, k):
-        return span(place.rows[j] // 2 * LEN + k * SPAN + place.cores[j] * OWN, OWN)
-
     for k in reversed(range(CHUNKS)):
-        mine_rows = part(k, core)
-        landed.append(
-            copies.local(down_in.at[mine_rows, own_lanes], input_grad_ref.at[held(0, k), :]).wait
-        )
-        for j in range(1, 4):
-            sent, got = copies.trade(
-                down_in.at[mine_rows, span(place.rows[j] * WIDTH, WIDTH)],
-                input_grad_ref.at[held(0, k), :],
-                input_grad_ref.at[held(j, k), :],
-                place.to_row(j),
-            )
-            landed += [sent, got]
-    run(top, 0, "back", "finish")
+        pump(f"h{k}")
+        need("start")
+        take_col(1, k, 0, 0, start, down_in)
+        send_input_grad(k)
     zero = jnp.zeros((1, WIDTH // 2), f32)
     for layer in range(LAYERS):
         found = [jnp.sum(sums[layer, i], axis=0, keepdims=True) for i in range(6)]
@@ -1573,12 +1599,7 @@
         out.start()
         copies.open.append(out.wait_send)
         line_waits.append(arriving.wait_recv)
-    queue = [(reductions[0, kind], s) for kind in (3, 2, 1, 0) for s in range(PIECES[kind][0])]
-    for i in range(len(queue) + 2):
-        for lag, name in enumerate(("over_chips", "to_middle", "back")):
-            if 0 <= i - lag < len(queue):
-                item, s = queue[i - lag]
-                getattr(item, name)(s)
+    pump("tail")
     for wait in line_waits:
         wait()
     small_out[...] = dp_land[0] + dp_land[1] + dp_land[2] + dp_land[3]
@@ -1643,7 +1664,7 @@
         in_specs=[anywhere] + [inside] * 2 + [anywhere] * 12,
         out_specs=[anywhere, inside] + [anywhere] * 4,
         scratch_shapes=[pltpu.VMEM(*v) for v in scratch]
-        + [pltpu.SemaphoreType.REGULAR((12,)), pltpu.SemaphoreType.DMA((480,))],
+        + [pltpu.SemaphoreType.REGULAR((12,)), pltpu.SemaphoreType.DMA((840,))],
         compiler_params=pltpu.CompilerParams(
             collective_id=1, has_side_effects=True, vmem_limit_bytes=60 * 1024 * 1024
         ),

time: 480 us -> 400 us (0.83)
  Pallas kernels: 450 us -> 369 us
    pallas_call x1, Pallas kernels: 301 us -> 222 us  [backward_call(): pl.pallas_call(backward_body, out_shape=[like(*v) for v in outs], in_spec...]
where the time goes in v4:
time: 400 us; the launch traced here: 392 us
  Pallas kernels  369 us (92%)
  other arithmetic  12.6 us (3%)
  local copies, waits for them, and re-layouts  9.68 us (2%)
    pallas_call x1, Pallas kernels, backward_call(): pl.pallas_call(backward_body, out_shape=[like(*v) for v in outs], in_spec...  222 us
    pallas_call x1, Pallas kernels, forward_call(): pl.pallas_call(forward_body, out_shape=[like(*v) for v in outs], in_specs...  146 us

profile of v4, /device:TPU:0, one launch (start us, length us, event | category | flops | bytes accessed | tf_op | source)
XLA Modules:
  0.0 392.1 jit_solution(2321445879762929611)
XLA Ops:
  0.7 0.7 copy.37
  1.3 0.7 reshape.43
  2.0 0.7 reshape.44
  2.7 0.7 reshape.46
  3.4 0.8 concatenate.3
  4.2 1.3 fusion
  5.5 0.0 copy-start.5
  5.5 0.6 pad_convert_fusion.refs_2_
  6.1 1.0 copy.27.refs_3_
  7.2 0.0 copy-done.5
  7.2 146.3 %shard_map.220 = (bf16[2048,256]{1,0:T(8,128)(2,1)}, bf16[2,256,1024]{2,1,0:T(8,128)(2,1)}, f32[24,1024]{1,0:T(8,128)}, bf16[2,3,1024,256]{3,2,1,0:T(8,128)(2,1)...) custom-call(bf16[2048,256]{1,0:T(8,128)(2,1)} %refs_0_.1, ...), custom_call_target="tpu_custom_call" | custom-call | tf_op jit(solution)/shard_map/pallas_call | solution.py:929
  153.5 222.3 %shard_map.221 = (bf16[2048,256]{1,0:T(8,128)(2,1)}, f32[32,256]{1,0:T(8,128)}, bf16[2,3,256,512]{3,2,1,0:T(8,128)(2,1)}, bf16[2,512,256]{2,1,0:T(8,128)(2,1)}, ...) custom-call(bf16[2,256,1024]{2,1,0:T(8,128)(2,1)} %get-tuple-element.34.refs_0_, ...), custom_call_target="tpu_custom_call" | custom-call | tf_op jit(solution)/shard_map/pallas_call | solution.py:1661
  375.8 0.0 copy-start.4
  375.8 0.0 copy-start.2
  375.8 1.5 fusion.1
  377.3 1.4 slice_bitcast_fusion
  378.7 0.6 copy.33
  379.3 0.6 copy_bitcast_fusion
  379.9 2.7 convert_element_type.28
  382.6 0.0 copy-done.4
  382.6 0.0 copy-start.1
  382.6 1.0 convert_element_type.31
  383.6 0.0 copy-done.2
  383.6 2.1 convert_bitcast_fusion
  385.7 0.0 copy-done.1
  385.7 0.0 copy-start
  385.7 2.5 convert_element_type.32
  388.3 0.0 copy-done
  388.3 0.0 copy-start.3
  388.3 2.3 convert_element_type.33
  390.6 0.0 copy-done.3
  390.6 1.0 copy.39
Async XLA Ops:
  5.5 1.6 copy-start.5
  375.8 6.8 %copy-start.4 = (bf16[2,512,256]{2,1,0:T(8,128)(2,1)S(1)}, bf16[2,512,256]{2,1,0:T(8,128)(2,1)}, u32[]{:S(2)}) copy-start(bf16[2,512,256]{2,1,0:T(8,128)(2,1)} %get-tuple-element.51) | copy-start | bytes 1572868
  375.8 7.9 %copy-start.2 = (bf16[2,3,256,512]{3,2,1,0:T(8,128)(2,1)S(1)}, bf16[2,3,256,512]{3,2,1,0:T(8,128)(2,1)}, u32[]{:S(2)}) copy-start(bf16[2,3,256,512]{3,2,1,0:T(8,128)(2,1)} %get-tuple-element.50) | copy-start | bytes 4718596
  382.6 3.2 copy-start.1
  385.7 2.5 copy-start
  388.3 2.3 copy-start.3
